TPU v7x, 256 devices: a whole 4x4x8 slice. The times are simulated.
256 devices in a mesh: dp: 16 (over y, x_hi, core), ctx: 16 (over z, x_lo).
Axes of the slice: x: 4 (x_hi: 2, x_lo: 2; x = x_hi * 2 + x_lo), y: 4, z: 8, core: 2. Of those that a mesh axis runs over, the one named last changes fastest.
Arguments:
- queries: bfloat16 [16, 8192, 640], P('dp', 'ctx'), may hold values from -6 to 6
- keys: bfloat16 [16, 8192, 640], P('dp', 'ctx'), may hold values from -6 to 6
- values: bfloat16 [16, 8192, 640], P('dp', 'ctx'), may hold values from -16 to 16
- grad_out: bfloat16 [16, 8192, 1280], P('dp', 'ctx'), may hold values from -6 to 6
- out_proj: bfloat16 [640, 1280], replicated, may hold values from -0.25 to 0.25
Outputs:
- grad_queries: bfloat16 [16, 8192, 640], P('dp', 'ctx')
- grad_keys: bfloat16 [16, 8192, 640], P('dp', 'ctx')
- grad_values: bfloat16 [16, 8192, 640], P('dp', 'ctx')
- grad_out_proj: float32 [1280, 640], P(('dp', 'ctx'))
All inputs are finite; a program needn't handle non-finite values.
Results may differ from a plain program's by a relative error of at most 0.028.
Values may be sent and summed in bfloat16 or wider, within the bound.
No kernel may reach another device: no remote copies, remote signals or barrier semaphores. Data moves between devices by JAX's collectives and lax.ppermute only.
A program may use at most 64 MiB of HBM per device.

v0:
```python
import jax
import jax.numpy as jnp
from jax import lax
from jax.sharding import PartitionSpec as P

HEADS = 10
HDIM = 64
REACH = 2


def passed_along(x, axis, by):
    devices = lax.axis_size(axis)
    pairs = [(i, i + by) for i in range(devices) if 0 <= i + by < devices]
    return lax.ppermute(x, axis, pairs)


def shards(queries, keys, values, grad_out, out_proj):
    tok = queries.shape[1]
    width = 2 * REACH + 1
    scale = HDIM ** (-0.5)
    index = lax.axis_index("ctx")
    blocks = lax.axis_size("ctx")
    q_loc = queries[0]
    k_loc = keys[0]
    v_loc = values[0]
    dy_loc = grad_out[0]
    grad_attn = lax.dot_general(
        dy_loc, out_proj, (((1,), (1,)), ((), ())), preferred_element_type=jnp.float32
    ).astype(jnp.bfloat16)
    nearby = {0: (k_loc, v_loc)}
    for offset in (-2, -1, 1, 2):
        nearby[offset] = passed_along((k_loc, v_loc), "ctx", -offset)
    order = list(range(-REACH, REACH + 1))
    key_all = jnp.concatenate([nearby[o][0] for o in order], axis=0)
    val_all = jnp.concatenate([nearby[o][1] for o in order], axis=0)
    valid = jnp.stack([(index + o >= 0) & (index + o < blocks) for o in order])
    key_mask = jnp.repeat(valid, tok)
    q_heads = q_loc.reshape(tok, HEADS, HDIM).transpose(1, 0, 2)
    k_heads = key_all.reshape(width * tok, HEADS, HDIM).transpose(1, 0, 2)
    v_heads = val_all.reshape(width * tok, HEADS, HDIM).transpose(1, 0, 2)
    g_heads = grad_attn.reshape(tok, HEADS, HDIM).transpose(1, 0, 2)

    def head_grads(inputs):
        q_one, k_one, v_one, g_one = inputs
        scores = (
            lax.dot_general(
                q_one, k_one, (((1,), (1,)), ((), ())), preferred_element_type=jnp.float32
            )
            * scale
        )
        scores = jnp.where(key_mask[None, :], scores, -jnp.inf)
        top = jnp.max(scores, axis=-1, keepdims=True)
        lse = top + jnp.log(jnp.sum(jnp.exp(scores - top), axis=-1, keepdims=True))
        probs = jnp.exp(scores - lse)
        probs_b = probs.astype(jnp.bfloat16)
        attn_one = jnp.dot(probs_b, v_one, preferred_element_type=jnp.float32).astype(jnp.bfloat16)
        delta = jnp.sum(
            g_one.astype(jnp.float32) * attn_one.astype(jnp.float32), axis=-1, keepdims=True
        )
        dprob = lax.dot_general(
            g_one, v_one, (((1,), (1,)), ((), ())), preferred_element_type=jnp.float32
        )
        dscore = (probs * (dprob - delta)).astype(jnp.bfloat16)
        gq_one = (jnp.dot(dscore, k_one, preferred_element_type=jnp.float32) * scale).astype(
            jnp.bfloat16
        )
        pk_one = (
            lax.dot_general(
                dscore, q_one, (((0,), (0,)), ((), ())), preferred_element_type=jnp.float32
            )
            * scale
        ).astype(jnp.bfloat16)
        pv_one = lax.dot_general(
            probs_b, g_one, (((0,), (0,)), ((), ())), preferred_element_type=jnp.float32
        ).astype(jnp.bfloat16)
        return (gq_one, pk_one, pv_one, attn_one)

    grad_q, part_k, part_v, attn = lax.map(head_grads, (q_heads, k_heads, v_heads, g_heads))
    grad_q = grad_q.transpose(1, 0, 2).reshape(tok, -1)
    attn = attn.transpose(1, 0, 2)
    part_k = part_k.transpose(1, 0, 2).reshape(width, tok, -1)
    part_v = part_v.transpose(1, 0, 2).reshape(width, tok, -1)
    total_k = part_k[REACH].astype(jnp.float32)
    total_v = part_v[REACH].astype(jnp.float32)
    for offset in (-2, -1, 1, 2):
        got = passed_along((part_k[offset + REACH], part_v[offset + REACH]), "ctx", offset)
        total_k = total_k + got[0].astype(jnp.float32)
        total_v = total_v + got[1].astype(jnp.float32)
    attn_flat = attn.reshape(tok, -1)
    norm = float(tok * blocks * lax.axis_size("dp")) ** (-0.5)
    proj = lax.psum_scatter(
        lax.dot_general(
            dy_loc, attn_flat, (((0,), (0,)), ((), ())), preferred_element_type=jnp.float32
        )
        * norm,
        ("dp", "ctx"),
        scatter_dimension=0,
        tiled=True,
    )
    return (
        grad_q.reshape(1, tok, -1),
        total_k.astype(jnp.bfloat16)[None],
        total_v.astype(jnp.bfloat16)[None],
        proj,
    )


def solution(mesh):
    in_specs = (
        P("dp", "ctx", None),
        P("dp", "ctx", None),
        P("dp", "ctx", None),
        P("dp", "ctx", None),
        P(),
    )
    out_specs = (
        P("dp", "ctx", None),
        P("dp", "ctx", None),
        P("dp", "ctx", None),
        P(("dp", "ctx"), None),
    )
    return jax.shard_map(shards, mesh=mesh, in_specs=in_specs, out_specs=out_specs, check_vma=False)
```

profile of v0, /device:TPU:38, one launch (start us, length us, event | category | flops | bytes accessed | tf_op | source)
XLA Modules:
  0.0 517.4 jit_solution(13631272105901636577)
XLA Ops:
  7.2 2.3 copy.39
  9.5 3.8 collective-permute-start.4
  13.3 2.2 copy.36
  15.5 3.8 collective-permute-start
  19.3 5.3 %collective-permute-start.5 = (bf16[512,640]{0,1:T(8,128)(2,1)}, bf16[512,640]{0,1:T(8,128)(2,1)}, u32[]{:S(2)}, u32[]{:S(2)}) collective-permute-start(bf16[512,640]{0,1:T(8,128)(2,1)} %bitcast.12), channel_id=1, source_target_pairs={{0,1},{1,2},{2,3},{3,4},{4,5},{5,6},{6,7},{7,8},{8,9},{9,10},{10,1... | collective-permute-start | bytes 1966088 | tf_op jit(solution)/shard_map/ppermute | solution.py:14
  26.6 2.3 collective-permute-start.7
  28.9 2.5 convolution_convert_fusion.2
  33.2 4.4 collective-permute-start.1
  38.8 4.6 collective-permute-done
  46.4 10.5 %collective-permute-done.5 = bf16[512,640]{0,1:T(8,128)(2,1)} collective-permute-done((bf16[512,640]{0,1:T(8,128)(2,1)}, bf16[512,640]{0,1:T(8,128)(2,1)}, u32[]{:S(2)}, u32[]{:S(2)}) %collective-permute-start.5) | collective-permute-done | bytes 655392 | tf_op jit(solution)/shard_map/ppermute | solution.py:14
  63.5 15.9 %collective-permute-done.1 = bf16[512,640]{0,1:T(8,128)(2,1)S(1)} collective-permute-done((bf16[512,640]{0,1:T(8,128)(2,1)}, bf16[512,640]{0,1:T(8,128)(2,1)S(1)}, u32[]{:S(2)}, u32[]{:S(2)}) %collective-permute-start.1) | collective-permute-done | bytes 655392 | tf_op jit(solution)/shard_map/ppermute | solution.py:14
  80.7 2.6 collective-permute-done.2
  85.1 132.3 %while.17 = (s32[]{:T(128)}, bf16[10,512,64]{1,2,0:T(8,128)(2,1)}, bf16[10,2560,64]{1,2,0:T(8,128)(2,1)}, bf16[10,2560,64]{1,2,0:T(8,128)(2,1)}, bf16[10,512,64]...) while((s32[]{:T(128)}, bf16[10,512,64]{1,2,0:T(8,128)(2,1)}, ...), condition=%wide.region_4.5_spmd.clone, body=%wide.region_0.4_spmd.clone.sunk | while | flops 1024392192 | bytes 36674672 | solution.py:78
  91.8 2.1 multiply_convert_fusion.2
  95.2 2.5 fusion.76
  105.0 2.1 multiply_convert_fusion.2
  108.4 2.5 fusion.76
  118.3 2.1 multiply_convert_fusion.2
  121.7 2.5 fusion.76
  131.5 2.1 multiply_convert_fusion.2
  134.9 2.5 fusion.76
  144.7 2.1 multiply_convert_fusion.2
  148.1 2.5 fusion.76
  157.9 2.1 multiply_convert_fusion.2
  161.4 2.5 fusion.76
  171.1 2.1 multiply_convert_fusion.2
  174.6 2.5 fusion.76
  184.4 2.1 multiply_convert_fusion.2
  187.8 2.5 fusion.76
  201.0 2.5 fusion.76
  210.8 2.1 multiply_convert_fusion.2
  214.3 2.5 fusion.76
  217.4 4.3 fusion.35
  221.7 3.1 fusion.49
  226.8 4.5 collective-permute-start.13
  231.3 3.4 collective-permute-start.14
  234.7 3.6 collective-permute-start.15
  239.9 3.9 collective-permute-start.10
  244.1 5.9 %collective-permute-start.11 = (bf16[512,640]{0,1:T(8,128)(2,1)}, bf16[512,640]{0,1:T(8,128)(2,1)}, u32[]{:S(2)}, u32[]{:S(2)}) collective-permute-start(bf16[512,640]{0,1:T(8,128)(2,1)} %bitcast.31), channel_id=1, source_target_pairs={{0,2},{1,3},{2,4},{3,5},{4,6},{5,7},{6,8},{7,9},{8,10},{9,11},{10,... | collective-permute-start | bytes 1966088 | tf_op jit(solution)/shard_map/ppermute | solution.py:14
  250.0 12.3 %collective-permute-done.13 = bf16[512,640]{0,1:T(8,128)(2,1)S(1)} collective-permute-done((bf16[512,640]{0,1:T(8,128)(2,1)S(1)}, bf16[512,640]{0,1:T(8,128)(2,1)S(1)}, u32[]{:S(2)}, u32[]{:S(2)}) %collective-permute-start.13) | collective-permute-done | bytes 655392 | tf_op jit(solution)/shard_map/ppermute | solution.py:14
  264.4 2.8 collective-permute-done.14
  270.0 2.2 copy.44
  272.1 3.0 fusion.47
  275.1 2.2 copy.46
  277.3 6.9 %collective-permute-done.10 = bf16[512,640]{0,1:T(8,128)(2,1)} collective-permute-done((bf16[512,640]{0,1:T(8,128)(2,1)}, bf16[512,640]{0,1:T(8,128)(2,1)}, u32[]{:S(2)}, u32[]{:S(2)}) %collective-permute-start.10) | collective-permute-done | bytes 655392 | tf_op jit(solution)/shard_map/ppermute | solution.py:14
  284.2 15.7 %collective-permute-done.11 = bf16[512,640]{0,1:T(8,128)(2,1)} collective-permute-done((bf16[512,640]{0,1:T(8,128)(2,1)}, bf16[512,640]{0,1:T(8,128)(2,1)}, u32[]{:S(2)}, u32[]{:S(2)}) %collective-permute-start.11) | collective-permute-done | bytes 655392 | tf_op jit(solution)/shard_map/ppermute | solution.py:14
  299.9 2.1 fusion.46
  303.1 205.5 %all-reduce.3.cloned.1.call-done = f32[1280,640]{0,1:T(8,128)} async-done(((f32[1280,640]{0,1:T(8,128)}), f32[1280,640]{0,1:T(8,128)}) %all-reduce.3.cloned.1.call-update) | async-done | bytes 3276816
  (142 shorter events, 117.2 us)
Async XLA Ops:
  7.2 21.7 %copy-start = (bf16[640,1280]{1,0:T(8,128)(2,1)S(1)}, bf16[640,1280]{1,0:T(8,128)(2,1)}, u32[]{:S(2)}) copy-start(bf16[640,1280]{1,0:T(8,128)(2,1)} %param.11) | copy-start | bytes 4915204
  7.2 501.4 %all-reduce.3.cloned.1.call-start = ((), (), s32[]{:S(2)}) async-start(), calls=%async_computation | async-start | bytes 6553600
  9.5 23.7 %collective-permute-start.4 = (bf16[512,640]{0,1:T(8,128)(2,1)}, bf16[512,640]{0,1:T(8,128)(2,1)}, u32[]{:S(2)}, u32[]{:S(2)}) collective-permute-start(bf16[512,640]{0,1:T(8,128)(2,1)} %bitcast.12), channel_id=1, source_target_pairs={{0,2},{1,3},{2,4},{3,5},{4,6},{5,7},{6,8},{7,9},{8,10},{9,11},{10,... | collective-permute-start | bytes 1966088 | tf_op jit(solution)/shard_map/ppermute | solution.py:14
  15.5 27.9 %collective-permute-start = (bf16[512,640]{0,1:T(8,128)(2,1)}, bf16[512,640]{0,1:T(8,128)(2,1)}, u32[]{:S(2)}, u32[]{:S(2)}) collective-permute-start(bf16[512,640]{0,1:T(8,128)(2,1)} %bitcast.2), channel_id=1, source_target_pairs={{0,2},{1,3},{2,4},{3,5},{4,6},{5,7},{6,8},{7,9},{8,10},{9,11},{10,... | collective-permute-start | bytes 1966088 | tf_op jit(solution)/shard_map/ppermute | solution.py:14
  19.3 37.6 %collective-permute-start.5 = (bf16[512,640]{0,1:T(8,128)(2,1)}, bf16[512,640]{0,1:T(8,128)(2,1)}, u32[]{:S(2)}, u32[]{:S(2)}) collective-permute-start(bf16[512,640]{0,1:T(8,128)(2,1)} %bitcast.12), channel_id=1, source_target_pairs={{0,1},{1,2},{2,3},{3,4},{4,5},{5,6},{6,7},{7,8},{8,9},{9,10},{10,1... | collective-permute-start | bytes 1966088 | tf_op jit(solution)/shard_map/ppermute | solution.py:14
  24.6 36.6 %collective-permute-start.6 = (bf16[512,640]{0,1:T(8,128)(2,1)}, bf16[512,640]{0,1:T(8,128)(2,1)}, u32[]{:S(2)}, u32[]{:S(2)}) collective-permute-start(bf16[512,640]{0,1:T(8,128)(2,1)} %bitcast.12), channel_id=1, source_target_pairs={{1,0},{2,1},{3,2},{4,3},{5,4},{6,5},{7,6},{8,7},{9,8},{10,9},{11,1... | collective-permute-start | bytes 1966088 | tf_op jit(solution)/shard_map/ppermute | solution.py:14
  26.6 35.8 %collective-permute-start.7 = (bf16[512,640]{0,1:T(8,128)(2,1)}, bf16[512,640]{0,1:T(8,128)(2,1)}, u32[]{:S(2)}, u32[]{:S(2)}) collective-permute-start(bf16[512,640]{0,1:T(8,128)(2,1)} %bitcast.12), channel_id=1, source_target_pairs={{2,0},{3,1},{4,2},{5,3},{6,4},{7,5},{8,6},{9,7},{10,8},{11,9},{12,... | collective-permute-start | bytes 1966088 | tf_op jit(solution)/shard_map/ppermute | solution.py:14
  33.2 46.3 %collective-permute-start.1 = (bf16[512,640]{0,1:T(8,128)(2,1)}, bf16[512,640]{0,1:T(8,128)(2,1)S(1)}, u32[]{:S(2)}, u32[]{:S(2)}) collective-permute-start(bf16[512,640]{0,1:T(8,128)(2,1)} %bitcast.2), channel_id=1, source_target_pairs={{0,1},{1,2},{2,3},{3,4},{4,5},{5,6},{6,7},{7,8},{8,9},{9,10},{10,1... | collective-permute-start | bytes 1966088 | tf_op jit(solution)/shard_map/ppermute | solution.py:14
  43.4 40.0 %collective-permute-start.2 = (bf16[512,640]{0,1:T(8,128)(2,1)}, bf16[512,640]{0,1:T(8,128)(2,1)S(1)}, u32[]{:S(2)}, u32[]{:S(2)}) collective-permute-start(bf16[512,640]{0,1:T(8,128)(2,1)} %bitcast.2), channel_id=1, source_target_pairs={{1,0},{2,1},{3,2},{4,3},{5,4},{6,5},{7,6},{8,7},{9,8},{10,9},{11,1... | collective-permute-start | bytes 1966088 | tf_op jit(solution)/shard_map/ppermute | solution.py:14
  56.9 26.5 %collective-permute-start.3 = (bf16[512,640]{0,1:T(8,128)(2,1)}, bf16[512,640]{0,1:T(8,128)(2,1)S(1)}, u32[]{:S(2)}, u32[]{:S(2)}) collective-permute-start(bf16[512,640]{0,1:T(8,128)(2,1)} %bitcast.2), channel_id=1, source_target_pairs={{2,0},{3,1},{4,2},{5,3},{6,4},{7,5},{8,6},{9,7},{10,8},{11,9},{12,... | collective-permute-start | bytes 1966088 | tf_op jit(solution)/shard_map/ppermute | solution.py:14
  63.5 20.0 %copy-start.2 = (bf16[2560,10,64]{0,2,1:T(8,128)(2,1)}, bf16[2560,10,64]{0,2,1:T(8,128)(2,1)S(1)}, u32[]{:S(2)}) copy-start(bf16[2560,10,64]{0,2,1:T(8,128)(2,1)S(1)} %constant_dynamic-update-slice_fusion.5) | copy-start | bytes 9830404
  83.5 1.7 copy-start.1
  221.7 16.6 %copy-start.3 = (bf16[10,2560,64]{1,2,0:T(8,128)(2,1)S(1)}, bf16[10,2560,64]{1,2,0:T(8,128)(2,1)}, u32[]{:S(2)}) copy-start(bf16[10,2560,64]{1,2,0:T(8,128)(2,1)} %get-tuple-element.60) | copy-start | bytes 9830404
  224.8 19.3 %collective-permute-start.12 = (bf16[512,640]{0,1:T(8,128)(2,1)S(1)}, bf16[512,640]{0,1:T(8,128)(2,1)S(1)}, u32[]{:S(2)}, u32[]{:S(2)}) collective-permute-start(bf16[512,640]{0,1:T(8,128)(2,1)S(1)} %bitcast.149), channel_id=1, source_target_pairs={{2,0},{3,1},{4,2},{5,3},{6,4},{7,5},{8,6},{9,7},{10,8},{11,9},{12,... | collective-permute-start | bytes 1966088 | tf_op jit(solution)/shard_map/ppermute | solution.py:14
  226.8 35.6 %collective-permute-start.13 = (bf16[512,640]{0,1:T(8,128)(2,1)S(1)}, bf16[512,640]{0,1:T(8,128)(2,1)S(1)}, u32[]{:S(2)}, u32[]{:S(2)}) collective-permute-start(bf16[512,640]{0,1:T(8,128)(2,1)S(1)} %bitcast.148), channel_id=1, source_target_pairs={{1,0},{2,1},{3,2},{4,3},{5,4},{6,5},{7,6},{8,7},{9,8},{10,9},{11,1... | collective-permute-start | bytes 1966088 | tf_op jit(solution)/shard_map/ppermute | solution.py:14
  231.3 35.9 %collective-permute-start.14 = (bf16[512,640]{0,1:T(8,128)(2,1)S(1)}, bf16[512,640]{0,1:T(8,128)(2,1)S(1)}, u32[]{:S(2)}, u32[]{:S(2)}) collective-permute-start(bf16[512,640]{0,1:T(8,128)(2,1)S(1)} %bitcast.147), channel_id=1, source_target_pairs={{0,1},{1,2},{2,3},{3,4},{4,5},{5,6},{6,7},{7,8},{8,9},{9,10},{10,1... | collective-permute-start | bytes 1966088 | tf_op jit(solution)/shard_map/ppermute | solution.py:14
  234.7 37.5 %collective-permute-start.15 = (bf16[512,640]{0,1:T(8,128)(2,1)}, bf16[512,640]{0,1:T(8,128)(2,1)}, u32[]{:S(2)}, u32[]{:S(2)}) collective-permute-start(bf16[512,640]{0,1:T(8,128)(2,1)} %bitcast.38), channel_id=1, source_target_pairs={{0,2},{1,3},{2,4},{3,5},{4,6},{5,7},{6,8},{7,9},{8,10},{9,11},{10,... | collective-permute-start | bytes 1966088 | tf_op jit(solution)/shard_map/ppermute | solution.py:14
  239.9 44.3 %collective-permute-start.10 = (bf16[512,640]{0,1:T(8,128)(2,1)}, bf16[512,640]{0,1:T(8,128)(2,1)}, u32[]{:S(2)}, u32[]{:S(2)}) collective-permute-start(bf16[512,640]{0,1:T(8,128)(2,1)} %bitcast.30), channel_id=1, source_target_pairs={{0,1},{1,2},{2,3},{3,4},{4,5},{5,6},{6,7},{7,8},{8,9},{9,10},{10,1... | collective-permute-start | bytes 1966088 | tf_op jit(solution)/shard_map/ppermute | solution.py:14
  244.1 23.1 %copy-start.4 = (bf16[512,640]{0,1:T(8,128)(2,1)}, bf16[512,640]{0,1:T(8,128)(2,1)S(1)}, u32[]{:S(2)}) copy-start(bf16[512,640]{0,1:T(8,128)(2,1)S(1)} %collective-permute-done.12) | copy-start | bytes 1966084
  244.1 55.8 %collective-permute-start.11 = (bf16[512,640]{0,1:T(8,128)(2,1)}, bf16[512,640]{0,1:T(8,128)(2,1)}, u32[]{:S(2)}, u32[]{:S(2)}) collective-permute-start(bf16[512,640]{0,1:T(8,128)(2,1)} %bitcast.31), channel_id=1, source_target_pairs={{0,2},{1,3},{2,4},{3,5},{4,6},{5,7},{6,8},{7,9},{8,10},{9,11},{10,... | collective-permute-start | bytes 1966088 | tf_op jit(solution)/shard_map/ppermute | solution.py:14
  262.3 4.9 copy-start.5
  262.3 37.6 %collective-permute-start.8 = (bf16[512,640]{0,1:T(8,128)(2,1)}, bf16[512,640]{0,1:T(8,128)(2,1)}, u32[]{:S(2)}, u32[]{:S(2)}) collective-permute-start(bf16[512,640]{0,1:T(8,128)(2,1)} %bitcast.28), channel_id=1, source_target_pairs={{2,0},{3,1},{4,2},{5,3},{6,4},{7,5},{8,6},{9,7},{10,8},{11,9},{12,... | collective-permute-start | bytes 1966088 | tf_op jit(solution)/shard_map/ppermute | solution.py:14
  267.2 0.8 copy-start.6
  268.0 31.8 %collective-permute-start.9 = (bf16[512,640]{0,1:T(8,128)(2,1)}, bf16[512,640]{0,1:T(8,128)(2,1)}, u32[]{:S(2)}, u32[]{:S(2)}) collective-permute-start(bf16[512,640]{0,1:T(8,128)(2,1)} %bitcast.29), channel_id=1, source_target_pairs={{1,0},{2,1},{3,2},{4,3},{5,4},{6,5},{7,6},{8,7},{9,8},{10,9},{11,1... | collective-permute-start | bytes 1966088 | tf_op jit(solution)/shard_map/ppermute | solution.py:14
Sparse Core Ops, SparseCore 0:
  221.8 286.7 all-reduce.2
where the time goes:
time: 523 us; the launch traced here: 517 us
  waiting for transfers between devices  277 us (53%)
  matrix products  123 us (24%)
  starting transfers between devices  52.7 us (10%)
  local copies, waits for them, and re-layouts  36.2 us (7%)
  between operations  14.4 us (3%)
  other arithmetic  13.6 us (3%)
    unnamed x2, waiting for transfers between devices  205 us
    ppermute x16, waiting for transfers between devices, passed_along(): return lax.ppermute(x, axis, pairs)  71.7 us
    ppermute x16, starting transfers between devices, passed_along(): return lax.ppermute(x, axis, pairs)  52.6 us
    dot_general x10, matrix products, head_grads(): jnp.dot(dscore, k_one, preferred_element_type=jnp.float32) * scale  25.1 us
    unnamed x30, local copies, waits for them, and re-layouts  22.7 us
    dot_general x10, matrix products, head_grads(): lax.dot_general(g_one, v_one, (((1,), (1,)), ((), ())), preferred_element...  21.1 us
    dot_general x10, matrix products, head_grads(): jnp.dot(probs_b, v_one, preferred_element_type=jnp.float32)  19.8 us
    dot_general x10, matrix products, head_grads(): lax.dot_general(q_one, k_one, (((1,), (1,)), ((), ())), preferred_element...  19.7 us
  transfers between devices with their start and end apart: 17, of which 10 were waited for; matrix products, arithmetic and copies ran while one was open for 6% of the time, Pallas kernels for 0%

commit v1 on v0

--- a/solution.py
+++ b/solution.py
@@ -88,15 +88,17 @@
         total_v = total_v + got[1].astype(jnp.float32)
     attn_flat = attn.reshape(tok, -1)
     norm = float(tok * blocks * lax.axis_size("dp")) ** (-0.5)
-    proj = lax.psum_scatter(
-        lax.dot_general(
-            dy_loc, attn_flat, (((0,), (0,)), ((), ())), preferred_element_type=jnp.float32
-        )
-        * norm,
-        ("dp", "ctx"),
-        scatter_dimension=0,
-        tiled=True,
+    term = lax.dot_general(
+        dy_loc, attn_flat, (((0,), (0,)), ((), ())), preferred_element_type=jnp.float32
     )
+    term = (term * norm).astype(jnp.bfloat16)
+    dps = lax.axis_size("dp")
+    term = term.reshape(dps, -1, term.shape[1])
+    term = lax.all_to_all(term, "dp", 0, 0)
+    term = jnp.sum(term.astype(jnp.float32), axis=0)
+    term = term.reshape(blocks, -1, term.shape[1])
+    term = lax.all_to_all(term, "ctx", 0, 0)
+    proj = jnp.sum(term, axis=0)
     return (
         grad_q.reshape(1, tok, -1),
         total_k.astype(jnp.bfloat16)[None],

time: 523 us -> 336 us (0.64)
  waiting for transfers between devices: 277 us -> 86.3 us
  starting transfers between devices: 52.7 us -> 73.9 us
  between operations: 14.4 us -> 1.08 us
    unnamed x2 -> x0, waiting for transfers between devices: 205 us -> none
    all_to_all x0 -> x2, starting transfers between devices: none -> 18.7 us  [the longest x1 11.2 us: shards(): term = lax.all_to_all(term, 'ctx', 0, 0)]
    all_to_all x0 -> x2, waiting for transfers between devices: none -> 7.65 us  [the longest x1 7.65 us: shards(): term = lax.all_to_all(term, 'ctx', 0, 0)]
    ppermute x16, waiting for transfers between devices: 71.7 us -> 78.7 us  [passed_along(): return lax.ppermute(x, axis, pairs)]
  transfers between devices with their start and end apart: 17 -> 18, of which waited for: 10 -> 7; matrix products, arithmetic and copies ran while one was open for 6% -> 9% of each run, Pallas kernels for 0% -> 0%
where the time goes in v1:
time: 336 us; the launch traced here: 333 us
  matrix products  121 us (36%)
  waiting for transfers between devices  86.3 us (26%)
  starting transfers between devices  73.9 us (22%)
  local copies, waits for them, and re-layouts  36.7 us (11%)
  other arithmetic  13.8 us (4%)
    ppermute x16, waiting for transfers between devices, passed_along(): return lax.ppermute(x, axis, pairs)  78.7 us
    ppermute x16, starting transfers between devices, passed_along(): return lax.ppermute(x, axis, pairs)  55.2 us
    dot_general x10, matrix products, head_grads(): jnp.dot(dscore, k_one, preferred_element_type=jnp.float32) * scale  25.1 us
    dot_general x10, matrix products, head_grads(): lax.dot_general(g_one, v_one, (((1,), (1,)), ((), ())), preferred_element...  21.1 us
    dot_general x10, matrix products, head_grads(): jnp.dot(probs_b, v_one, preferred_element_type=jnp.float32)  19.8 us
    dot_general x10, matrix products, head_grads(): lax.dot_general(q_one, k_one, (((1,), (1,)), ((), ())), preferred_element...  19.7 us
    unnamed x30, local copies, waits for them, and re-layouts  19.7 us
    dot_general x10, matrix products, head_grads(): lax.dot_general(probs_b, g_one, (((0,), (0,)), ((), ())), preferred_eleme...  17.5 us
  transfers between devices with their start and end apart: 18, of which 7 were waited for; matrix products, arithmetic and copies ran while one was open for 9% of the time, Pallas kernels for 0%

profile of v1, /device:TPU:38, one launch (start us, length us, event | category | flops | bytes accessed | tf_op | source)
XLA Modules:
  0.0 333.4 jit_solution(505133413899741295)
XLA Ops:
  0.6 2.3 copy.25
  2.9 3.8 %collective-permute-start.4 = (bf16[512,640]{0,1:T(8,128)(2,1)}, bf16[512,640]{0,1:T(8,128)(2,1)}, u32[]{:S(2)}, u32[]{:S(2)}) collective-permute-start(bf16[512,640]{0,1:T(8,128)(2,1)} %bitcast.12), channel_id=1, source_target_pairs={{0,2},{1,3},{2,4},{3,5},{4,6},{5,7},{6,8},{7,9},{8,10},{9,11},{10,... | collective-permute-start | bytes 1966088 | tf_op jit(solution)/shard_map/ppermute | solution.py:14
  6.8 2.2 copy.22
  8.9 3.8 %collective-permute-start = (bf16[512,640]{0,1:T(8,128)(2,1)}, bf16[512,640]{0,1:T(8,128)(2,1)}, u32[]{:S(2)}, u32[]{:S(2)}) collective-permute-start(bf16[512,640]{0,1:T(8,128)(2,1)} %bitcast.2), channel_id=1, source_target_pairs={{0,2},{1,3},{2,4},{3,5},{4,6},{5,7},{6,8},{7,9},{8,10},{9,11},{10,... | collective-permute-start | bytes 1966088 | tf_op jit(solution)/shard_map/ppermute | solution.py:14
  12.8 5.3 %collective-permute-start.5 = (bf16[512,640]{0,1:T(8,128)(2,1)}, bf16[512,640]{0,1:T(8,128)(2,1)}, u32[]{:S(2)}, u32[]{:S(2)}) collective-permute-start(bf16[512,640]{0,1:T(8,128)(2,1)} %bitcast.12), channel_id=1, source_target_pairs={{0,1},{1,2},{2,3},{3,4},{4,5},{5,6},{6,7},{7,8},{8,9},{9,10},{10,1... | collective-permute-start | bytes 1966088 | tf_op jit(solution)/shard_map/ppermute | solution.py:14
  20.0 2.4 collective-permute-start.7
  22.4 2.5 convolution_convert_fusion.2
  26.7 4.4 %collective-permute-start.1 = (bf16[512,640]{0,1:T(8,128)(2,1)}, bf16[512,640]{0,1:T(8,128)(2,1)S(1)}, u32[]{:S(2)}, u32[]{:S(2)}) collective-permute-start(bf16[512,640]{0,1:T(8,128)(2,1)} %bitcast.2), channel_id=1, source_target_pairs={{0,1},{1,2},{2,3},{3,4},{4,5},{5,6},{6,7},{7,8},{8,9},{9,10},{10,1... | collective-permute-start | bytes 1966088 | tf_op jit(solution)/shard_map/ppermute | solution.py:14
  32.2 4.6 %collective-permute-done = bf16[512,640]{0,1:T(8,128)(2,1)} collective-permute-done((bf16[512,640]{0,1:T(8,128)(2,1)}, bf16[512,640]{0,1:T(8,128)(2,1)}, u32[]{:S(2)}, u32[]{:S(2)}) %collective-permute-start) | collective-permute-done | bytes 655392 | tf_op jit(solution)/shard_map/ppermute | solution.py:14
  39.9 10.5 %collective-permute-done.5 = bf16[512,640]{0,1:T(8,128)(2,1)} collective-permute-done((bf16[512,640]{0,1:T(8,128)(2,1)}, bf16[512,640]{0,1:T(8,128)(2,1)}, u32[]{:S(2)}, u32[]{:S(2)}) %collective-permute-start.5) | collective-permute-done | bytes 655392 | tf_op jit(solution)/shard_map/ppermute | solution.py:14
  57.0 15.9 %collective-permute-done.1 = bf16[512,640]{0,1:T(8,128)(2,1)S(1)} collective-permute-done((bf16[512,640]{0,1:T(8,128)(2,1)}, bf16[512,640]{0,1:T(8,128)(2,1)S(1)}, u32[]{:S(2)}, u32[]{:S(2)}) %collective-permute-start.1) | collective-permute-done | bytes 655392 | tf_op jit(solution)/shard_map/ppermute | solution.py:14
  74.1 2.6 collective-permute-done.2
  78.6 132.2 %while.17 = (s32[]{:T(128)}, bf16[10,512,64]{1,2,0:T(8,128)(2,1)}, bf16[10,2560,64]{1,2,0:T(8,128)(2,1)}, bf16[10,2560,64]{1,2,0:T(8,128)(2,1)}, bf16[10,512,64]...) while((s32[]{:T(128)}, bf16[10,512,64]{1,2,0:T(8,128)(2,1)}, ...), condition=%wide.region_4.5_spmd.clone, body=%wide.region_0.4_spmd.clone.sunk | while | flops 1024392192 | bytes 36674672 | solution.py:78
  88.7 2.5 fusion.77
  98.5 2.1 multiply_convert_fusion.2
  101.9 2.5 fusion.77
  111.7 2.1 multiply_convert_fusion.2
  115.1 2.5 fusion.77
  124.9 2.1 multiply_convert_fusion.2
  128.4 2.5 fusion.77
  138.2 2.1 multiply_convert_fusion.2
  141.6 2.5 fusion.77
  151.4 2.1 multiply_convert_fusion.2
  154.8 2.5 fusion.77
  164.6 2.1 multiply_convert_fusion.2
  168.1 2.5 fusion.77
  177.9 2.1 multiply_convert_fusion.2
  181.3 2.5 fusion.77
  194.5 2.5 fusion.77
  204.3 2.1 multiply_convert_fusion.2
  207.7 2.5 fusion.77
  210.9 2.5 fusion.36
  213.4 2.2 copy.30
  215.7 7.5 %all-to-all-start = ((bf16[16,80,640]{2,1,0:T(8,128)(2,1)}), bf16[16,80,640]{2,1,0:T(8,128)(2,1)S(1)}, u32[]{:S(2)}, u32[]{:S(2)}) async-start(bf16[16,80,640]{2,1,0:T(8,128)(2,1)} %bitcast.140), calls=%async_computation | async-start | bytes 3276800 | tf_op jit(solution)/shard_map/all_to_all | solution.py:97
  223.1 3.4 %fusion.50 = (bf16[512,10,64]{0,2,1:T(8,128)(2,1)}, bf16[512,10,64]{0,2,1:T(8,128)(2,1)}, bf16[512,10,64]{0,2,1:T(8,128)(2,1)S(1)}, bf16[512,10,64]{0,2,1:T(8,128)(2,1)S(1)}, bf16[512,10,64]{0,2,1:T(8,128)(2,1)S(1)}) fusion(bf16[2560,10,64]{0,2,1:T(8,128)(2,1)} %bitcast.145), kind=kLoop, calls=%fused_computation.73 | loop fusion | bytes 6553600 | tf_op jit(solution)/shard_map/slice | solution.py:84
  228.5 4.6 %collective-permute-start.13 = (bf16[512,640]{0,1:T(8,128)(2,1)S(1)}, bf16[512,640]{0,1:T(8,128)(2,1)S(1)}, u32[]{:S(2)}, u32[]{:S(2)}) collective-permute-start(bf16[512,640]{0,1:T(8,128)(2,1)S(1)} %bitcast.148), channel_id=1, source_target_pairs={{1,0},{2,1},{3,2},{4,3},{5,4},{6,5},{7,6},{8,7},{9,8},{10,9},{11,1... | collective-permute-start | bytes 1966088 | tf_op jit(solution)/shard_map/ppermute | solution.py:14
  233.0 3.4 %collective-permute-start.14 = (bf16[512,640]{0,1:T(8,128)(2,1)S(1)}, bf16[512,640]{0,1:T(8,128)(2,1)S(1)}, u32[]{:S(2)}, u32[]{:S(2)}) collective-permute-start(bf16[512,640]{0,1:T(8,128)(2,1)S(1)} %bitcast.147), channel_id=1, source_target_pairs={{0,1},{1,2},{2,3},{3,4},{4,5},{5,6},{6,7},{7,8},{8,9},{9,10},{10,1... | collective-permute-start | bytes 1966088 | tf_op jit(solution)/shard_map/ppermute | solution.py:14
  236.4 3.6 %collective-permute-start.15 = (bf16[512,640]{0,1:T(8,128)(2,1)}, bf16[512,640]{0,1:T(8,128)(2,1)}, u32[]{:S(2)}, u32[]{:S(2)}) collective-permute-start(bf16[512,640]{0,1:T(8,128)(2,1)} %bitcast.38), channel_id=1, source_target_pairs={{0,2},{1,3},{2,4},{3,5},{4,6},{5,7},{6,8},{7,9},{8,10},{9,11},{10,... | collective-permute-start | bytes 1966088 | tf_op jit(solution)/shard_map/ppermute | solution.py:14
  241.8 3.9 %collective-permute-start.10 = (bf16[512,640]{0,1:T(8,128)(2,1)}, bf16[512,640]{0,1:T(8,128)(2,1)}, u32[]{:S(2)}, u32[]{:S(2)}) collective-permute-start(bf16[512,640]{0,1:T(8,128)(2,1)} %bitcast.30), channel_id=1, source_target_pairs={{0,1},{1,2},{2,3},{3,4},{4,5},{5,6},{6,7},{7,8},{8,9},{9,10},{10,1... | collective-permute-start | bytes 1966088 | tf_op jit(solution)/shard_map/ppermute | solution.py:14
  245.7 6.1 %collective-permute-start.11 = (bf16[512,640]{0,1:T(8,128)(2,1)}, bf16[512,640]{0,1:T(8,128)(2,1)}, u32[]{:S(2)}, u32[]{:S(2)}) collective-permute-start(bf16[512,640]{0,1:T(8,128)(2,1)} %bitcast.31), channel_id=1, source_target_pairs={{0,2},{1,3},{2,4},{3,5},{4,6},{5,7},{6,8},{7,9},{8,10},{9,11},{10,... | collective-permute-start | bytes 1966088 | tf_op jit(solution)/shard_map/ppermute | solution.py:14
  251.8 32.4 %collective-permute-done.13 = bf16[512,640]{0,1:T(8,128)(2,1)S(1)} collective-permute-done((bf16[512,640]{0,1:T(8,128)(2,1)S(1)}, bf16[512,640]{0,1:T(8,128)(2,1)S(1)}, u32[]{:S(2)}, u32[]{:S(2)}) %collective-permute-start.13) | collective-permute-done | bytes 655392 | tf_op jit(solution)/shard_map/ppermute | solution.py:14
  287.0 4.4 %collective-permute-start.9 = (bf16[512,640]{0,1:T(8,128)(2,1)}, bf16[512,640]{0,1:T(8,128)(2,1)}, u32[]{:S(2)}, u32[]{:S(2)}) collective-permute-start(bf16[512,640]{0,1:T(8,128)(2,1)} %bitcast.29), channel_id=1, source_target_pairs={{1,0},{2,1},{3,2},{4,3},{5,4},{6,5},{7,6},{8,7},{9,8},{10,9},{11,1... | collective-permute-start | bytes 1966088 | tf_op jit(solution)/shard_map/ppermute | solution.py:14
  291.4 2.2 copy.31
  294.6 11.2 %all-to-all-start.1 = ((f32[16,5,640]{2,1,0:T(8,128)}), f32[16,5,640]{2,1,0:T(8,128)S(1)}, u32[]{:S(2)}, u32[]{:S(2)}) async-start(f32[16,5,640]{2,1,0:T(8,128)} %reshape.74), calls=%async_computation.1 | async-start | bytes 655360 | tf_op jit(solution)/shard_map/all_to_all | solution.py:100
  305.8 2.3 fusion.48
  309.2 12.6 %collective-permute-done.9 = bf16[512,640]{0,1:T(8,128)(2,1)} collective-permute-done((bf16[512,640]{0,1:T(8,128)(2,1)}, bf16[512,640]{0,1:T(8,128)(2,1)}, u32[]{:S(2)}, u32[]{:S(2)}) %collective-permute-start.9) | collective-permute-done | bytes 655392 | tf_op jit(solution)/shard_map/ppermute | solution.py:14
  321.9 2.1 fusion.47
  325.1 7.6 %all-to-all-done.1 = f32[16,5,640]{2,1,0:T(8,128)S(1)} async-done(((f32[16,5,640]{2,1,0:T(8,128)}), f32[16,5,640]{2,1,0:T(8,128)S(1)}, u32[]{:S(2)}, u32[]{:S(2)}) %all-to-all-start.1) | async-done | bytes 204832 | tf_op jit(solution)/shard_map/all_to_all | solution.py:100
  (147 shorter events, 117.7 us)
Async XLA Ops:
  0.6 21.7 %copy-start = (bf16[640,1280]{1,0:T(8,128)(2,1)S(1)}, bf16[640,1280]{1,0:T(8,128)(2,1)}, u32[]{:S(2)}) copy-start(bf16[640,1280]{1,0:T(8,128)(2,1)} %param.11) | copy-start | bytes 4915204
  2.9 23.8 %collective-permute-start.4 = (bf16[512,640]{0,1:T(8,128)(2,1)}, bf16[512,640]{0,1:T(8,128)(2,1)}, u32[]{:S(2)}, u32[]{:S(2)}) collective-permute-start(bf16[512,640]{0,1:T(8,128)(2,1)} %bitcast.12), channel_id=1, source_target_pairs={{0,2},{1,3},{2,4},{3,5},{4,6},{5,7},{6,8},{7,9},{8,10},{9,11},{10,... | collective-permute-start | bytes 1966088 | tf_op jit(solution)/shard_map/ppermute | solution.py:14
  8.9 27.9 %collective-permute-start = (bf16[512,640]{0,1:T(8,128)(2,1)}, bf16[512,640]{0,1:T(8,128)(2,1)}, u32[]{:S(2)}, u32[]{:S(2)}) collective-permute-start(bf16[512,640]{0,1:T(8,128)(2,1)} %bitcast.2), channel_id=1, source_target_pairs={{0,2},{1,3},{2,4},{3,5},{4,6},{5,7},{6,8},{7,9},{8,10},{9,11},{10,... | collective-permute-start | bytes 1966088 | tf_op jit(solution)/shard_map/ppermute | solution.py:14
  12.8 37.6 %collective-permute-start.5 = (bf16[512,640]{0,1:T(8,128)(2,1)}, bf16[512,640]{0,1:T(8,128)(2,1)}, u32[]{:S(2)}, u32[]{:S(2)}) collective-permute-start(bf16[512,640]{0,1:T(8,128)(2,1)} %bitcast.12), channel_id=1, source_target_pairs={{0,1},{1,2},{2,3},{3,4},{4,5},{5,6},{6,7},{7,8},{8,9},{9,10},{10,1... | collective-permute-start | bytes 1966088 | tf_op jit(solution)/shard_map/ppermute | solution.py:14
  18.1 36.6 %collective-permute-start.6 = (bf16[512,640]{0,1:T(8,128)(2,1)}, bf16[512,640]{0,1:T(8,128)(2,1)}, u32[]{:S(2)}, u32[]{:S(2)}) collective-permute-start(bf16[512,640]{0,1:T(8,128)(2,1)} %bitcast.12), channel_id=1, source_target_pairs={{1,0},{2,1},{3,2},{4,3},{5,4},{6,5},{7,6},{8,7},{9,8},{10,9},{11,1... | collective-permute-start | bytes 1966088 | tf_op jit(solution)/shard_map/ppermute | solution.py:14
  20.0 35.8 %collective-permute-start.7 = (bf16[512,640]{0,1:T(8,128)(2,1)}, bf16[512,640]{0,1:T(8,128)(2,1)}, u32[]{:S(2)}, u32[]{:S(2)}) collective-permute-start(bf16[512,640]{0,1:T(8,128)(2,1)} %bitcast.12), channel_id=1, source_target_pairs={{2,0},{3,1},{4,2},{5,3},{6,4},{7,5},{8,6},{9,7},{10,8},{11,9},{12,... | collective-permute-start | bytes 1966088 | tf_op jit(solution)/shard_map/ppermute | solution.py:14
  26.7 46.2 %collective-permute-start.1 = (bf16[512,640]{0,1:T(8,128)(2,1)}, bf16[512,640]{0,1:T(8,128)(2,1)S(1)}, u32[]{:S(2)}, u32[]{:S(2)}) collective-permute-start(bf16[512,640]{0,1:T(8,128)(2,1)} %bitcast.2), channel_id=1, source_target_pairs={{0,1},{1,2},{2,3},{3,4},{4,5},{5,6},{6,7},{7,8},{8,9},{9,10},{10,1... | collective-permute-start | bytes 1966088 | tf_op jit(solution)/shard_map/ppermute | solution.py:14
  36.8 40.0 %collective-permute-start.2 = (bf16[512,640]{0,1:T(8,128)(2,1)}, bf16[512,640]{0,1:T(8,128)(2,1)S(1)}, u32[]{:S(2)}, u32[]{:S(2)}) collective-permute-start(bf16[512,640]{0,1:T(8,128)(2,1)} %bitcast.2), channel_id=1, source_target_pairs={{1,0},{2,1},{3,2},{4,3},{5,4},{6,5},{7,6},{8,7},{9,8},{10,9},{11,1... | collective-permute-start | bytes 1966088 | tf_op jit(solution)/shard_map/ppermute | solution.py:14
  50.3 26.5 %collective-permute-start.3 = (bf16[512,640]{0,1:T(8,128)(2,1)}, bf16[512,640]{0,1:T(8,128)(2,1)S(1)}, u32[]{:S(2)}, u32[]{:S(2)}) collective-permute-start(bf16[512,640]{0,1:T(8,128)(2,1)} %bitcast.2), channel_id=1, source_target_pairs={{2,0},{3,1},{4,2},{5,3},{6,4},{7,5},{8,6},{9,7},{10,8},{11,9},{12,... | collective-permute-start | bytes 1966088 | tf_op jit(solution)/shard_map/ppermute | solution.py:14
  57.0 20.0 %copy-start.2 = (bf16[2560,10,64]{0,2,1:T(8,128)(2,1)}, bf16[2560,10,64]{0,2,1:T(8,128)(2,1)S(1)}, u32[]{:S(2)}) copy-start(bf16[2560,10,64]{0,2,1:T(8,128)(2,1)S(1)} %constant_dynamic-update-slice_fusion.5) | copy-start | bytes 9830404
  76.9 1.7 copy-start.1
  215.7 77.9 %all-to-all-start = ((bf16[16,80,640]{2,1,0:T(8,128)(2,1)}), bf16[16,80,640]{2,1,0:T(8,128)(2,1)S(1)}, u32[]{:S(2)}, u32[]{:S(2)}) async-start(bf16[16,80,640]{2,1,0:T(8,128)(2,1)} %bitcast.140), calls=%async_computation | async-start | bytes 3276800 | tf_op jit(solution)/shard_map/all_to_all | solution.py:97
  223.1 16.9 %copy-start.3 = (bf16[10,2560,64]{1,2,0:T(8,128)(2,1)S(1)}, bf16[10,2560,64]{1,2,0:T(8,128)(2,1)}, u32[]{:S(2)}) copy-start(bf16[10,2560,64]{1,2,0:T(8,128)(2,1)} %get-tuple-element.60) | copy-start | bytes 9830404
  226.6 19.1 %collective-permute-start.12 = (bf16[512,640]{0,1:T(8,128)(2,1)S(1)}, bf16[512,640]{0,1:T(8,128)(2,1)S(1)}, u32[]{:S(2)}, u32[]{:S(2)}) collective-permute-start(bf16[512,640]{0,1:T(8,128)(2,1)S(1)} %bitcast.149), channel_id=1, source_target_pairs={{2,0},{3,1},{4,2},{5,3},{6,4},{7,5},{8,6},{9,7},{10,8},{11,9},{12,... | collective-permute-start | bytes 1966088 | tf_op jit(solution)/shard_map/ppermute | solution.py:14
  228.5 55.8 %collective-permute-start.13 = (bf16[512,640]{0,1:T(8,128)(2,1)S(1)}, bf16[512,640]{0,1:T(8,128)(2,1)S(1)}, u32[]{:S(2)}, u32[]{:S(2)}) collective-permute-start(bf16[512,640]{0,1:T(8,128)(2,1)S(1)} %bitcast.148), channel_id=1, source_target_pairs={{1,0},{2,1},{3,2},{4,3},{5,4},{6,5},{7,6},{8,7},{9,8},{10,9},{11,1... | collective-permute-start | bytes 1966088 | tf_op jit(solution)/shard_map/ppermute | solution.py:14
  233.0 53.1 %collective-permute-start.14 = (bf16[512,640]{0,1:T(8,128)(2,1)S(1)}, bf16[512,640]{0,1:T(8,128)(2,1)S(1)}, u32[]{:S(2)}, u32[]{:S(2)}) collective-permute-start(bf16[512,640]{0,1:T(8,128)(2,1)S(1)} %bitcast.147), channel_id=1, source_target_pairs={{0,1},{1,2},{2,3},{3,4},{4,5},{5,6},{6,7},{7,8},{8,9},{9,10},{10,1... | collective-permute-start | bytes 1966088 | tf_op jit(solution)/shard_map/ppermute | solution.py:14
  236.4 69.4 %collective-permute-start.15 = (bf16[512,640]{0,1:T(8,128)(2,1)}, bf16[512,640]{0,1:T(8,128)(2,1)}, u32[]{:S(2)}, u32[]{:S(2)}) collective-permute-start(bf16[512,640]{0,1:T(8,128)(2,1)} %bitcast.38), channel_id=1, source_target_pairs={{0,2},{1,3},{2,4},{3,5},{4,6},{5,7},{6,8},{7,9},{8,10},{9,11},{10,... | collective-permute-start | bytes 1966088 | tf_op jit(solution)/shard_map/ppermute | solution.py:14
  241.8 67.5 %collective-permute-start.10 = (bf16[512,640]{0,1:T(8,128)(2,1)}, bf16[512,640]{0,1:T(8,128)(2,1)}, u32[]{:S(2)}, u32[]{:S(2)}) collective-permute-start(bf16[512,640]{0,1:T(8,128)(2,1)} %bitcast.30), channel_id=1, source_target_pairs={{0,1},{1,2},{2,3},{3,4},{4,5},{5,6},{6,7},{7,8},{8,9},{9,10},{10,1... | collective-permute-start | bytes 1966088 | tf_op jit(solution)/shard_map/ppermute | solution.py:14
  245.7 40.5 %copy-start.5 = (bf16[512,640]{0,1:T(8,128)(2,1)}, bf16[512,640]{0,1:T(8,128)(2,1)S(1)}, u32[]{:S(2)}) copy-start(bf16[512,640]{0,1:T(8,128)(2,1)S(1)} %collective-permute-done.12) | copy-start | bytes 1966084
  245.7 63.5 %collective-permute-start.11 = (bf16[512,640]{0,1:T(8,128)(2,1)}, bf16[512,640]{0,1:T(8,128)(2,1)}, u32[]{:S(2)}, u32[]{:S(2)}) collective-permute-start(bf16[512,640]{0,1:T(8,128)(2,1)} %bitcast.31), channel_id=1, source_target_pairs={{0,2},{1,3},{2,4},{3,5},{4,6},{5,7},{6,8},{7,9},{8,10},{9,11},{10,... | collective-permute-start | bytes 1966088 | tf_op jit(solution)/shard_map/ppermute | solution.py:14
  284.2 2.0 copy-start.6
  284.2 25.0 %collective-permute-start.8 = (bf16[512,640]{0,1:T(8,128)(2,1)}, bf16[512,640]{0,1:T(8,128)(2,1)}, u32[]{:S(2)}, u32[]{:S(2)}) collective-permute-start(bf16[512,640]{0,1:T(8,128)(2,1)} %bitcast.28), channel_id=1, source_target_pairs={{2,0},{3,1},{4,2},{5,3},{6,4},{7,5},{8,6},{9,7},{10,8},{11,9},{12,... | collective-permute-start | bytes 1966088 | tf_op jit(solution)/shard_map/ppermute | solution.py:14
  286.2 0.9 copy-start.7
  287.0 34.9 %collective-permute-start.9 = (bf16[512,640]{0,1:T(8,128)(2,1)}, bf16[512,640]{0,1:T(8,128)(2,1)}, u32[]{:S(2)}, u32[]{:S(2)}) collective-permute-start(bf16[512,640]{0,1:T(8,128)(2,1)} %bitcast.29), channel_id=1, source_target_pairs={{1,0},{2,1},{3,2},{4,3},{5,4},{6,5},{7,6},{8,7},{9,8},{10,9},{11,1... | collective-permute-start | bytes 1966088 | tf_op jit(solution)/shard_map/ppermute | solution.py:14
  293.8 28.1 %copy-start.4 = (bf16[512,10,64]{0,2,1:T(8,128)(2,1)S(1)}, bf16[512,10,64]{0,2,1:T(8,128)(2,1)}, u32[]{:S(2)}) copy-start(bf16[512,10,64]{0,2,1:T(8,128)(2,1)} %get-tuple-element.129) | copy-start | bytes 1966084
  294.6 38.1 %all-to-all-start.1 = ((f32[16,5,640]{2,1,0:T(8,128)}), f32[16,5,640]{2,1,0:T(8,128)S(1)}, u32[]{:S(2)}, u32[]{:S(2)}) async-start(f32[16,5,640]{2,1,0:T(8,128)} %reshape.74), calls=%async_computation.1 | async-start | bytes 655360 | tf_op jit(solution)/shard_map/all_to_all | solution.py:100

commit v2 on v1

v2 whole, which is shorter than its diff:
```python
import functools
import math

import jax
import jax.numpy as jnp
from jax import lax
from jax.experimental import pallas as pl
from jax.experimental.pallas import tpu as pltpu
from jax.sharding import PartitionSpec as P

HEADS = 10
HDIM = 64
HALF = HEADS // 2
ROWS = HALF * HDIM
TOK = 512
SCALE = HDIM ** (-0.5)
BASE2 = SCALE * math.log2(math.e)
BIG = 1e30
F32 = jnp.float32
BF16 = jnp.bfloat16

UNSEEN = ((5,), (0,))


def params(us):
    return dict(
        compiler_params=pltpu.CompilerParams(vmem_limit_bytes=60 * 2**20),
        cost_estimate=pl.CostEstimate(
            flops=int(us * 1.15e9), bytes_accessed=int(us * 1e5), transcendentals=0
        ),
    )


def mm(a, b, ca, cb):
    return lax.dot_general(a, b, (((ca,), (cb,)), ((), ())), preferred_element_type=F32)


def head_block(parts):
    return pl.BlockSpec((parts, HDIM, TOK), lambda h, s: (0, h, 0))


LSE_BLOCK = pl.BlockSpec((1, 2, TOK), lambda h, s: (h, 0, 0))


def head_major(parts, dtype=BF16):
    return jax.ShapeDtypeStruct((parts, ROWS, TOK), dtype)


def whole(shape):
    return pl.BlockSpec(shape, lambda i, s: (0,) * len(shape))


def halves(x):
    return x[:ROWS], x[ROWS:]


def in_order(odd, mine, partners):
    first = jnp.where(odd, partners, mine)
    return jnp.concatenate([first, jnp.where(odd, mine, partners)], axis=0)


def split_kernel(scal, a_ref, b_ref, mine, send):
    odd = scal[2] > 0
    for n, ref in enumerate((a_ref, b_ref)):
        low, high = halves(jnp.transpose(ref[...]))
        mine[n] = jnp.where(odd, high, low)
        send[n] = jnp.where(odd, low, high)


def split_heads(scal, a, b):
    return pl.pallas_call(
        split_kernel,
        grid_spec=pltpu.PrefetchScalarGridSpec(
            num_scalar_prefetch=1,
            grid=(1,),
            in_specs=[whole(a.shape)] * 2,
            out_specs=[whole((2, ROWS, TOK))] * 2,
        ),
        out_shape=[head_major(2)] * 2,
        name="split_kv",
        **params(3),
    )(scal, a, b)


def split_q_kernel(scal, q_ref, dy_ref, w_ref, mine, send):
    odd = scal[2] > 0
    grad = mm(w_ref[...], dy_ref[...], 1, 1).astype(BF16)
    for n, turned in enumerate((jnp.transpose(q_ref[...]), grad)):
        low, high = halves(turned)
        mine[n] = jnp.where(odd, high, low)
        send[n] = jnp.where(odd, low, high)


def split_queries(scal, q, dy, w):
    return pl.pallas_call(
        split_q_kernel,
        grid_spec=pltpu.PrefetchScalarGridSpec(
            num_scalar_prefetch=1,
            grid=(1,),
            in_specs=[whole(q.shape), whole(dy.shape), whole(w.shape)],
            out_specs=[whole((2, ROWS, TOK))] * 2,
        ),
        out_shape=[head_major(2)] * 2,
        name="split_q_and_grad",
        **params(5),
    )(scal, q, dy, w)


def side_flag(scal, j):
    return None if j in (2, 3) else scal[0] if j < 2 else scal[1]


def forward_kernel(scal, qm, qp, *refs):
    kv = refs[:6]
    om, op, lse = refs[6:]
    qs = (qm[0], qp[0])
    units = [(j, i) for j in (2, 3, 1, 4, 0, 5) for i in (0, 1) if j not in UNSEEN[i]]
    turned = {}

    def scores(j, i):
        if j not in turned:
            turned[j] = jnp.transpose(kv[j][0])
        return mm(turned[j], qs[i], 1, 0)

    top = [None, None]
    total = [None, None]
    out = [None, None]
    ahead = scores(*units[0])
    for n, (j, i) in enumerate(units):
        s = ahead
        if n + 1 < len(units):
            ahead = scores(*units[n + 1])
        flag = side_flag(scal, j)
        here = jnp.max(s, axis=0, keepdims=True) * BASE2
        if flag is not None:
            here = jnp.where(flag > 0, here, -BIG)
        first = top[i] is None
        new = here if first else jnp.maximum(top[i], here)
        sub = new if flag is None else jnp.where(flag > 0, new, BIG)
        e = jnp.exp2(s * BASE2 - sub)
        part = jnp.sum(e, axis=0, keepdims=True)
        pv = mm(kv[j][1], e.astype(BF16), 1, 0)
        if first:
            total[i], out[i] = part, pv
        else:
            fade = jnp.exp2(top[i] - new)
            total[i] = total[i] * fade + part
            out[i] = out[i] * fade + pv
        top[i] = new
    for i, ref in ((0, om), (1, op)):
        ref[0] = (out[i] * (1.0 / total[i])).astype(BF16)
        lse[0, i : i + 1, :] = top[i] + jnp.log2(total[i])


def forward(scal, qg, kv):
    return pl.pallas_call(
        forward_kernel,
        grid_spec=pltpu.PrefetchScalarGridSpec(
            num_scalar_prefetch=1,
            grid=(HALF,),
            in_specs=[head_block(1)] * 2 + [head_block(2)] * 6,
            out_specs=[head_block(1)] * 2 + [LSE_BLOCK],
        ),
        out_shape=[head_major(1)] * 2 + [jax.ShapeDtypeStruct((HALF, 2, TOK), F32)],
        name="attention_and_lse",
        **params(20),
    )(scal, *qg, *kv)


def backward_kernel(js, carry, last, scal, qgm, qgp, om, op, lse, *refs):
    n = len(js)
    kv, refs = refs[:n], refs[n:]
    if carry:
        dq_in, refs = refs[:2], refs[2:]
    dkv, dq_out = refs[:n], refs[n:]
    qs = (qgm[0], qgp[0])
    gs = (qgm[1], qgp[1])
    os = (om[0], op[0])
    ls = [lse[0, i : i + 1, :] for i in (0, 1)]
    delta = [
        jnp.sum(gs[i].astype(F32) * os[i].astype(F32), axis=0, keepdims=True) for i in (0, 1)
    ]
    q_turned = [jnp.transpose(x) for x in qs]
    g_turned = [jnp.transpose(x) for x in gs]
    dq = [dq_in[0][0], dq_in[1][0]] if carry else [None, None]
    for idx, j in enumerate(js):
        kt = kv[idx][0]
        k = jnp.transpose(kt)
        v = jnp.transpose(kv[idx][1])
        flag = side_flag(scal, j)
        dk = dv = None
        for i in (0, 1):
            if j in UNSEEN[i]:
                continue
            sub = ls[i] if flag is None else jnp.where(flag > 0, ls[i], BIG)
            p = jnp.exp2(mm(k, qs[i], 1, 0) * BASE2 - sub)
            ds = (p * (mm(v, gs[i], 1, 0) - delta[i])).astype(BF16)
            a = mm(p.astype(BF16), g_turned[i], 1, 0)
            b = mm(ds, q_turned[i], 1, 0)
            dv = a if dv is None else dv + a
            dk = b if dk is None else dk + b
            x = mm(kt, ds, 1, 0)
            dq[i] = x if dq[i] is None else dq[i] + x
        dkv[idx][0] = (jnp.transpose(dk) * SCALE).astype(dkv[idx].dtype)
        dkv[idx][1] = jnp.transpose(dv).astype(dkv[idx].dtype)
    for i in (0, 1):
        dq_out[i][0] = (dq[i] * SCALE).astype(BF16) if last else dq[i]


def backward(js, scal, qg, o, lse, kv, dq_in, last, dtypes, us):
    n = len(js)
    carry = dq_in is not None
    return pl.pallas_call(
        functools.partial(backward_kernel, js, carry, last),
        grid_spec=pltpu.PrefetchScalarGridSpec(
            num_scalar_prefetch=1,
            grid=(HALF,),
            in_specs=[head_block(2)] * 2
            + [head_block(1)] * 2
            + [LSE_BLOCK]
            + [head_block(2)] * n
            + [head_block(1)] * (2 if carry else 0),
            out_specs=[head_block(2)] * n + [head_block(1)] * 2,
        ),
        out_shape=[head_major(2, t) for t in dtypes]
        + [head_major(1, BF16 if last else F32)] * 2,
        name="backward_" + "".join(str(j) for j in js),
        **params(us),
    )(scal, *qg, *o, lse, *[kv[j] for j in js], *(dq_in if carry else ()))


def finish_kernel(scal, dq, dq_got, mid, a, b, got, gq, gk, gv):
    odd = scal[2] > 0
    gq[...] = jnp.transpose(in_order(odd, dq[0], dq_got[0]))
    for n, ref in ((0, gk), (1, gv)):
        total = mid[n] + a[n].astype(F32) + b[n].astype(F32)
        ref[...] = jnp.transpose(in_order(odd, total.astype(BF16), got[n]))


def finish(scal, dq, dq_got, mid, a, b, got):
    out = (TOK, 2 * ROWS)
    return pl.pallas_call(
        finish_kernel,
        grid_spec=pltpu.PrefetchScalarGridSpec(
            num_scalar_prefetch=1,
            grid=(1,),
            in_specs=[whole((1, ROWS, TOK))] * 2 + [whole((2, ROWS, TOK))] * 4,
            out_specs=[whole(out)] * 3,
        ),
        out_shape=[jax.ShapeDtypeStruct(out, BF16)] * 3,
        name="sum_and_turn",
        **params(4),
    )(scal, dq, dq_got, mid, a, b, got)


def project_kernel(norm, scal, o, o_got, dy, term):
    odd = scal[2] > 0
    attn = in_order(odd, o[0], o_got[0])
    turned = jnp.transpose(dy[...])
    term[...] = (mm(turned, attn, 1, 1) * norm).astype(BF16)


def project(scal, o, o_got, dy, norm):
    wide = 256
    return pl.pallas_call(
        functools.partial(project_kernel, norm),
        grid_spec=pltpu.PrefetchScalarGridSpec(
            num_scalar_prefetch=1,
            grid=(dy.shape[1] // wide,),
            in_specs=[whole((1, ROWS, TOK))] * 2
            + [pl.BlockSpec((TOK, wide), lambda i, s: (0, i))],
            out_specs=pl.BlockSpec((wide, 2 * ROWS), lambda i, s: (i, 0)),
        ),
        out_shape=jax.ShapeDtypeStruct((dy.shape[1], 2 * ROWS), BF16),
        name="projection_term",
        **params(4),
    )(scal, o, o_got, dy)


def shards(queries, keys, values, grad_out, out_proj):
    me = lax.axis_index("ctx")
    blocks = lax.axis_size("ctx")
    odd = me % 2
    below = (me >= 2).astype(jnp.int32)
    above = (me < blocks - 2).astype(jnp.int32)
    scal = jnp.stack(
        [jnp.where(odd == 0, below, above), jnp.where(odd == 0, above, below), odd]
    ).astype(jnp.int32)
    swap_pairs = [(i, i ^ 1) for i in range(blocks)]
    step_a = [(i, i + (2 if i % 2 == 0 else -2)) for i in range(blocks)]
    step_b = [(i, i - (2 if i % 2 == 0 else -2)) for i in range(blocks)]
    step_a = [(i, t) for i, t in step_a if 0 <= t < blocks]
    step_b = [(i, t) for i, t in step_b if 0 <= t < blocks]

    def swap(x):
        return lax.ppermute(x, "ctx", swap_pairs)

    def to_a(x):
        return lax.ppermute(x, "ctx", step_a)

    def to_b(x):
        return lax.ppermute(x, "ctx", step_b)

    dy = grad_out[0]
    kv_mine, kv_send = split_heads(scal, keys[0], values[0])
    kv_got = swap(kv_send)
    a_mine, b_mine = to_a(kv_mine), to_b(kv_mine)
    qg_mine, qg_send = split_queries(scal, queries[0], dy, out_proj)
    qg_got = swap(qg_send)
    a_got, b_got = to_a(kv_got), to_b(kv_got)
    kv = (a_mine, a_got, kv_mine, kv_got, b_mine, b_got)
    qg = (qg_mine, qg_got)
    o_mine, o_send, lse = forward(scal, qg, kv)
    o_got = swap(o_send)
    o = (o_mine, o_send)

    pa_p, pb_p, dq_m, dq_p = backward(
        (1, 5), scal, qg, o, lse, kv, None, False, (BF16, BF16), 13
    )
    back_a_p, back_b_p = to_b(pa_p), to_a(pb_p)
    pa_m, pb_m, mid_p, dq_m, dq_p = backward(
        (0, 4, 3), scal, qg, o, lse, kv, (dq_m, dq_p), False, (BF16, BF16, F32), 20
    )
    back_a_m, back_b_m = to_b(pa_m), to_a(pb_m)
    sum_p = (mid_p + back_a_p.astype(F32) + back_b_p.astype(F32)).astype(BF16)
    got_kv = swap(sum_p)
    mid_m, dq_m, dq_p = backward((2,), scal, qg, o, lse, kv, (dq_m, dq_p), True, (F32,), 9)
    dq_got = swap(dq_p)

    dps = lax.axis_size("dp")
    norm = float(TOK * blocks * dps) ** (-0.5)
    term = project(scal, o_mine, o_got, dy, norm)
    term = lax.all_to_all(term.reshape(dps, -1, term.shape[1]), "dp", 0, 0)
    term = jnp.sum(term.astype(F32), axis=0)
    term = lax.all_to_all(term.reshape(blocks, -1, term.shape[1]), "ctx", 0, 0)
    proj = jnp.sum(term, axis=0)

    gq, gk, gv = finish(scal, dq_m, dq_got, mid_m, back_a_m, back_b_m, got_kv)
    return gq[None], gk[None], gv[None], proj


def solution(mesh):
    rows = P("dp", "ctx", None)
    return jax.shard_map(
        shards,
        mesh=mesh,
        in_specs=(rows, rows, rows, rows, P()),
        out_specs=(rows, rows, rows, P(("dp", "ctx"), None)),
        check_vma=False,
    )
```

time: 336 us -> 173 us (0.51)
  matrix products: 121 us -> 0 us
  Pallas kernels: 0 us -> 85.2 us
  waiting for transfers between devices: 86.3 us -> 27.5 us
  local copies, waits for them, and re-layouts: 36.7 us -> 3.94 us
  starting transfers between devices: 73.9 us -> 48.8 us
  other arithmetic: 13.8 us -> 3.27 us
    dot_general x62 -> x0, matrix products: 121 us -> none  [the longest x10 25.1 us: head_grads(): jnp.dot(dscore, k_one, preferred_element_type=jnp.float32) * scale]
    pallas_call x0 -> x8, Pallas kernels: none -> 85.2 us  [the longest x3 45 us: backward(): pl.pallas_call(functools.partial(backward_kernel, js, carry, last), grid_...]
    ppermute x16 -> x13, waiting for transfers between devices: 78.7 us -> 23.4 us  [the longest x5 13.4 us: swap(): return lax.ppermute(x, 'ctx', swap_pairs)]
    ppermute x16 -> x13, starting transfers between devices: 55.2 us -> 32.3 us  [the longest x4 17.5 us: to_b(): return lax.ppermute(x, 'ctx', step_b)]
    unnamed x30 -> x20, local copies, waits for them, and re-layouts: 19.7 us -> 3.16 us
    reduce_sum x11 -> x1, other arithmetic: 8.67 us -> 0.23 us  [shards(): term = jnp.sum(term.astype(F32), axis=0)]
    dynamic_update_slice x10 -> x0, local copies, waits for them, and re-layouts: 6.33 us -> none  [shards(): lax.map(head_grads, (q_heads, k_heads, v_heads, g_heads))]
    slice x2 -> x0, local copies, waits for them, and re-layouts: 5.21 us -> none  [the longest x1 3.45 us: shards(): total_v = part_v[REACH].astype(jnp.float32)]
  transfers between devices with their start and end apart: 18 -> 15, of which waited for: 7 -> 6; matrix products, arithmetic and copies ran while one was open for 9% -> 2% of each run, Pallas kernels for 0% -> 35%
where the time goes in v2:
time: 173 us; the launch traced here: 170 us
  Pallas kernels  85.2 us (49%)
  starting transfers between devices  48.8 us (28%)
  waiting for transfers between devices  27.5 us (16%)
  local copies, waits for them, and re-layouts  3.94 us (2%)
  other arithmetic  3.27 us (2%)
    pallas_call x3, Pallas kernels, backward(): pl.pallas_call(functools.partial(backward_kernel, js, carry, last), grid_...  45 us
    pallas_call x1, Pallas kernels, forward(): pl.pallas_call(forward_kernel, grid_spec=pltpu.PrefetchScalarGridSpec(num...  21.6 us
    ppermute x4, starting transfers between devices, to_b(): return lax.ppermute(x, 'ctx', step_b)  17.5 us
    ppermute x5, waiting for transfers between devices, swap(): return lax.ppermute(x, 'ctx', swap_pairs)  13.4 us
    all_to_all x1, starting transfers between devices, shards(): term = lax.all_to_all(term.reshape(blocks, -1, term.shape[1]), 'ctx', 0, 0)  8.98 us
    ppermute x4, waiting for transfers between devices, to_a(): return lax.ppermute(x, 'ctx', step_a)  8.23 us
    ppermute x4, starting transfers between devices, to_a(): return lax.ppermute(x, 'ctx', step_a)  7.93 us
    all_to_all x1, starting transfers between devices, shards(): term = lax.all_to_all(term.reshape(dps, -1, term.shape[1]), 'dp', 0, 0)  7.45 us
  transfers between devices with their start and end apart: 15, of which 6 were waited for; matrix products, arithmetic and copies ran while one was open for 2% of the time, Pallas kernels for 35%

profile of v2, /device:TPU:38, one launch (start us, length us, event | category | flops | bytes accessed | tf_op | source)
XLA Modules:
  0.0 169.6 jit_solution(1193695705847666631)
XLA Ops:
  0.6 0.7 pad_add_fusion.scal
  1.3 3.4 %split_kv.1 = (bf16[2,320,512]{2,1,0:T(8,128)(2,1)}, bf16[2,320,512]{2,1,0:T(8,128)(2,1)}) custom-call(s32[3]{0:T(128)} %pad_add_fusion.scal, bf16[512,640]{1,0:T(8,128)(2,1)} %bitcast.14, bf16[512,640]{1,0:T(8,128)(2,1)} %bitcast.15), custom_call_target="tpu_custom_call" | custom-call | flops 3449999872 | bytes 300000 | tf_op jit(solution)/shard_map/split_kv/pallas_call | solution.py:71
  4.7 0.8 collective-permute-start.2
  5.5 4.9 %split_q_and_grad.1 = (bf16[2,320,512]{2,1,0:T(8,128)(2,1)}, bf16[2,320,512]{2,1,0:T(8,128)(2,1)}) custom-call(s32[3]{0:T(128)} %pad_add_fusion.scal, bf16[512,640]{1,0:T(8,128)(2,1)} %bitcast.16, bf16[512,1280]{1,0:T(8,128)(2,1)} %bitcast.12, bf16[640,1280]{1,0:T(8,128)(2,1)} %w_ref.1), custom_call_target="tpu_custom_call" | custom-call | flops 5750000128 | bytes 500000 | tf_op jit(solution)/shard_map/split_q_and_grad/pallas_call | solution.py:95
  10.5 1.2 collective-permute-start
  11.7 0.0 copy-done.1
  11.7 2.0 %collective-permute-start.1 = (bf16[2,320,512]{2,1,0:T(8,128)(2,1)S(1)}, bf16[2,320,512]{2,1,0:T(8,128)(2,1)S(1)}, u32[]{:S(2)}, u32[]{:S(2)}) collective-permute-start(bf16[2,320,512]{2,1,0:T(8,128)(2,1)S(1)} %copy-done.1), channel_id=1, source_target_pairs={{0,2},{2,4},{3,1},{4,6},{5,3},{6,8},{7,5},{8,10},{9,7},{10,12},{11... | collective-permute-start | bytes 1966088 | tf_op jit(solution)/shard_map/ppermute | solution.py:299
  13.7 3.8 %collective-permute-start.4 = (bf16[2,320,512]{2,1,0:T(8,128)(2,1)S(1)}, bf16[2,320,512]{2,1,0:T(8,128)(2,1)S(1)}, u32[]{:S(2)}, u32[]{:S(2)}) collective-permute-start(bf16[2,320,512]{2,1,0:T(8,128)(2,1)S(1)} %copy-done.1), channel_id=1, source_target_pairs={{1,3},{2,0},{3,5},{4,2},{5,7},{6,4},{7,9},{8,6},{9,11},{10,8},{11,... | collective-permute-start | bytes 1966088 | tf_op jit(solution)/shard_map/ppermute | solution.py:302
  17.5 5.0 %collective-permute-done.2.refs_3_.refs_2_ = bf16[2,320,512]{2,1,0:T(8,128)(2,1)S(1)} collective-permute-done((bf16[2,320,512]{2,1,0:T(8,128)(2,1)}, bf16[2,320,512]{2,1,0:T(8,128)(2,1)S(1)}, u32[]{:S(2)}, u32[]{:S(2)}) %collective-permute-start.2) | collective-permute-done | bytes 655392 | tf_op jit(solution)/shard_map/ppermute | solution.py:296
  22.5 2.0 %collective-permute-start.3 = (bf16[2,320,512]{2,1,0:T(8,128)(2,1)S(1)}, bf16[2,320,512]{2,1,0:T(8,128)(2,1)S(1)}, u32[]{:S(2)}, u32[]{:S(2)}) collective-permute-start(bf16[2,320,512]{2,1,0:T(8,128)(2,1)S(1)} %collective-permute-done.2.refs_3_.refs_2_), channel_id=1, source_target_pairs={{0,2},{2,4},{3,1},{4,6},{5,3},{6,8},{7,5},{8,10},{9,7},{10,12},{11... | collective-permute-start | bytes 1966088 | tf_op jit(solution)/shard_map/ppermute | solution.py:299
  24.6 3.8 %collective-permute-start.5 = (bf16[2,320,512]{2,1,0:T(8,128)(2,1)S(1)}, bf16[2,320,512]{2,1,0:T(8,128)(2,1)S(1)}, u32[]{:S(2)}, u32[]{:S(2)}) collective-permute-start(bf16[2,320,512]{2,1,0:T(8,128)(2,1)S(1)} %collective-permute-done.2.refs_3_.refs_2_), channel_id=1, source_target_pairs={{1,3},{2,0},{3,5},{4,2},{5,7},{6,4},{7,9},{8,6},{9,11},{10,8},{11,... | collective-permute-start | bytes 1966088 | tf_op jit(solution)/shard_map/ppermute | solution.py:302
  28.4 7.0 %collective-permute-done.qp.qgp = bf16[2,320,512]{2,1,0:T(8,128)(2,1)S(1)} collective-permute-done((bf16[2,320,512]{2,1,0:T(8,128)(2,1)}, bf16[2,320,512]{2,1,0:T(8,128)(2,1)S(1)}, u32[]{:S(2)}, u32[]{:S(2)}) %collective-permute-start) | collective-permute-done | bytes 655392 | tf_op jit(solution)/shard_map/ppermute | solution.py:296
  35.4 0.0 collective-permute-done.1.refs_0_
  35.4 0.0 collective-permute-done.4.refs_4_.refs_1_
  35.5 8.2 %collective-permute-done.3.refs_1_.refs_0_ = bf16[2,320,512]{2,1,0:T(8,128)(2,1)S(1)} collective-permute-done((bf16[2,320,512]{2,1,0:T(8,128)(2,1)S(1)}, bf16[2,320,512]{2,1,0:T(8,128)(2,1)S(1)}, u32[]{:S(2)}, u32[]{:S(2)}) %collective-permute-start.3) | collective-permute-done | bytes 655392 | tf_op jit(solution)/shard_map/ppermute | solution.py:299
  43.7 1.7 %collective-permute-done.5.refs_5_.refs_1_ = bf16[2,320,512]{2,1,0:T(8,128)(2,1)S(1)} collective-permute-done((bf16[2,320,512]{2,1,0:T(8,128)(2,1)S(1)}, bf16[2,320,512]{2,1,0:T(8,128)(2,1)S(1)}, u32[]{:S(2)}, u32[]{:S(2)}) %collective-permute-start.5) | collective-permute-done | bytes 655392 | tf_op jit(solution)/shard_map/ppermute | solution.py:302
  45.4 0.9 copy-done.7
  46.3 21.6 %attention_and_lse.1 = (bf16[1,320,512]{2,1,0:T(8,128)(2,1)}, bf16[1,320,512]{2,1,0:T(8,128)(2,1)}, f32[5,2,512]{2,1,0:T(2,128)}) custom-call(s32[3]{0:T(128)} %pad_add_fusion.scal, bf16[2,320,512]{2,1,0:T(8,128)(2,1)} %get-tuple-element.26.qm.qgm, bf16[2,320,512]{2,1,0:T(8,128)(2,1)} %copy-done.2, bf16[2,320,512]{2,1,0:T(8,128)(2,1)} %copy-done.4, ...), custom_call_target="tpu_custom_call" | custom-call | flops 23000000512 | bytes 2000000 | tf_op jit(solution)/shard_map/attention_and_lse/pallas_call | solution.py:156
  67.9 2.7 %collective-permute-start.12 = (bf16[1,320,512]{2,1,0:T(8,128)(2,1)}, bf16[1,320,512]{2,1,0:T(8,128)(2,1)S(1)}, u32[]{:S(2)}, u32[]{:S(2)}) collective-permute-start(bf16[1,320,512]{2,1,0:T(8,128)(2,1)} %get-tuple-element.31.op), channel_id=1, source_target_pairs={{0,1},{1,0},{2,3},{3,2},{4,5},{5,4},{6,7},{7,6},{8,9},{9,8},{10,11... | collective-permute-start | bytes 983048 | tf_op jit(solution)/shard_map/ppermute | solution.py:296
  70.7 13.7 %backward_15.1 = (bf16[2,320,512]{2,1,0:T(8,128)(2,1)}, bf16[2,320,512]{2,1,0:T(8,128)(2,1)}, f32[1,320,512]{2,1,0:T(8,128)}, f32[1,320,512]{2,1,0:T(8,128)}) custom-call(s32[3]{0:T(128)} %pad_add_fusion.scal, bf16[2,320,512]{2,1,0:T(8,128)(2,1)} %get-tuple-element.26.qm.qgm, bf16[2,320,512]{2,1,0:T(8,128)(2,1)} %copy-done.2, ...), custom_call_target="tpu_custom_call" | custom-call | flops 14949999616 | bytes 1300000 | tf_op jit(solution)/shard_map/backward_15/pallas_call | solution.py:213
  84.4 2.0 %collective-permute-start.10 = (bf16[2,320,512]{2,1,0:T(8,128)(2,1)}, bf16[2,320,512]{2,1,0:T(8,128)(2,1)S(1)}, u32[]{:S(2)}, u32[]{:S(2)}) collective-permute-start(bf16[2,320,512]{2,1,0:T(8,128)(2,1)} %get-tuple-element.44), channel_id=1, source_target_pairs={{0,2},{2,4},{3,1},{4,6},{5,3},{6,8},{7,5},{8,10},{9,7},{10,12},{11... | collective-permute-start | bytes 1966088 | tf_op jit(solution)/shard_map/ppermute | solution.py:299
  86.4 4.9 %collective-permute-start.9 = (bf16[2,320,512]{2,1,0:T(8,128)(2,1)}, bf16[2,320,512]{2,1,0:T(8,128)(2,1)S(1)}, u32[]{:S(2)}, u32[]{:S(2)}) collective-permute-start(bf16[2,320,512]{2,1,0:T(8,128)(2,1)} %get-tuple-element.43), channel_id=1, source_target_pairs={{1,3},{2,0},{3,5},{4,2},{5,7},{6,4},{7,9},{8,6},{9,11},{10,8},{11,... | collective-permute-start | bytes 1966088 | tf_op jit(solution)/shard_map/ppermute | solution.py:302
  91.3 0.0 collective-permute-done.12.o_got
  91.3 0.7 copy-done.9
  92.1 6.0 %projection_term.1 = bf16[1280,640]{1,0:T(8,128)(2,1)} custom-call(s32[3]{0:T(128)} %pad_add_fusion.scal, bf16[1,320,512]{2,1,0:T(8,128)(2,1)} %get-tuple-element.30.om.o, bf16[1,320,512]{2,1,0:T(8,128)(2,1)} %copy-done.9, bf16[512,1280]{1,0:T(8,128)(2,1)} %bitcast.13), custom_call_target="tpu_custom_call" | custom-call | flops 4600000000 | bytes 400000 | tf_op jit(solution)/shard_map/projection_term/pallas_call | solution.py:265
  98.1 7.5 %all-to-all-start = ((bf16[16,80,640]{2,1,0:T(8,128)(2,1)}), bf16[16,80,640]{2,1,0:T(8,128)(2,1)S(1)}, u32[]{:S(2)}, u32[]{:S(2)}) async-start(bf16[16,80,640]{2,1,0:T(8,128)(2,1)} %bitcast.11), calls=%async_computation | async-start | bytes 3276800 | tf_op jit(solution)/shard_map/all_to_all | solution.py:333
  105.5 20.8 %backward_043.1 = (bf16[2,320,512]{2,1,0:T(8,128)(2,1)}, bf16[2,320,512]{2,1,0:T(8,128)(2,1)}, f32[2,320,512]{2,1,0:T(8,128)}, f32[1,320,512]{2,1,0:T(8,128)}, f32[1,320,512]{2,1,0:T(8,128)}) custom-call(s32[3]{0:T(128)} %pad_add_fusion.scal, bf16[2,320,512]{2,1,0:T(8,128)(2,1)} %get-tuple-element.26.qm.qgm, bf16[2,320,512]{2,1,0:T(8,128)(2,1)} %copy-done.2, ...), custom_call_target="tpu_custom_call" | custom-call | flops 23000000512 | bytes 2000000 | tf_op jit(solution)/shard_map/backward_043/pallas_call | solution.py:213
  126.3 4.9 %collective-permute-start.7 = (bf16[2,320,512]{2,1,0:T(8,128)(2,1)}, bf16[2,320,512]{2,1,0:T(8,128)(2,1)}, u32[]{:S(2)}, u32[]{:S(2)}) collective-permute-start(bf16[2,320,512]{2,1,0:T(8,128)(2,1)} %get-tuple-element.40), channel_id=1, source_target_pairs={{1,3},{2,0},{3,5},{4,2},{5,7},{6,4},{7,9},{8,6},{9,11},{10,8},{11,... | collective-permute-start | bytes 1966088 | tf_op jit(solution)/shard_map/ppermute | solution.py:302
  131.2 1.9 %collective-permute-start.8 = (bf16[2,320,512]{2,1,0:T(8,128)(2,1)}, bf16[2,320,512]{2,1,0:T(8,128)(2,1)}, u32[]{:S(2)}, u32[]{:S(2)}) collective-permute-start(bf16[2,320,512]{2,1,0:T(8,128)(2,1)} %get-tuple-element.41), channel_id=1, source_target_pairs={{0,2},{2,4},{3,1},{4,6},{5,3},{6,8},{7,5},{8,10},{9,7},{10,12},{11... | collective-permute-start | bytes 1966088 | tf_op jit(solution)/shard_map/ppermute | solution.py:299
  133.2 0.0 collective-permute-done.10
  133.2 0.0 collective-permute-done.9
  133.2 0.8 copy-done
  134.0 1.8 %add_convert_fusion = bf16[2,320,512]{2,1,0:T(8,128)(2,1)S(1)} fusion(bf16[2,320,512]{2,1,0:T(8,128)(2,1)S(1)} %collective-permute-done.10, f32[2,320,512]{2,1,0:T(8,128)} %get-tuple-element.42, bf16[2,320,512]{2,1,0:T(8,128)(2,1)} %copy-done), kind=kLoop, calls=%fused_computation.1 | loop fusion | flops 1638400 | bytes 3276800 | tf_op jit(solution)/shard_map/convert_element_type | solution.py:325
  135.8 0.1 collective-permute-start.11
  135.9 10.6 %backward_2.1 = (f32[2,320,512]{2,1,0:T(8,128)}, bf16[1,320,512]{2,1,0:T(8,128)(2,1)}, bf16[1,320,512]{2,1,0:T(8,128)(2,1)}) custom-call(s32[3]{0:T(128)} %pad_add_fusion.scal, bf16[2,320,512]{2,1,0:T(8,128)(2,1)} %get-tuple-element.26.qm.qgm, bf16[2,320,512]{2,1,0:T(8,128)(2,1)} %copy-done.2, bf16[1,320,512]{2,1,0:T(8,128)(2,1)} %get-tuple-element.30.om.o, ...), custom_call_target="tpu_custom_call" | custom-call | flops 10350000128 | bytes 900000 | tf_op jit(solution)/shard_map/backward_2/pallas_call | solution.py:213
  146.4 2.1 %collective-permute-start.6 = (bf16[1,320,512]{2,1,0:T(8,128)(2,1)}, bf16[1,320,512]{2,1,0:T(8,128)(2,1)S(1)}, u32[]{:S(2)}, u32[]{:S(2)}) collective-permute-start(bf16[1,320,512]{2,1,0:T(8,128)(2,1)} %get-tuple-element.38), channel_id=1, source_target_pairs={{0,1},{1,0},{2,3},{3,2},{4,5},{5,4},{6,7},{7,6},{8,9},{9,8},{10,11... | collective-permute-start | bytes 983048 | tf_op jit(solution)/shard_map/ppermute | solution.py:296
  148.5 0.0 all-to-all-done
  148.5 0.2 convert_reduce_fusion
  148.7 0.8 reshape.15
  149.5 9.0 %all-to-all-start.1 = ((f32[16,5,640]{2,1,0:T(8,128)}), f32[16,5,640]{2,1,0:T(8,128)S(1)}, u32[]{:S(2)}, u32[]{:S(2)}) async-start(f32[16,5,640]{2,1,0:T(8,128)} %reshape.15), calls=%async_computation.1 | async-start | bytes 655360 | tf_op jit(solution)/shard_map/all_to_all | solution.py:335
  158.5 1.3 collective-permute-done.6.dq_got
  159.8 0.0 collective-permute-done.7.a
  159.8 0.0 collective-permute-done.8.b
  159.8 0.0 collective-permute-done.11.got
  159.8 0.7 copy-done.8
  160.5 4.3 %sum_and_turn.1 = (bf16[512,640]{1,0:T(8,128)(2,1)}, bf16[512,640]{1,0:T(8,128)(2,1)}, bf16[512,640]{1,0:T(8,128)(2,1)}) custom-call(s32[3]{0:T(128)} %pad_add_fusion.scal, bf16[1,320,512]{2,1,0:T(8,128)(2,1)} %get-tuple-element.37.dq, bf16[1,320,512]{2,1,0:T(8,128)(2,1)} %copy-done.8, f32[2,320,512]{2,1,0:T(8,128)} %get-tuple-element.39.mid, ...), custom_call_target="tpu_custom_call" | custom-call | flops 4600000000 | bytes 400000 | tf_op jit(solution)/shard_map/sum_and_turn/pallas_call | solution.py:242
  164.8 4.2 %all-to-all-done.1 = f32[16,5,640]{2,1,0:T(8,128)S(1)} async-done(((f32[16,5,640]{2,1,0:T(8,128)}), f32[16,5,640]{2,1,0:T(8,128)S(1)}, u32[]{:S(2)}, u32[]{:S(2)}) %all-to-all-start.1) | async-done | bytes 204832 | tf_op jit(solution)/shard_map/all_to_all | solution.py:335
  168.9 0.6 reduce_sum.19
  (15 shorter events, 0.0 us)
Async XLA Ops:
  4.7 17.8 %collective-permute-start.2 = (bf16[2,320,512]{2,1,0:T(8,128)(2,1)}, bf16[2,320,512]{2,1,0:T(8,128)(2,1)S(1)}, u32[]{:S(2)}, u32[]{:S(2)}) collective-permute-start(bf16[2,320,512]{2,1,0:T(8,128)(2,1)} %get-tuple-element.29), channel_id=1, source_target_pairs={{0,1},{1,0},{2,3},{3,2},{4,5},{5,4},{6,7},{7,6},{8,9},{9,8},{10,11... | collective-permute-start | bytes 1966088 | tf_op jit(solution)/shard_map/ppermute | solution.py:296
  5.5 6.1 %copy-start.1 = (bf16[2,320,512]{2,1,0:T(8,128)(2,1)S(1)}, bf16[2,320,512]{2,1,0:T(8,128)(2,1)}, u32[]{:S(2)}) copy-start(bf16[2,320,512]{2,1,0:T(8,128)(2,1)} %get-tuple-element.28.refs_2_.refs_0_) | copy-start | bytes 1966084
  10.5 25.0 %collective-permute-start = (bf16[2,320,512]{2,1,0:T(8,128)(2,1)}, bf16[2,320,512]{2,1,0:T(8,128)(2,1)S(1)}, u32[]{:S(2)}, u32[]{:S(2)}) collective-permute-start(bf16[2,320,512]{2,1,0:T(8,128)(2,1)} %get-tuple-element.27), channel_id=1, source_target_pairs={{0,1},{1,0},{2,3},{3,2},{4,5},{5,4},{6,7},{7,6},{8,9},{9,8},{10,11... | collective-permute-start | bytes 1966088 | tf_op jit(solution)/shard_map/ppermute | solution.py:296
  11.7 23.8 %collective-permute-start.1 = (bf16[2,320,512]{2,1,0:T(8,128)(2,1)S(1)}, bf16[2,320,512]{2,1,0:T(8,128)(2,1)S(1)}, u32[]{:S(2)}, u32[]{:S(2)}) collective-permute-start(bf16[2,320,512]{2,1,0:T(8,128)(2,1)S(1)} %copy-done.1), channel_id=1, source_target_pairs={{0,2},{2,4},{3,1},{4,6},{5,3},{6,8},{7,5},{8,10},{9,7},{10,12},{11... | collective-permute-start | bytes 1966088 | tf_op jit(solution)/shard_map/ppermute | solution.py:299
  13.7 21.8 %collective-permute-start.4 = (bf16[2,320,512]{2,1,0:T(8,128)(2,1)S(1)}, bf16[2,320,512]{2,1,0:T(8,128)(2,1)S(1)}, u32[]{:S(2)}, u32[]{:S(2)}) collective-permute-start(bf16[2,320,512]{2,1,0:T(8,128)(2,1)S(1)} %copy-done.1), channel_id=1, source_target_pairs={{1,3},{2,0},{3,5},{4,2},{5,7},{6,4},{7,9},{8,6},{9,11},{10,8},{11,... | collective-permute-start | bytes 1966088 | tf_op jit(solution)/shard_map/ppermute | solution.py:302
  22.5 23.7 %copy-start.3 = (bf16[2,320,512]{2,1,0:T(8,128)(2,1)}, bf16[2,320,512]{2,1,0:T(8,128)(2,1)S(1)}, u32[]{:S(2)}) copy-start(bf16[2,320,512]{2,1,0:T(8,128)(2,1)S(1)} %collective-permute-done.2.refs_3_.refs_2_) | copy-start | bytes 1966084
  22.5 21.1 %collective-permute-start.3 = (bf16[2,320,512]{2,1,0:T(8,128)(2,1)S(1)}, bf16[2,320,512]{2,1,0:T(8,128)(2,1)S(1)}, u32[]{:S(2)}, u32[]{:S(2)}) collective-permute-start(bf16[2,320,512]{2,1,0:T(8,128)(2,1)S(1)} %collective-permute-done.2.refs_3_.refs_2_), channel_id=1, source_target_pairs={{0,2},{2,4},{3,1},{4,6},{5,3},{6,8},{7,5},{8,10},{9,7},{10,12},{11... | collective-permute-start | bytes 1966088 | tf_op jit(solution)/shard_map/ppermute | solution.py:299
  24.6 20.9 %collective-permute-start.5 = (bf16[2,320,512]{2,1,0:T(8,128)(2,1)S(1)}, bf16[2,320,512]{2,1,0:T(8,128)(2,1)S(1)}, u32[]{:S(2)}, u32[]{:S(2)}) collective-permute-start(bf16[2,320,512]{2,1,0:T(8,128)(2,1)S(1)} %collective-permute-done.2.refs_3_.refs_2_), channel_id=1, source_target_pairs={{1,3},{2,0},{3,5},{4,2},{5,7},{6,4},{7,9},{8,6},{9,11},{10,8},{11,... | collective-permute-start | bytes 1966088 | tf_op jit(solution)/shard_map/ppermute | solution.py:302
  35.4 10.9 %copy-start.2 = (bf16[2,320,512]{2,1,0:T(8,128)(2,1)}, bf16[2,320,512]{2,1,0:T(8,128)(2,1)S(1)}, u32[]{:S(2)}) copy-start(bf16[2,320,512]{2,1,0:T(8,128)(2,1)S(1)} %collective-permute-done.qp.qgp) | copy-start | bytes 1966084
  35.4 10.9 %copy-start.4 = (bf16[2,320,512]{2,1,0:T(8,128)(2,1)}, bf16[2,320,512]{2,1,0:T(8,128)(2,1)S(1)}, u32[]{:S(2)}) copy-start(bf16[2,320,512]{2,1,0:T(8,128)(2,1)S(1)} %collective-permute-done.1.refs_0_) | copy-start | bytes 1966084
  35.5 10.8 %copy-start.5 = (bf16[2,320,512]{2,1,0:T(8,128)(2,1)}, bf16[2,320,512]{2,1,0:T(8,128)(2,1)S(1)}, u32[]{:S(2)}) copy-start(bf16[2,320,512]{2,1,0:T(8,128)(2,1)S(1)} %collective-permute-done.4.refs_4_.refs_1_) | copy-start | bytes 1966084
  43.7 2.6 %copy-start.6 = (bf16[2,320,512]{2,1,0:T(8,128)(2,1)}, bf16[2,320,512]{2,1,0:T(8,128)(2,1)S(1)}, u32[]{:S(2)}) copy-start(bf16[2,320,512]{2,1,0:T(8,128)(2,1)S(1)} %collective-permute-done.3.refs_1_.refs_0_) | copy-start | bytes 1966084
  45.4 0.9 copy-start.7
  67.9 23.4 %collective-permute-start.12 = (bf16[1,320,512]{2,1,0:T(8,128)(2,1)}, bf16[1,320,512]{2,1,0:T(8,128)(2,1)S(1)}, u32[]{:S(2)}, u32[]{:S(2)}) collective-permute-start(bf16[1,320,512]{2,1,0:T(8,128)(2,1)} %get-tuple-element.31.op), channel_id=1, source_target_pairs={{0,1},{1,0},{2,3},{3,2},{4,5},{5,4},{6,7},{7,6},{8,9},{9,8},{10,11... | collective-permute-start | bytes 983048 | tf_op jit(solution)/shard_map/ppermute | solution.py:296
  84.4 48.8 %collective-permute-start.10 = (bf16[2,320,512]{2,1,0:T(8,128)(2,1)}, bf16[2,320,512]{2,1,0:T(8,128)(2,1)S(1)}, u32[]{:S(2)}, u32[]{:S(2)}) collective-permute-start(bf16[2,320,512]{2,1,0:T(8,128)(2,1)} %get-tuple-element.44), channel_id=1, source_target_pairs={{0,2},{2,4},{3,1},{4,6},{5,3},{6,8},{7,5},{8,10},{9,7},{10,12},{11... | collective-permute-start | bytes 1966088 | tf_op jit(solution)/shard_map/ppermute | solution.py:299
  86.4 46.8 %collective-permute-start.9 = (bf16[2,320,512]{2,1,0:T(8,128)(2,1)}, bf16[2,320,512]{2,1,0:T(8,128)(2,1)S(1)}, u32[]{:S(2)}, u32[]{:S(2)}) collective-permute-start(bf16[2,320,512]{2,1,0:T(8,128)(2,1)} %get-tuple-element.43), channel_id=1, source_target_pairs={{1,3},{2,0},{3,5},{4,2},{5,7},{6,4},{7,9},{8,6},{9,11},{10,8},{11,... | collective-permute-start | bytes 1966088 | tf_op jit(solution)/shard_map/ppermute | solution.py:302
  91.3 0.8 copy-start.9
  98.1 50.4 %all-to-all-start = ((bf16[16,80,640]{2,1,0:T(8,128)(2,1)}), bf16[16,80,640]{2,1,0:T(8,128)(2,1)S(1)}, u32[]{:S(2)}, u32[]{:S(2)}) async-start(bf16[16,80,640]{2,1,0:T(8,128)(2,1)} %bitcast.11), calls=%async_computation | async-start | bytes 3276800 | tf_op jit(solution)/shard_map/all_to_all | solution.py:333
  126.3 33.5 %collective-permute-start.7 = (bf16[2,320,512]{2,1,0:T(8,128)(2,1)}, bf16[2,320,512]{2,1,0:T(8,128)(2,1)}, u32[]{:S(2)}, u32[]{:S(2)}) collective-permute-start(bf16[2,320,512]{2,1,0:T(8,128)(2,1)} %get-tuple-element.40), channel_id=1, source_target_pairs={{1,3},{2,0},{3,5},{4,2},{5,7},{6,4},{7,9},{8,6},{9,11},{10,8},{11,... | collective-permute-start | bytes 1966088 | tf_op jit(solution)/shard_map/ppermute | solution.py:302
  131.2 28.6 %collective-permute-start.8 = (bf16[2,320,512]{2,1,0:T(8,128)(2,1)}, bf16[2,320,512]{2,1,0:T(8,128)(2,1)}, u32[]{:S(2)}, u32[]{:S(2)}) collective-permute-start(bf16[2,320,512]{2,1,0:T(8,128)(2,1)} %get-tuple-element.41), channel_id=1, source_target_pairs={{0,2},{2,4},{3,1},{4,6},{5,3},{6,8},{7,5},{8,10},{9,7},{10,12},{11... | collective-permute-start | bytes 1966088 | tf_op jit(solution)/shard_map/ppermute | solution.py:299
  133.2 0.8 copy-start
  135.8 24.1 %collective-permute-start.11 = (bf16[2,320,512]{2,1,0:T(8,128)(2,1)S(1)}, bf16[2,320,512]{2,1,0:T(8,128)(2,1)}, u32[]{:S(2)}, u32[]{:S(2)}) collective-permute-start(bf16[2,320,512]{2,1,0:T(8,128)(2,1)S(1)} %add_convert_fusion), channel_id=1, source_target_pairs={{0,1},{1,0},{2,3},{3,2},{4,5},{5,4},{6,7},{7,6},{8,9},{9,8},{10,11... | collective-permute-start | bytes 1966088 | tf_op jit(solution)/shard_map/ppermute | solution.py:296
  146.4 13.4 %collective-permute-start.6 = (bf16[1,320,512]{2,1,0:T(8,128)(2,1)}, bf16[1,320,512]{2,1,0:T(8,128)(2,1)S(1)}, u32[]{:S(2)}, u32[]{:S(2)}) collective-permute-start(bf16[1,320,512]{2,1,0:T(8,128)(2,1)} %get-tuple-element.38), channel_id=1, source_target_pairs={{0,1},{1,0},{2,3},{3,2},{4,5},{5,4},{6,7},{7,6},{8,9},{9,8},{10,11... | collective-permute-start | bytes 983048 | tf_op jit(solution)/shard_map/ppermute | solution.py:296
  149.5 19.4 %all-to-all-start.1 = ((f32[16,5,640]{2,1,0:T(8,128)}), f32[16,5,640]{2,1,0:T(8,128)S(1)}, u32[]{:S(2)}, u32[]{:S(2)}) async-start(f32[16,5,640]{2,1,0:T(8,128)} %reshape.15), calls=%async_computation.1 | async-start | bytes 655360 | tf_op jit(solution)/shard_map/all_to_all | solution.py:335
  159.8 0.7 copy-start.8

commit v3 on v2

v3 whole, which is shorter than its diff:
```python
import functools
import math

import jax
import jax.numpy as jnp
from jax import lax
from jax.experimental import pallas as pl
from jax.experimental.pallas import tpu as pltpu
from jax.sharding import PartitionSpec as P

HEADS = 10
HDIM = 64
HALF = HEADS // 2
ROWS = HALF * HDIM
TOK = 512
SCALE = HDIM ** (-0.5)
BASE2 = SCALE * math.log2(math.e)
BIG = 1e30
F32 = jnp.float32
BF16 = jnp.bfloat16

UNSEEN = ((5,), (0,))


def params(us):
    return dict(
        compiler_params=pltpu.CompilerParams(vmem_limit_bytes=63 * 2**20),
        cost_estimate=pl.CostEstimate(
            flops=int(us * 1.15e9), bytes_accessed=int(us * 1e5), transcendentals=0
        ),
    )


def mm(a, b, ca, cb):
    return lax.dot_general(a, b, (((ca,), (cb,)), ((), ())), preferred_element_type=F32)


def head_block(parts):
    return pl.BlockSpec((parts, HDIM, TOK), lambda h, s: (0, h, 0))


def head_major(parts, dtype=BF16):
    return jax.ShapeDtypeStruct((parts, ROWS, TOK), dtype)


def whole(shape):
    return pl.BlockSpec(shape, lambda i, s: (0,) * len(shape))


def halves(x):
    return x[:ROWS], x[ROWS:]


def in_order(odd, mine, partners):
    first = jnp.where(odd, partners, mine)
    return jnp.concatenate([first, jnp.where(odd, mine, partners)], axis=0)


def split_kernel(scal, k_ref, v_ref, q_ref, kv_mine, kv_send, q_mine, q_send):
    odd = scal[2] > 0
    for n, ref in enumerate((k_ref, v_ref)):
        low, high = halves(jnp.transpose(ref[...]))
        kv_mine[n] = jnp.where(odd, high, low)
        kv_send[n] = jnp.where(odd, low, high)
    low, high = halves(jnp.transpose(q_ref[...]))
    q_mine[0] = jnp.where(odd, high, low)
    q_send[0] = jnp.where(odd, low, high)


def split_heads(scal, k, v, q):
    return pl.pallas_call(
        split_kernel,
        grid_spec=pltpu.PrefetchScalarGridSpec(
            num_scalar_prefetch=1,
            grid=(1,),
            in_specs=[whole(k.shape)] * 3,
            out_specs=[whole((2, ROWS, TOK))] * 2 + [whole((1, ROWS, TOK))] * 2,
        ),
        out_shape=[head_major(2)] * 2 + [head_major(1)] * 2,
        name="split_kvq",
        **params(4),
    )(scal, k, v, q)


def grad_kernel(scal, dy_ref, w_ref, mine, send):
    odd = scal[2] > 0
    low, high = halves(mm(w_ref[...], dy_ref[...], 1, 1).astype(BF16))
    mine[0] = jnp.where(odd, high, low)
    send[0] = jnp.where(odd, low, high)


def attention_grad(scal, dy, w):
    return pl.pallas_call(
        grad_kernel,
        grid_spec=pltpu.PrefetchScalarGridSpec(
            num_scalar_prefetch=1,
            grid=(1,),
            in_specs=[whole(dy.shape), whole(w.shape)],
            out_specs=[whole((1, ROWS, TOK))] * 2,
        ),
        out_shape=[head_major(1)] * 2,
        name="attention_grad",
        **params(4),
    )(scal, dy, w)


def side_flag(scal, j):
    return None if j in (2, 3) else scal[0] if j < 2 else scal[1]


def forward_kernel(js, carry, last, scal, qm, qp, *refs):
    kv, refs = refs[: len(js)], refs[len(js) :]
    qs = (qm[0], qp[0])
    units = [(n, i) for n, j in enumerate(js) for i in (0, 1) if j not in UNSEEN[i]]
    turned = {}

    def scores(n, i):
        if n not in turned:
            turned[n] = jnp.transpose(kv[n][0])
        return mm(turned[n], qs[i], 1, 0)

    top = [None, None]
    total = [None, None]
    out = [None, None]
    if carry:
        stats, o_in, refs = refs[0], refs[1:3], refs[3:]
        for i in (0, 1):
            top[i] = stats[0, i : i + 1, :]
            total[i] = stats[0, 2 + i : 3 + i, :]
            out[i] = o_in[i][0]
    om, op, stats_out = refs
    ahead = scores(*units[0])
    for n, (b, i) in enumerate(units):
        s = ahead
        if n + 1 < len(units):
            ahead = scores(*units[n + 1])
        flag = side_flag(scal, js[b])
        here = jnp.max(s, axis=0, keepdims=True) * BASE2
        if flag is not None:
            here = jnp.where(flag > 0, here, -BIG)
        first = top[i] is None
        new = here if first else jnp.maximum(top[i], here)
        sub = new if flag is None else jnp.where(flag > 0, new, BIG)
        e = jnp.exp2(s * BASE2 - sub)
        part = jnp.sum(e, axis=0, keepdims=True)
        pv = mm(kv[b][1], e.astype(BF16), 1, 0)
        if first:
            total[i], out[i] = part, pv
        else:
            fade = jnp.exp2(top[i] - new)
            total[i] = total[i] * fade + part
            out[i] = out[i] * fade + pv
        top[i] = new
    for i, ref in ((0, om), (1, op)):
        if last:
            ref[0] = (out[i] * (1.0 / total[i])).astype(BF16)
            stats_out[0, i : i + 1, :] = top[i] + jnp.log2(total[i])
        else:
            ref[0] = out[i]
            stats_out[0, i : i + 1, :] = top[i]
            stats_out[0, 2 + i : 3 + i, :] = total[i]


def stat_block(rows):
    return pl.BlockSpec((1, rows, TOK), lambda h, s: (h, 0, 0))


def forward(js, scal, q, kv, carry, last, us):
    given = () if carry is None else carry
    rows = 2 if last else 4
    return pl.pallas_call(
        functools.partial(forward_kernel, js, bool(given), last),
        grid_spec=pltpu.PrefetchScalarGridSpec(
            num_scalar_prefetch=1,
            grid=(HALF,),
            in_specs=[head_block(1)] * 2
            + [head_block(2)] * len(js)
            + ([stat_block(4)] + [head_block(1)] * 2 if given else []),
            out_specs=[head_block(1)] * 2 + [stat_block(rows)],
        ),
        out_shape=[head_major(1, BF16 if last else F32)] * 2
        + [jax.ShapeDtypeStruct((HALF, rows, TOK), F32)],
        name="forward_" + "".join(str(j) for j in js),
        **params(us),
    )(scal, *q, *[kv[j] for j in js], *given)


def backward_kernel(js, carry, last, scal, qm, qp, gm, gp, om, op, lse, *refs):
    n = len(js)
    kv, refs = refs[:n], refs[n:]
    if carry:
        dq_in, refs = refs[:2], refs[2:]
    dkv, dq_out = refs[:n], refs[n:]
    qs = (qm[0], qp[0])
    gs = (gm[0], gp[0])
    os = (om[0], op[0])
    ls = [lse[0, i : i + 1, :] for i in (0, 1)]
    delta = [
        jnp.sum(gs[i].astype(F32) * os[i].astype(F32), axis=0, keepdims=True) for i in (0, 1)
    ]
    q_turned = [jnp.transpose(x) for x in qs]
    dq = [dq_in[0][0], dq_in[1][0]] if carry else [None, None]
    units = [(idx, i) for idx, j in enumerate(js) for i in (0, 1) if j not in UNSEEN[i]]
    turned = {}

    def products(idx, i):
        if idx not in turned:
            turned[idx] = (jnp.transpose(kv[idx][0]), jnp.transpose(kv[idx][1]))
        k, v = turned[idx]
        return mm(k, qs[i], 1, 0), mm(v, gs[i], 1, 0)

    ahead = products(*units[0])
    dk = dv = None
    for n, (idx, i) in enumerate(units):
        s, dp = ahead
        if n + 1 < len(units):
            ahead = products(*units[n + 1])
        flag = side_flag(scal, js[idx])
        sub = ls[i] if flag is None else jnp.where(flag > 0, ls[i], BIG)
        p = jnp.exp2(s * BASE2 - sub)
        ds = (p * (dp - delta[i])).astype(BF16)
        a = mm(gs[i], p.astype(BF16), 1, 1)
        b = mm(ds, q_turned[i], 1, 0)
        dv = a if dv is None else dv + a
        dk = b if dk is None else dk + b
        x = mm(kv[idx][0], ds, 1, 0)
        dq[i] = x if dq[i] is None else dq[i] + x
        if n + 1 == len(units) or units[n + 1][0] != idx:
            dkv[idx][0] = (jnp.transpose(dk) * SCALE).astype(dkv[idx].dtype)
            dkv[idx][1] = dv.astype(dkv[idx].dtype)
            dk = dv = None
    for i in (0, 1):
        dq_out[i][0] = (dq[i] * SCALE).astype(BF16) if last else dq[i]


def backward(js, scal, q, g, o, lse, kv, dq_in, last, dtypes, us):
    n = len(js)
    carry = dq_in is not None
    return pl.pallas_call(
        functools.partial(backward_kernel, js, carry, last),
        grid_spec=pltpu.PrefetchScalarGridSpec(
            num_scalar_prefetch=1,
            grid=(HALF,),
            in_specs=[head_block(1)] * 6
            + [stat_block(2)]
            + [head_block(2)] * n
            + [head_block(1)] * (2 if carry else 0),
            out_specs=[head_block(2)] * n + [head_block(1)] * 2,
        ),
        out_shape=[head_major(2, t) for t in dtypes]
        + [head_major(1, BF16 if last else F32)] * 2,
        name="backward_" + "".join(str(j) for j in js),
        **params(us),
    )(scal, *q, *g, *o, lse, *[kv[j] for j in js], *(dq_in if carry else ()))


def finish_kernel(scal, dq, dq_got, mid, a, b, got, gq, gk, gv):
    odd = scal[2] > 0
    gq[...] = jnp.transpose(in_order(odd, dq[0], dq_got[0]))
    for n, ref in ((0, gk), (1, gv)):
        total = mid[n] + a[n].astype(F32) + b[n].astype(F32)
        ref[...] = jnp.transpose(in_order(odd, total.astype(BF16), got[n]))


def finish(scal, dq, dq_got, mid, a, b, got):
    out = (TOK, 2 * ROWS)
    return pl.pallas_call(
        finish_kernel,
        grid_spec=pltpu.PrefetchScalarGridSpec(
            num_scalar_prefetch=1,
            grid=(1,),
            in_specs=[whole((1, ROWS, TOK))] * 2 + [whole((2, ROWS, TOK))] * 4,
            out_specs=[whole(out)] * 3,
        ),
        out_shape=[jax.ShapeDtypeStruct(out, BF16)] * 3,
        name="sum_and_turn",
        **params(4),
    )(scal, dq, dq_got, mid, a, b, got)


def project_kernel(norm, scal, o, o_got, dy, term):
    odd = scal[2] > 0
    attn = in_order(odd, o[0], o_got[0])
    turned = jnp.transpose(dy[...])
    term[...] = (mm(turned, attn, 1, 1) * norm).astype(BF16)


def project(scal, o, o_got, dy, norm):
    wide = 256
    return pl.pallas_call(
        functools.partial(project_kernel, norm),
        grid_spec=pltpu.PrefetchScalarGridSpec(
            num_scalar_prefetch=1,
            grid=(dy.shape[1] // wide,),
            in_specs=[whole((1, ROWS, TOK))] * 2
            + [pl.BlockSpec((TOK, wide), lambda i, s: (0, i))],
            out_specs=pl.BlockSpec((wide, 2 * ROWS), lambda i, s: (i, 0)),
        ),
        out_shape=jax.ShapeDtypeStruct((dy.shape[1], 2 * ROWS), BF16),
        name="projection_term",
        **params(4),
    )(scal, o, o_got, dy)


def shards(queries, keys, values, grad_out, out_proj):
    me = lax.axis_index("ctx")
    blocks = lax.axis_size("ctx")
    odd = me % 2
    below = (me >= 2).astype(jnp.int32)
    above = (me < blocks - 2).astype(jnp.int32)
    scal = jnp.stack(
        [jnp.where(odd == 0, below, above), jnp.where(odd == 0, above, below), odd]
    ).astype(jnp.int32)
    swap_pairs = [(i, i ^ 1) for i in range(blocks)]
    step_a = [(i, i + (2 if i % 2 == 0 else -2)) for i in range(blocks)]
    step_b = [(i, i - (2 if i % 2 == 0 else -2)) for i in range(blocks)]
    step_a = [(i, t) for i, t in step_a if 0 <= t < blocks]
    step_b = [(i, t) for i, t in step_b if 0 <= t < blocks]

    def swap(x):
        return lax.ppermute(x, "ctx", swap_pairs)

    def to_a(x):
        return lax.ppermute(x, "ctx", step_a)

    def to_b(x):
        return lax.ppermute(x, "ctx", step_b)

    dy = grad_out[0]
    kv_mine, kv_send, q_mine, q_send = split_heads(scal, keys[0], values[0], queries[0])
    kv_got = swap(kv_send)
    a_mine, b_mine = to_a(kv_mine), to_b(kv_mine)
    q_got = swap(q_send)
    g_mine, g_send = attention_grad(scal, dy, out_proj)
    g_got = swap(g_send)
    a_got, b_got = to_a(kv_got), to_b(kv_got)
    kv = (a_mine, a_got, kv_mine, kv_got, b_mine, b_got)
    q = (q_mine, q_got)
    g = (g_mine, g_got)
    early_m, early_p, stats = forward((2, 3, 4, 0), scal, q, kv, None, False, 16)
    o_mine, o_send, lse = forward((1, 5), scal, q, kv, (stats, early_m, early_p), True, 8)
    o_got = swap(o_send)
    o = (o_mine, o_send)

    pa_p, pb_p, dq_m, dq_p = backward(
        (1, 5), scal, q, g, o, lse, kv, None, False, (BF16, BF16), 13
    )
    back_a_p, back_b_p = to_b(pa_p), to_a(pb_p)
    pa_m, pb_m, mid_p, dq_m, dq_p = backward(
        (0, 4, 3), scal, q, g, o, lse, kv, (dq_m, dq_p), False, (BF16, BF16, F32), 20
    )
    back_a_m, back_b_m = to_b(pa_m), to_a(pb_m)
    sum_p = (mid_p + back_a_p.astype(F32) + back_b_p.astype(F32)).astype(BF16)
    got_kv = swap(sum_p)

    dps = lax.axis_size("dp")
    norm = float(TOK * blocks * dps) ** (-0.5)
    term = project(scal, o_mine, o_got, dy, norm)
    term = lax.all_to_all(term.reshape(dps, -1, term.shape[1]), "dp", 0, 0)
    term = jnp.sum(term.astype(F32), axis=0)
    term = term.reshape(blocks, -1, term.shape[1])
    term, dq_m = lax.optimization_barrier((term, dq_m))
    term = lax.all_to_all(term, "ctx", 0, 0)
    proj = jnp.sum(term, axis=0)

    mid_m, dq_m, dq_p = backward(
        (2,), scal, q, g, o, lse, kv, (dq_m, dq_p), True, (F32,), 9
    )
    dq_got = swap(dq_p)
    gq, gk, gv = finish(scal, dq_m, dq_got, mid_m, back_a_m, back_b_m, got_kv)
    return gq[None], gk[None], gv[None], proj


def solution(mesh):
    rows = P("dp", "ctx", None)
    return jax.shard_map(
        shards,
        mesh=mesh,
        in_specs=(rows, rows, rows, rows, P()),
        out_specs=(rows, rows, rows, P(("dp", "ctx"), None)),
        check_vma=False,
    )
```

time: 173 us -> 161 us (0.931)
  waiting for transfers between devices: 27.5 us -> 15 us
  Pallas kernels: 85.2 us -> 87.8 us
    ppermute x4, waiting for transfers between devices: 8.23 us -> 0.01 us  [to_a(): return lax.ppermute(x, 'ctx', step_a)]
    ppermute x5 -> x6, waiting for transfers between devices: 13.4 us -> 8.81 us  [swap(): return lax.ppermute(x, 'ctx', swap_pairs)]
    pallas_call x2 -> x3, Pallas kernels: 26.6 us -> 30.8 us  [the longest x2 26.4 us: forward(): pl.pallas_call(functools.partial(forward_kernel, js, bool(given), last),...]
    all_to_all x1, waiting for transfers between devices: 4.15 us -> 6.17 us  [shards(): term = lax.all_to_all(term, 'ctx', 0, 0)]
    pallas_call x3, Pallas kernels: 45 us -> 43 us  [backward(): pl.pallas_call(functools.partial(backward_kernel, js, carry, last), grid_...]
    ppermute x5 -> x6, starting transfers between devices: 6.94 us -> 5.14 us  [swap(): return lax.ppermute(x, 'ctx', swap_pairs)]
    ppermute x4, waiting for transfers between devices: 1.75 us -> 0.01 us  [to_b(): return lax.ppermute(x, 'ctx', step_b)]
  transfers between devices with their start and end apart: 15 -> 16, of which waited for: 6 -> 3; matrix products, arithmetic and copies ran while one was open for 2% -> 3% of each run, Pallas kernels for 35% -> 53%
where the time goes in v3:
time: 161 us; the launch traced here: 158 us
  Pallas kernels  87.8 us (55%)
  starting transfers between devices  47.3 us (29%)
  waiting for transfers between devices  15 us (9%)
  other arithmetic  4.85 us (3%)
  local copies, waits for them, and re-layouts  2.3 us (1%)
    pallas_call x3, Pallas kernels, backward(): pl.pallas_call(functools.partial(backward_kernel, js, carry, last), grid_...  43 us
    pallas_call x2, Pallas kernels, forward(): pl.pallas_call(functools.partial(forward_kernel, js, bool(given), last),...  26.4 us
    ppermute x4, starting transfers between devices, to_b(): return lax.ppermute(x, 'ctx', step_b)  16.3 us
    all_to_all x1, starting transfers between devices, shards(): term = lax.all_to_all(term, 'ctx', 0, 0)  9.55 us
    ppermute x4, starting transfers between devices, to_a(): return lax.ppermute(x, 'ctx', step_a)  8.86 us
    ppermute x6, waiting for transfers between devices, swap(): return lax.ppermute(x, 'ctx', swap_pairs)  8.81 us
    all_to_all x1, starting transfers between devices, shards(): term = lax.all_to_all(term.reshape(dps, -1, term.shape[1]), 'dp', 0, 0)  7.44 us
    all_to_all x1, waiting for transfers between devices, shards(): term = lax.all_to_all(term, 'ctx', 0, 0)  6.17 us
  transfers between devices with their start and end apart: 16, of which 3 were waited for; matrix products, arithmetic and copies ran while one was open for 3% of the time, Pallas kernels for 53%

profile of v3, /device:TPU:38, one launch (start us, length us, event | category | flops | bytes accessed | tf_op | source)
XLA Modules:
  0.0 158.2 jit_solution(219441097857894223)
XLA Ops:
  0.6 0.6 pad_add_fusion.scal
  1.2 3.8 %split_kvq.1 = (bf16[2,320,512]{2,1,0:T(8,128)(2,1)}, bf16[2,320,512]{2,1,0:T(8,128)(2,1)}, bf16[1,320,512]{2,1,0:T(8,128)(2,1)}, bf16[1,320,512]{2,1,0:T(8,128)(2,1)}) custom-call(s32[3]{0:T(128)} %pad_add_fusion.scal, bf16[512,640]{1,0:T(8,128)(2,1)} %bitcast.14, bf16[512,640]{1,0:T(8,128)(2,1)} %bitcast.15, bf16[512,640]{1,0:T(8,128)(2,1)} %bitcast.16), custom_call_target="tpu_custom_call" | custom-call | flops 4600000000 | bytes 400000 | tf_op jit(solution)/shard_map/split_kvq/pallas_call | solution.py:71
  5.0 0.8 collective-permute-start.2
  5.9 3.8 %collective-permute-start.5 = (bf16[2,320,512]{2,1,0:T(8,128)(2,1)}, bf16[2,320,512]{2,1,0:T(8,128)(2,1)}, u32[]{:S(2)}, u32[]{:S(2)}) collective-permute-start(bf16[2,320,512]{2,1,0:T(8,128)(2,1)} %get-tuple-element.38.refs_0_), channel_id=1, source_target_pairs={{1,3},{2,0},{3,5},{4,2},{5,7},{6,4},{7,9},{8,6},{9,11},{10,8},{11,... | collective-permute-start | bytes 1966088 | tf_op jit(solution)/shard_map/ppermute | solution.py:327
  9.7 2.9 %collective-permute-start.6 = (bf16[2,320,512]{2,1,0:T(8,128)(2,1)}, bf16[2,320,512]{2,1,0:T(8,128)(2,1)}, u32[]{:S(2)}, u32[]{:S(2)}) collective-permute-start(bf16[2,320,512]{2,1,0:T(8,128)(2,1)} %get-tuple-element.38.refs_0_), channel_id=1, source_target_pairs={{0,2},{2,4},{3,1},{4,6},{5,3},{6,8},{7,5},{8,10},{9,7},{10,12},{11... | collective-permute-start | bytes 1966088 | tf_op jit(solution)/shard_map/ppermute | solution.py:324
  12.6 0.4 collective-permute-start
  13.0 4.4 %attention_grad.1 = (bf16[1,320,512]{2,1,0:T(8,128)(2,1)}, bf16[1,320,512]{2,1,0:T(8,128)(2,1)}) custom-call(s32[3]{0:T(128)} %pad_add_fusion.scal, bf16[512,1280]{1,0:T(8,128)(2,1)} %bitcast.12, bf16[640,1280]{1,0:T(8,128)(2,1)} %w_ref.1), custom_call_target="tpu_custom_call" | custom-call | flops 4600000000 | bytes 400000 | tf_op jit(solution)/shard_map/attention_grad/pallas_call | solution.py:93
  17.4 1.7 %collective-permute-start.1 = (bf16[1,320,512]{2,1,0:T(8,128)(2,1)}, bf16[1,320,512]{2,1,0:T(8,128)(2,1)}, u32[]{:S(2)}, u32[]{:S(2)}) collective-permute-start(bf16[1,320,512]{2,1,0:T(8,128)(2,1)} %get-tuple-element.36), channel_id=1, source_target_pairs={{0,1},{1,0},{2,3},{3,2},{4,5},{5,4},{6,7},{7,6},{8,9},{9,8},{10,11... | collective-permute-start | bytes 983048 | tf_op jit(solution)/shard_map/ppermute | solution.py:321
  19.1 3.8 %collective-permute-done.2.refs_1_.refs_2_ = bf16[2,320,512]{2,1,0:T(8,128)(2,1)S(1)} collective-permute-done((bf16[2,320,512]{2,1,0:T(8,128)(2,1)}, bf16[2,320,512]{2,1,0:T(8,128)(2,1)S(1)}, u32[]{:S(2)}, u32[]{:S(2)}) %collective-permute-start.2) | collective-permute-done | bytes 655392 | tf_op jit(solution)/shard_map/ppermute | solution.py:321
  22.9 2.0 %collective-permute-start.3 = (bf16[2,320,512]{2,1,0:T(8,128)(2,1)S(1)}, bf16[2,320,512]{2,1,0:T(8,128)(2,1)}, u32[]{:S(2)}, u32[]{:S(2)}) collective-permute-start(bf16[2,320,512]{2,1,0:T(8,128)(2,1)S(1)} %collective-permute-done.2.refs_1_.refs_2_), channel_id=1, source_target_pairs={{0,2},{2,4},{3,1},{4,6},{5,3},{6,8},{7,5},{8,10},{9,7},{10,12},{11... | collective-permute-start | bytes 1966088 | tf_op jit(solution)/shard_map/ppermute | solution.py:324
  24.9 5.0 %collective-permute-done.qp = bf16[1,320,512]{2,1,0:T(8,128)(2,1)S(1)} collective-permute-done((bf16[1,320,512]{2,1,0:T(8,128)(2,1)}, bf16[1,320,512]{2,1,0:T(8,128)(2,1)S(1)}, u32[]{:S(2)}, u32[]{:S(2)}) %collective-permute-start) | collective-permute-done | bytes 327712 | tf_op jit(solution)/shard_map/ppermute | solution.py:321
  29.9 3.8 %collective-permute-start.4 = (bf16[2,320,512]{2,1,0:T(8,128)(2,1)S(1)}, bf16[2,320,512]{2,1,0:T(8,128)(2,1)}, u32[]{:S(2)}, u32[]{:S(2)}) collective-permute-start(bf16[2,320,512]{2,1,0:T(8,128)(2,1)S(1)} %collective-permute-done.2.refs_1_.refs_2_), channel_id=1, source_target_pairs={{1,3},{2,0},{3,5},{4,2},{5,7},{6,4},{7,9},{8,6},{9,11},{10,8},{11,... | collective-permute-start | bytes 1966088 | tf_op jit(solution)/shard_map/ppermute | solution.py:327
  33.7 0.0 collective-permute-done.5.refs_2_.refs_1_
  33.7 0.0 collective-permute-done.6.refs_3_.refs_0_
  33.8 16.3 %forward_2340.1 = (f32[1,320,512]{2,1,0:T(8,128)}, f32[1,320,512]{2,1,0:T(8,128)}, f32[5,4,512]{2,1,0:T(4,128)}) custom-call(s32[3]{0:T(128)} %pad_add_fusion.scal, bf16[1,320,512]{2,1,0:T(8,128)(2,1)} %get-tuple-element.33.qm, bf16[1,320,512]{2,1,0:T(8,128)(2,1)} %copy-done.2, bf16[2,320,512]{2,1,0:T(8,128)(2,1)} %get-tuple-element.38.refs_0_, ...), custom_call_target="tpu_custom_call" | custom-call | flops 18400000000 | bytes 1600000 | tf_op jit(solution)/shard_map/forward_2340/pallas_call | solution.py:171
  50.1 0.0 collective-permute-done.3.refs_0_
  50.1 0.0 collective-permute-done.4.refs_1_
  50.1 10.1 %forward_15.1 = (bf16[1,320,512]{2,1,0:T(8,128)(2,1)}, bf16[1,320,512]{2,1,0:T(8,128)(2,1)}, f32[5,2,512]{2,1,0:T(2,128)}) custom-call(s32[3]{0:T(128)} %pad_add_fusion.scal, bf16[1,320,512]{2,1,0:T(8,128)(2,1)} %get-tuple-element.33.qm, bf16[1,320,512]{2,1,0:T(8,128)(2,1)} %copy-done.2, bf16[2,320,512]{2,1,0:T(8,128)(2,1)} %collective-permute-done.3.refs_0_, ...), custom_call_target="tpu_custom_call" | custom-call | flops 9200000000 | bytes 800000 | tf_op jit(solution)/shard_map/forward_15/pallas_call | solution.py:171
  60.1 0.0 collective-permute-start.7
  60.2 0.0 collective-permute-done.1.gp
  60.2 12.8 %backward_15.1 = (bf16[2,320,512]{2,1,0:T(8,128)(2,1)}, bf16[2,320,512]{2,1,0:T(8,128)(2,1)}, f32[1,320,512]{2,1,0:T(8,128)}, f32[1,320,512]{2,1,0:T(8,128)}) custom-call(s32[3]{0:T(128)} %pad_add_fusion.scal, bf16[1,320,512]{2,1,0:T(8,128)(2,1)} %get-tuple-element.33.qm, bf16[1,320,512]{2,1,0:T(8,128)(2,1)} %copy-done.2, ...), custom_call_target="tpu_custom_call" | custom-call | flops 14949999616 | bytes 1300000 | tf_op jit(solution)/shard_map/backward_15/pallas_call | solution.py:239
  73.0 3.8 %collective-permute-start.11 = (bf16[2,320,512]{2,1,0:T(8,128)(2,1)}, bf16[2,320,512]{2,1,0:T(8,128)(2,1)S(1)}, u32[]{:S(2)}, u32[]{:S(2)}) collective-permute-start(bf16[2,320,512]{2,1,0:T(8,128)(2,1)} %get-tuple-element.56), channel_id=1, source_target_pairs={{1,3},{2,0},{3,5},{4,2},{5,7},{6,4},{7,9},{8,6},{9,11},{10,8},{11,... | collective-permute-start | bytes 1966088 | tf_op jit(solution)/shard_map/ppermute | solution.py:327
  76.8 2.1 %collective-permute-start.12 = (bf16[2,320,512]{2,1,0:T(8,128)(2,1)}, bf16[2,320,512]{2,1,0:T(8,128)(2,1)}, u32[]{:S(2)}, u32[]{:S(2)}) collective-permute-start(bf16[2,320,512]{2,1,0:T(8,128)(2,1)} %get-tuple-element.57), channel_id=1, source_target_pairs={{0,2},{2,4},{3,1},{4,6},{5,3},{6,8},{7,5},{8,10},{9,7},{10,12},{11... | collective-permute-start | bytes 1966088 | tf_op jit(solution)/shard_map/ppermute | solution.py:324
  78.9 0.0 collective-permute-done.7.o_got
  78.9 0.7 copy-done.3
  79.6 6.0 %projection_term.1 = bf16[1280,640]{1,0:T(8,128)(2,1)} custom-call(s32[3]{0:T(128)} %pad_add_fusion.scal, bf16[1,320,512]{2,1,0:T(8,128)(2,1)} %get-tuple-element.42.o.om, bf16[1,320,512]{2,1,0:T(8,128)(2,1)} %copy-done.3, bf16[512,1280]{1,0:T(8,128)(2,1)} %bitcast.13), custom_call_target="tpu_custom_call" | custom-call | flops 4600000000 | bytes 400000 | tf_op jit(solution)/shard_map/projection_term/pallas_call | solution.py:290
  85.6 7.4 %all-to-all-start = ((bf16[16,80,640]{2,1,0:T(8,128)(2,1)}), bf16[16,80,640]{2,1,0:T(8,128)(2,1)}, u32[]{:S(2)}, u32[]{:S(2)}) async-start(bf16[16,80,640]{2,1,0:T(8,128)(2,1)} %bitcast.11), calls=%async_computation | async-start | bytes 3276800 | tf_op jit(solution)/shard_map/all_to_all | solution.py:359
  93.1 19.9 %backward_043.1 = (bf16[2,320,512]{2,1,0:T(8,128)(2,1)}, bf16[2,320,512]{2,1,0:T(8,128)(2,1)}, f32[2,320,512]{2,1,0:T(8,128)}, f32[1,320,512]{2,1,0:T(8,128)}, f32[1,320,512]{2,1,0:T(8,128)}) custom-call(s32[3]{0:T(128)} %pad_add_fusion.scal, bf16[1,320,512]{2,1,0:T(8,128)(2,1)} %get-tuple-element.33.qm, bf16[1,320,512]{2,1,0:T(8,128)(2,1)} %copy-done.2, ...), custom_call_target="tpu_custom_call" | custom-call | flops 23000000512 | bytes 2000000 | tf_op jit(solution)/shard_map/backward_043/pallas_call | solution.py:239
  113.0 1.9 %collective-permute-start.10 = (bf16[2,320,512]{2,1,0:T(8,128)(2,1)}, bf16[2,320,512]{2,1,0:T(8,128)(2,1)}, u32[]{:S(2)}, u32[]{:S(2)}) collective-permute-start(bf16[2,320,512]{2,1,0:T(8,128)(2,1)} %get-tuple-element.54), channel_id=1, source_target_pairs={{0,2},{2,4},{3,1},{4,6},{5,3},{6,8},{7,5},{8,10},{9,7},{10,12},{11... | collective-permute-start | bytes 1966088 | tf_op jit(solution)/shard_map/ppermute | solution.py:324
  114.9 4.9 %collective-permute-start.9 = (bf16[2,320,512]{2,1,0:T(8,128)(2,1)}, bf16[2,320,512]{2,1,0:T(8,128)(2,1)}, u32[]{:S(2)}, u32[]{:S(2)}) collective-permute-start(bf16[2,320,512]{2,1,0:T(8,128)(2,1)} %get-tuple-element.53), channel_id=1, source_target_pairs={{1,3},{2,0},{3,5},{4,2},{5,7},{6,4},{7,9},{8,6},{9,11},{10,8},{11,... | collective-permute-start | bytes 1966088 | tf_op jit(solution)/shard_map/ppermute | solution.py:327
  119.8 0.0 collective-permute-done.11
  119.8 0.0 copy-start
  119.8 0.0 collective-permute-done.12
  119.8 0.8 copy-done
  120.6 1.9 %add_convert_fusion = bf16[2,320,512]{2,1,0:T(8,128)(2,1)S(1)} fusion(bf16[2,320,512]{2,1,0:T(8,128)(2,1)} %collective-permute-done.12, f32[2,320,512]{2,1,0:T(8,128)} %get-tuple-element.55, bf16[2,320,512]{2,1,0:T(8,128)(2,1)} %copy-done), kind=kLoop, calls=%fused_computation.1 | loop fusion | flops 1638400 | bytes 3276800 | tf_op jit(solution)/shard_map/convert_element_type | solution.py:353
  122.6 2.1 %collective-permute-start.13 = (bf16[2,320,512]{2,1,0:T(8,128)(2,1)S(1)}, bf16[2,320,512]{2,1,0:T(8,128)(2,1)}, u32[]{:S(2)}, u32[]{:S(2)}) collective-permute-start(bf16[2,320,512]{2,1,0:T(8,128)(2,1)S(1)} %add_convert_fusion), channel_id=1, source_target_pairs={{0,1},{1,0},{2,3},{3,2},{4,5},{5,4},{6,7},{7,6},{8,9},{9,8},{10,11... | collective-permute-start | bytes 1966088 | tf_op jit(solution)/shard_map/ppermute | solution.py:321
  124.7 0.0 all-to-all-done
  124.7 1.7 %convert_reduce_fusion = f32[80,640]{1,0:T(8,128)S(1)} fusion(bf16[16,80,640]{2,1,0:T(8,128)(2,1)} %all-to-all-done), kind=kLoop, calls=%fused_computation | loop fusion | flops 1587200 | bytes 1843200 | tf_op jit(solution)/shard_map/reduce_sum | solution.py:360
  126.3 0.8 reshape.15
  127.1 10.3 %backward_2.1 = (f32[2,320,512]{2,1,0:T(8,128)}, bf16[1,320,512]{2,1,0:T(8,128)(2,1)}, bf16[1,320,512]{2,1,0:T(8,128)(2,1)}) custom-call(s32[3]{0:T(128)} %pad_add_fusion.scal, bf16[1,320,512]{2,1,0:T(8,128)(2,1)} %get-tuple-element.33.qm, bf16[1,320,512]{2,1,0:T(8,128)(2,1)} %copy-done.2, bf16[1,320,512]{2,1,0:T(8,128)(2,1)} %get-tuple-element.35.gm, ...), custom_call_target="tpu_custom_call" | custom-call | flops 10350000128 | bytes 900000 | tf_op jit(solution)/shard_map/backward_2/pallas_call | solution.py:239
  137.4 0.1 collective-permute-start.8
  137.5 9.6 %all-to-all-start.1 = ((f32[16,5,640]{2,1,0:T(8,128)}), f32[16,5,640]{2,1,0:T(8,128)S(1)}, u32[]{:S(2)}, u32[]{:S(2)}) async-start(f32[16,5,640]{2,1,0:T(8,128)} %reshape.15), calls=%async_computation.1 | async-start | bytes 655360 | tf_op jit(solution)/shard_map/all_to_all | solution.py:363
  147.1 0.0 collective-permute-done.10.b
  147.1 0.0 collective-permute-done.9.a
  147.1 0.0 collective-permute-done.13.got
  147.1 4.3 %sum_and_turn.1 = (bf16[512,640]{1,0:T(8,128)(2,1)}, bf16[512,640]{1,0:T(8,128)(2,1)}, bf16[512,640]{1,0:T(8,128)(2,1)}) custom-call(s32[3]{0:T(128)} %pad_add_fusion.scal, bf16[1,320,512]{2,1,0:T(8,128)(2,1)} %get-tuple-element.50.dq, bf16[1,320,512]{2,1,0:T(8,128)(2,1)} %collective-permute-done.8.dq_got, f32[2,320,512]{2,1,0:T(8,128)} %get-tuple-element.52.mid, ...), custom_call_target="tpu_custom_call" | custom-call | flops 4600000000 | bytes 400000 | tf_op jit(solution)/shard_map/sum_and_turn/pallas_call | solution.py:267
  151.4 6.2 %all-to-all-done.1 = f32[16,5,640]{2,1,0:T(8,128)S(1)} async-done(((f32[16,5,640]{2,1,0:T(8,128)}), f32[16,5,640]{2,1,0:T(8,128)S(1)}, u32[]{:S(2)}, u32[]{:S(2)}) %all-to-all-start.1) | async-done | bytes 204832 | tf_op jit(solution)/shard_map/all_to_all | solution.py:363
  157.5 0.6 reduce_sum.19
  (6 shorter events, 0.0 us)
Async XLA Ops:
  5.0 17.8 %collective-permute-start.2 = (bf16[2,320,512]{2,1,0:T(8,128)(2,1)}, bf16[2,320,512]{2,1,0:T(8,128)(2,1)S(1)}, u32[]{:S(2)}, u32[]{:S(2)}) collective-permute-start(bf16[2,320,512]{2,1,0:T(8,128)(2,1)} %get-tuple-element.37), channel_id=1, source_target_pairs={{0,1},{1,0},{2,3},{3,2},{4,5},{5,4},{6,7},{7,6},{8,9},{9,8},{10,11... | collective-permute-start | bytes 1966088 | tf_op jit(solution)/shard_map/ppermute | solution.py:321
  5.9 27.9 %collective-permute-start.5 = (bf16[2,320,512]{2,1,0:T(8,128)(2,1)}, bf16[2,320,512]{2,1,0:T(8,128)(2,1)}, u32[]{:S(2)}, u32[]{:S(2)}) collective-permute-start(bf16[2,320,512]{2,1,0:T(8,128)(2,1)} %get-tuple-element.38.refs_0_), channel_id=1, source_target_pairs={{1,3},{2,0},{3,5},{4,2},{5,7},{6,4},{7,9},{8,6},{9,11},{10,8},{11,... | collective-permute-start | bytes 1966088 | tf_op jit(solution)/shard_map/ppermute | solution.py:327
  9.7 24.0 %collective-permute-start.6 = (bf16[2,320,512]{2,1,0:T(8,128)(2,1)}, bf16[2,320,512]{2,1,0:T(8,128)(2,1)}, u32[]{:S(2)}, u32[]{:S(2)}) collective-permute-start(bf16[2,320,512]{2,1,0:T(8,128)(2,1)} %get-tuple-element.38.refs_0_), channel_id=1, source_target_pairs={{0,2},{2,4},{3,1},{4,6},{5,3},{6,8},{7,5},{8,10},{9,7},{10,12},{11... | collective-permute-start | bytes 1966088 | tf_op jit(solution)/shard_map/ppermute | solution.py:324
  12.6 17.3 %collective-permute-start = (bf16[1,320,512]{2,1,0:T(8,128)(2,1)}, bf16[1,320,512]{2,1,0:T(8,128)(2,1)S(1)}, u32[]{:S(2)}, u32[]{:S(2)}) collective-permute-start(bf16[1,320,512]{2,1,0:T(8,128)(2,1)} %get-tuple-element.34), channel_id=1, source_target_pairs={{0,1},{1,0},{2,3},{3,2},{4,5},{5,4},{6,7},{7,6},{8,9},{9,8},{10,11... | collective-permute-start | bytes 983048 | tf_op jit(solution)/shard_map/ppermute | solution.py:321
  17.4 42.8 %collective-permute-start.1 = (bf16[1,320,512]{2,1,0:T(8,128)(2,1)}, bf16[1,320,512]{2,1,0:T(8,128)(2,1)}, u32[]{:S(2)}, u32[]{:S(2)}) collective-permute-start(bf16[1,320,512]{2,1,0:T(8,128)(2,1)} %get-tuple-element.36), channel_id=1, source_target_pairs={{0,1},{1,0},{2,3},{3,2},{4,5},{5,4},{6,7},{7,6},{8,9},{9,8},{10,11... | collective-permute-start | bytes 983048 | tf_op jit(solution)/shard_map/ppermute | solution.py:321
  22.9 10.9 %copy-start.1 = (bf16[2,320,512]{2,1,0:T(8,128)(2,1)}, bf16[2,320,512]{2,1,0:T(8,128)(2,1)S(1)}, u32[]{:S(2)}) copy-start(bf16[2,320,512]{2,1,0:T(8,128)(2,1)S(1)} %collective-permute-done.2.refs_1_.refs_2_) | copy-start | bytes 1966084
  22.9 27.2 %collective-permute-start.3 = (bf16[2,320,512]{2,1,0:T(8,128)(2,1)S(1)}, bf16[2,320,512]{2,1,0:T(8,128)(2,1)}, u32[]{:S(2)}, u32[]{:S(2)}) collective-permute-start(bf16[2,320,512]{2,1,0:T(8,128)(2,1)S(1)} %collective-permute-done.2.refs_1_.refs_2_), channel_id=1, source_target_pairs={{0,2},{2,4},{3,1},{4,6},{5,3},{6,8},{7,5},{8,10},{9,7},{10,12},{11... | collective-permute-start | bytes 1966088 | tf_op jit(solution)/shard_map/ppermute | solution.py:324
  29.9 3.9 %copy-start.2 = (bf16[1,320,512]{2,1,0:T(8,128)(2,1)}, bf16[1,320,512]{2,1,0:T(8,128)(2,1)S(1)}, u32[]{:S(2)}) copy-start(bf16[1,320,512]{2,1,0:T(8,128)(2,1)S(1)} %collective-permute-done.qp) | copy-start | bytes 983044
  29.9 20.2 %collective-permute-start.4 = (bf16[2,320,512]{2,1,0:T(8,128)(2,1)S(1)}, bf16[2,320,512]{2,1,0:T(8,128)(2,1)}, u32[]{:S(2)}, u32[]{:S(2)}) collective-permute-start(bf16[2,320,512]{2,1,0:T(8,128)(2,1)S(1)} %collective-permute-done.2.refs_1_.refs_2_), channel_id=1, source_target_pairs={{1,3},{2,0},{3,5},{4,2},{5,7},{6,4},{7,9},{8,6},{9,11},{10,8},{11,... | collective-permute-start | bytes 1966088 | tf_op jit(solution)/shard_map/ppermute | solution.py:327
  60.1 18.8 %collective-permute-start.7 = (bf16[1,320,512]{2,1,0:T(8,128)(2,1)}, bf16[1,320,512]{2,1,0:T(8,128)(2,1)S(1)}, u32[]{:S(2)}, u32[]{:S(2)}) collective-permute-start(bf16[1,320,512]{2,1,0:T(8,128)(2,1)} %get-tuple-element.43.op), channel_id=1, source_target_pairs={{0,1},{1,0},{2,3},{3,2},{4,5},{5,4},{6,7},{7,6},{8,9},{9,8},{10,11... | collective-permute-start | bytes 983048 | tf_op jit(solution)/shard_map/ppermute | solution.py:321
  73.0 46.8 %collective-permute-start.11 = (bf16[2,320,512]{2,1,0:T(8,128)(2,1)}, bf16[2,320,512]{2,1,0:T(8,128)(2,1)S(1)}, u32[]{:S(2)}, u32[]{:S(2)}) collective-permute-start(bf16[2,320,512]{2,1,0:T(8,128)(2,1)} %get-tuple-element.56), channel_id=1, source_target_pairs={{1,3},{2,0},{3,5},{4,2},{5,7},{6,4},{7,9},{8,6},{9,11},{10,8},{11,... | collective-permute-start | bytes 1966088 | tf_op jit(solution)/shard_map/ppermute | solution.py:327
  76.8 43.0 %collective-permute-start.12 = (bf16[2,320,512]{2,1,0:T(8,128)(2,1)}, bf16[2,320,512]{2,1,0:T(8,128)(2,1)}, u32[]{:S(2)}, u32[]{:S(2)}) collective-permute-start(bf16[2,320,512]{2,1,0:T(8,128)(2,1)} %get-tuple-element.57), channel_id=1, source_target_pairs={{0,2},{2,4},{3,1},{4,6},{5,3},{6,8},{7,5},{8,10},{9,7},{10,12},{11... | collective-permute-start | bytes 1966088 | tf_op jit(solution)/shard_map/ppermute | solution.py:324
  78.9 0.7 copy-start.3
  85.6 39.0 %all-to-all-start = ((bf16[16,80,640]{2,1,0:T(8,128)(2,1)}), bf16[16,80,640]{2,1,0:T(8,128)(2,1)}, u32[]{:S(2)}, u32[]{:S(2)}) async-start(bf16[16,80,640]{2,1,0:T(8,128)(2,1)} %bitcast.11), calls=%async_computation | async-start | bytes 3276800 | tf_op jit(solution)/shard_map/all_to_all | solution.py:359
  113.0 34.1 %collective-permute-start.10 = (bf16[2,320,512]{2,1,0:T(8,128)(2,1)}, bf16[2,320,512]{2,1,0:T(8,128)(2,1)}, u32[]{:S(2)}, u32[]{:S(2)}) collective-permute-start(bf16[2,320,512]{2,1,0:T(8,128)(2,1)} %get-tuple-element.54), channel_id=1, source_target_pairs={{0,2},{2,4},{3,1},{4,6},{5,3},{6,8},{7,5},{8,10},{9,7},{10,12},{11... | collective-permute-start | bytes 1966088 | tf_op jit(solution)/shard_map/ppermute | solution.py:324
  114.9 32.2 %collective-permute-start.9 = (bf16[2,320,512]{2,1,0:T(8,128)(2,1)}, bf16[2,320,512]{2,1,0:T(8,128)(2,1)}, u32[]{:S(2)}, u32[]{:S(2)}) collective-permute-start(bf16[2,320,512]{2,1,0:T(8,128)(2,1)} %get-tuple-element.53), channel_id=1, source_target_pairs={{1,3},{2,0},{3,5},{4,2},{5,7},{6,4},{7,9},{8,6},{9,11},{10,8},{11,... | collective-permute-start | bytes 1966088 | tf_op jit(solution)/shard_map/ppermute | solution.py:327
  119.8 0.8 copy-start
  122.6 24.5 %collective-permute-start.13 = (bf16[2,320,512]{2,1,0:T(8,128)(2,1)S(1)}, bf16[2,320,512]{2,1,0:T(8,128)(2,1)}, u32[]{:S(2)}, u32[]{:S(2)}) collective-permute-start(bf16[2,320,512]{2,1,0:T(8,128)(2,1)S(1)} %add_convert_fusion), channel_id=1, source_target_pairs={{0,1},{1,0},{2,3},{3,2},{4,5},{5,4},{6,7},{7,6},{8,9},{9,8},{10,11... | collective-permute-start | bytes 1966088 | tf_op jit(solution)/shard_map/ppermute | solution.py:321
  137.4 9.7 %collective-permute-start.8 = (bf16[1,320,512]{2,1,0:T(8,128)(2,1)}, bf16[1,320,512]{2,1,0:T(8,128)(2,1)}, u32[]{:S(2)}, u32[]{:S(2)}) collective-permute-start(bf16[1,320,512]{2,1,0:T(8,128)(2,1)} %get-tuple-element.51), channel_id=1, source_target_pairs={{0,1},{1,0},{2,3},{3,2},{4,5},{5,4},{6,7},{7,6},{8,9},{9,8},{10,11... | collective-permute-start | bytes 983048 | tf_op jit(solution)/shard_map/ppermute | solution.py:321
  137.5 20.0 %all-to-all-start.1 = ((f32[16,5,640]{2,1,0:T(8,128)}), f32[16,5,640]{2,1,0:T(8,128)S(1)}, u32[]{:S(2)}, u32[]{:S(2)}) async-start(f32[16,5,640]{2,1,0:T(8,128)} %reshape.15), calls=%async_computation.1 | async-start | bytes 655360 | tf_op jit(solution)/shard_map/all_to_all | solution.py:363

commit v4 on v3

--- a/solution.py
+++ b/solution.py
@@ -82,11 +82,12 @@
     )(scal, k, v, q)
 
 
-def grad_kernel(scal, dy_ref, w_ref, mine, send):
+def grad_kernel(scal, dy_ref, w_ref, mine, send, dy_turned):
     odd = scal[2] > 0
     low, high = halves(mm(w_ref[...], dy_ref[...], 1, 1).astype(BF16))
     mine[0] = jnp.where(odd, high, low)
     send[0] = jnp.where(odd, low, high)
+    dy_turned[...] = jnp.transpose(dy_ref[...])
 
 
 def attention_grad(scal, dy, w):
@@ -96,9 +97,9 @@
             num_scalar_prefetch=1,
             grid=(1,),
             in_specs=[whole(dy.shape), whole(w.shape)],
-            out_specs=[whole((1, ROWS, TOK))] * 2,
-        ),
-        out_shape=[head_major(1)] * 2,
+            out_specs=[whole((1, ROWS, TOK))] * 2 + [whole(dy.shape[::-1])],
+        ),
+        out_shape=[head_major(1)] * 2 + [jax.ShapeDtypeStruct(dy.shape[::-1], BF16)],
         name="attention_grad",
         **params(4),
     )(scal, dy, w)
@@ -185,11 +186,11 @@
     )(scal, *q, *[kv[j] for j in js], *given)
 
 
-def backward_kernel(js, carry, last, scal, qm, qp, gm, gp, om, op, lse, *refs):
+def backward_kernel(js, late, scal, qm, qp, gm, gp, om, op, lse, *refs):
     n = len(js)
     kv, refs = refs[:n], refs[n:]
-    if carry:
-        dq_in, refs = refs[:2], refs[2:]
+    if late:
+        dq_in, arrived, refs = refs[:2], refs[2:4], refs[4:]
     dkv, dq_out = refs[:n], refs[n:]
     qs = (qm[0], qp[0])
     gs = (gm[0], gp[0])
@@ -199,7 +200,7 @@
         jnp.sum(gs[i].astype(F32) * os[i].astype(F32), axis=0, keepdims=True) for i in (0, 1)
     ]
     q_turned = [jnp.transpose(x) for x in qs]
-    dq = [dq_in[0][0], dq_in[1][0]] if carry else [None, None]
+    dq = [dq_in[0][0], dq_in[1][0]] if late else [None, None]
     units = [(idx, i) for idx, j in enumerate(js) for i in (0, 1) if j not in UNSEEN[i]]
     turned = {}
 
@@ -226,80 +227,88 @@
         x = mm(kv[idx][0], ds, 1, 0)
         dq[i] = x if dq[i] is None else dq[i] + x
         if n + 1 == len(units) or units[n + 1][0] != idx:
-            dkv[idx][0] = (jnp.transpose(dk) * SCALE).astype(dkv[idx].dtype)
+            dk = jnp.transpose(dk) * SCALE
+            if late and js[idx] == 3:
+                dk = dk + arrived[0][0].astype(F32) + arrived[1][0].astype(F32)
+                dv = dv + arrived[0][1].astype(F32) + arrived[1][1].astype(F32)
+            dkv[idx][0] = dk.astype(dkv[idx].dtype)
             dkv[idx][1] = dv.astype(dkv[idx].dtype)
             dk = dv = None
-    for i in (0, 1):
-        dq_out[i][0] = (dq[i] * SCALE).astype(BF16) if last else dq[i]
-
-
-def backward(js, scal, q, g, o, lse, kv, dq_in, last, dtypes, us):
-    n = len(js)
-    carry = dq_in is not None
-    return pl.pallas_call(
-        functools.partial(backward_kernel, js, carry, last),
+    if late:
+        dq_out[0][0] = (dq[0] * SCALE).astype(BF16)
+        dkv[js.index(3)][2] = (dq[1] * SCALE).astype(BF16)
+    else:
+        dq_out[0][0] = dq[0]
+        dq_out[1][0] = dq[1]
+
+
+def backward(js, scal, q, g, o, lse, kv, outs, dq_in=(), arrived=(), us=13):
+    late = bool(arrived)
+    dq_out = [head_major(1, BF16)] if late else [head_major(1, F32)] * 2
+    return pl.pallas_call(
+        functools.partial(backward_kernel, js, late),
         grid_spec=pltpu.PrefetchScalarGridSpec(
             num_scalar_prefetch=1,
             grid=(HALF,),
             in_specs=[head_block(1)] * 6
             + [stat_block(2)]
-            + [head_block(2)] * n
-            + [head_block(1)] * (2 if carry else 0),
-            out_specs=[head_block(2)] * n + [head_block(1)] * 2,
-        ),
-        out_shape=[head_major(2, t) for t in dtypes]
-        + [head_major(1, BF16 if last else F32)] * 2,
+            + [head_block(2)] * len(js)
+            + [head_block(1)] * len(dq_in)
+            + [head_block(2)] * len(arrived),
+            out_specs=[head_block(x.shape[0]) for x in outs]
+            + [head_block(1)] * len(dq_out),
+        ),
+        out_shape=list(outs) + dq_out,
         name="backward_" + "".join(str(j) for j in js),
         **params(us),
-    )(scal, *q, *g, *o, lse, *[kv[j] for j in js], *(dq_in if carry else ()))
-
-
-def finish_kernel(scal, dq, dq_got, mid, a, b, got, gq, gk, gv):
+    )(scal, *q, *g, *o, lse, *[kv[j] for j in js], *dq_in, *arrived)
+
+
+def finish_kernel(scal, dq, mid, a, b, got, gq, gk, gv):
     odd = scal[2] > 0
-    gq[...] = jnp.transpose(in_order(odd, dq[0], dq_got[0]))
+    gq[...] = jnp.transpose(in_order(odd, dq[0], got[2]))
     for n, ref in ((0, gk), (1, gv)):
         total = mid[n] + a[n].astype(F32) + b[n].astype(F32)
         ref[...] = jnp.transpose(in_order(odd, total.astype(BF16), got[n]))
 
 
-def finish(scal, dq, dq_got, mid, a, b, got):
+def finish(scal, dq, mid, a, b, got):
     out = (TOK, 2 * ROWS)
     return pl.pallas_call(
         finish_kernel,
         grid_spec=pltpu.PrefetchScalarGridSpec(
             num_scalar_prefetch=1,
             grid=(1,),
-            in_specs=[whole((1, ROWS, TOK))] * 2 + [whole((2, ROWS, TOK))] * 4,
+            in_specs=[whole((1, ROWS, TOK))]
+            + [whole((2, ROWS, TOK))] * 3
+            + [whole((3, ROWS, TOK))],
             out_specs=[whole(out)] * 3,
         ),
         out_shape=[jax.ShapeDtypeStruct(out, BF16)] * 3,
         name="sum_and_turn",
         **params(4),
-    )(scal, dq, dq_got, mid, a, b, got)
-
-
-def project_kernel(norm, scal, o, o_got, dy, term):
-    odd = scal[2] > 0
-    attn = in_order(odd, o[0], o_got[0])
-    turned = jnp.transpose(dy[...])
-    term[...] = (mm(turned, attn, 1, 1) * norm).astype(BF16)
-
-
-def project(scal, o, o_got, dy, norm):
-    wide = 256
+    )(scal, dq, mid, a, b, got)
+
+
+def project_kernel(norm, scal, o, o_got, dy_turned, term):
+    attn = in_order(scal[2] > 0, o[0], o_got[0])
+    term[...] = (mm(dy_turned[...], attn, 1, 1) * norm).astype(BF16)
+
+
+def project(scal, o, o_got, dy_turned, norm):
+    out = (dy_turned.shape[0], 2 * ROWS)
     return pl.pallas_call(
         functools.partial(project_kernel, norm),
         grid_spec=pltpu.PrefetchScalarGridSpec(
             num_scalar_prefetch=1,
-            grid=(dy.shape[1] // wide,),
-            in_specs=[whole((1, ROWS, TOK))] * 2
-            + [pl.BlockSpec((TOK, wide), lambda i, s: (0, i))],
-            out_specs=pl.BlockSpec((wide, 2 * ROWS), lambda i, s: (i, 0)),
-        ),
-        out_shape=jax.ShapeDtypeStruct((dy.shape[1], 2 * ROWS), BF16),
+            grid=(1,),
+            in_specs=[whole((1, ROWS, TOK))] * 2 + [whole(dy_turned.shape)],
+            out_specs=whole(out),
+        ),
+        out_shape=jax.ShapeDtypeStruct(out, BF16),
         name="projection_term",
         **params(4),
-    )(scal, o, o_got, dy)
+    )(scal, o, o_got, dy_turned)
 
 
 def shards(queries, keys, values, grad_out, out_proj):
@@ -331,7 +340,7 @@
     kv_got = swap(kv_send)
     a_mine, b_mine = to_a(kv_mine), to_b(kv_mine)
     q_got = swap(q_send)
-    g_mine, g_send = attention_grad(scal, dy, out_proj)
+    g_mine, g_send, dy_turned = attention_grad(scal, dy, out_proj)
     g_got = swap(g_send)
     a_got, b_got = to_a(kv_got), to_b(kv_got)
     kv = (a_mine, a_got, kv_mine, kv_got, b_mine, b_got)
@@ -342,32 +351,26 @@
     o_got = swap(o_send)
     o = (o_mine, o_send)
 
-    pa_p, pb_p, dq_m, dq_p = backward(
-        (1, 5), scal, q, g, o, lse, kv, None, False, (BF16, BF16), 13
+    pair = head_major(2)
+    pa, pb, dq_m, dq_p = backward((1, 5), scal, q, g, o, lse, kv, (pair, pair))
+    arrived = (to_b(pa), to_a(pb))
+    outs = (head_major(3), pair, pair, head_major(2, F32))
+    for_partner, pa, pb, mid, dq = backward(
+        (3, 0, 4, 2), scal, q, g, o, lse, kv, outs, (dq_m, dq_p), arrived, 27
     )
-    back_a_p, back_b_p = to_b(pa_p), to_a(pb_p)
-    pa_m, pb_m, mid_p, dq_m, dq_p = backward(
-        (0, 4, 3), scal, q, g, o, lse, kv, (dq_m, dq_p), False, (BF16, BF16, F32), 20
-    )
-    back_a_m, back_b_m = to_b(pa_m), to_a(pb_m)
-    sum_p = (mid_p + back_a_p.astype(F32) + back_b_p.astype(F32)).astype(BF16)
-    got_kv = swap(sum_p)
+    got = swap(for_partner)
+    back_a, back_b = to_b(pa), to_a(pb)
 
     dps = lax.axis_size("dp")
     norm = float(TOK * blocks * dps) ** (-0.5)
-    term = project(scal, o_mine, o_got, dy, norm)
+    term = project(scal, o_mine, o_got, dy_turned, norm)
     term = lax.all_to_all(term.reshape(dps, -1, term.shape[1]), "dp", 0, 0)
     term = jnp.sum(term.astype(F32), axis=0)
     term = term.reshape(blocks, -1, term.shape[1])
-    term, dq_m = lax.optimization_barrier((term, dq_m))
     term = lax.all_to_all(term, "ctx", 0, 0)
     proj = jnp.sum(term, axis=0)
 
-    mid_m, dq_m, dq_p = backward(
-        (2,), scal, q, g, o, lse, kv, (dq_m, dq_p), True, (F32,), 9
-    )
-    dq_got = swap(dq_p)
-    gq, gk, gv = finish(scal, dq_m, dq_got, mid_m, back_a_m, back_b_m, got_kv)
+    gq, gk, gv = finish(scal, dq, mid, back_a, back_b, got)
     return gq[None], gk[None], gv[None], proj
 
 

time: 161 us -> 157 us (0.975)
  Pallas kernels: 87.8 us -> 83.6 us
  waiting for transfers between devices: 15 us -> 19 us
  other arithmetic: 4.85 us -> 2.98 us
    ppermute x4, waiting for transfers between devices: 0.01 us -> 8.4 us  [to_a(): return lax.ppermute(x, 'ctx', step_a)]
    all_to_all x1, waiting for transfers between devices: 6.17 us -> 2.27 us  [shards(): term = lax.all_to_all(term, 'ctx', 0, 0)]
    pallas_call x3 -> x2, Pallas kernels: 43 us -> 39.8 us  [backward(): pl.pallas_call(functools.partial(backward_kernel, js, late), grid_spec=pl...]
    convert_element_type x1 -> x0, other arithmetic: 1.95 us -> none  [shards(): sum_p = (mid_p + back_a_p.astype(F32) + back_b_p.astype(F32)).astype(BF16)]
    ppermute x6 -> x5, waiting for transfers between devices: 8.81 us -> 7.4 us  [swap(): return lax.ppermute(x, 'ctx', swap_pairs)]
    ppermute x6 -> x5, starting transfers between devices: 5.14 us -> 5.7 us  [swap(): return lax.ppermute(x, 'ctx', swap_pairs)]
  transfers between devices with their start and end apart: 16 -> 15, of which waited for: 3 -> 6; matrix products, arithmetic and copies ran while one was open for 3% -> 2% of each run, Pallas kernels for 53% -> 52%
where the time goes in v4:
time: 157 us; the launch traced here: 155 us
  Pallas kernels  83.6 us (53%)
  starting transfers between devices  46.7 us (30%)
  waiting for transfers between devices  19 us (12%)
  other arithmetic  2.98 us (2%)
    pallas_call x2, Pallas kernels, backward(): pl.pallas_call(functools.partial(backward_kernel, js, late), grid_spec=pl...  39.8 us
    pallas_call x2, Pallas kernels, forward(): pl.pallas_call(functools.partial(forward_kernel, js, bool(given), last),...  26.4 us
    ppermute x4, starting transfers between devices, to_b(): return lax.ppermute(x, 'ctx', step_b)  15.1 us
    all_to_all x1, starting transfers between devices, shards(): term = lax.all_to_all(term, 'ctx', 0, 0)  10.2 us
    ppermute x4, waiting for transfers between devices, to_a(): return lax.ppermute(x, 'ctx', step_a)  8.4 us
    ppermute x4, starting transfers between devices, to_a(): return lax.ppermute(x, 'ctx', step_a)  8.3 us
    all_to_all x1, starting transfers between devices, shards(): term = lax.all_to_all(term.reshape(dps, -1, term.shape[1]), 'dp', 0, 0)  7.45 us
    ppermute x5, waiting for transfers between devices, swap(): return lax.ppermute(x, 'ctx', swap_pairs)  7.4 us
  transfers between devices with their start and end apart: 15, of which 6 were waited for; matrix products, arithmetic and copies ran while one was open for 2% of the time, Pallas kernels for 52%

profile of v4, /device:TPU:38, one launch (start us, length us, event | category | flops | bytes accessed | tf_op | source)
XLA Modules:
  0.0 154.7 jit_solution(16188642107728736365)
XLA Ops:
  0.6 0.7 pad_add_fusion.scal
  1.3 3.8 %split_kvq.1 = (bf16[2,320,512]{2,1,0:T(8,128)(2,1)}, bf16[2,320,512]{2,1,0:T(8,128)(2,1)}, bf16[1,320,512]{2,1,0:T(8,128)(2,1)}, bf16[1,320,512]{2,1,0:T(8,128)(2,1)}) custom-call(s32[3]{0:T(128)} %pad_add_fusion.scal, bf16[512,640]{1,0:T(8,128)(2,1)} %bitcast.13, bf16[512,640]{1,0:T(8,128)(2,1)} %bitcast.14, bf16[512,640]{1,0:T(8,128)(2,1)} %bitcast.15), custom_call_target="tpu_custom_call" | custom-call | flops 4600000000 | bytes 400000 | tf_op jit(solution)/shard_map/split_kvq/pallas_call | solution.py:71
  5.1 0.8 collective-permute-start.2
  6.0 2.0 %collective-permute-start.6 = (bf16[2,320,512]{2,1,0:T(8,128)(2,1)}, bf16[2,320,512]{2,1,0:T(8,128)(2,1)}, u32[]{:S(2)}, u32[]{:S(2)}) collective-permute-start(bf16[2,320,512]{2,1,0:T(8,128)(2,1)} %get-tuple-element.34.refs_0_.refs_3_), channel_id=1, source_target_pairs={{0,2},{2,4},{3,1},{4,6},{5,3},{6,8},{7,5},{8,10},{9,7},{10,12},{11... | collective-permute-start | bytes 1966088 | tf_op jit(solution)/shard_map/ppermute | solution.py:333
  8.0 3.8 %collective-permute-start.5 = (bf16[2,320,512]{2,1,0:T(8,128)(2,1)}, bf16[2,320,512]{2,1,0:T(8,128)(2,1)}, u32[]{:S(2)}, u32[]{:S(2)}) collective-permute-start(bf16[2,320,512]{2,1,0:T(8,128)(2,1)} %get-tuple-element.34.refs_0_.refs_3_), channel_id=1, source_target_pairs={{1,3},{2,0},{3,5},{4,2},{5,7},{6,4},{7,9},{8,6},{9,11},{10,8},{11,... | collective-permute-start | bytes 1966088 | tf_op jit(solution)/shard_map/ppermute | solution.py:336
  11.8 2.1 %collective-permute-start = (bf16[1,320,512]{2,1,0:T(8,128)(2,1)}, bf16[1,320,512]{2,1,0:T(8,128)(2,1)S(1)}, u32[]{:S(2)}, u32[]{:S(2)}) collective-permute-start(bf16[1,320,512]{2,1,0:T(8,128)(2,1)} %get-tuple-element.30), channel_id=1, source_target_pairs={{0,1},{1,0},{2,3},{3,2},{4,5},{5,4},{6,7},{7,6},{8,9},{9,8},{10,11... | collective-permute-start | bytes 983048 | tf_op jit(solution)/shard_map/ppermute | solution.py:330
  13.9 4.8 %attention_grad.1 = (bf16[1,320,512]{2,1,0:T(8,128)(2,1)}, bf16[1,320,512]{2,1,0:T(8,128)(2,1)}, bf16[1280,512]{1,0:T(8,128)(2,1)}) custom-call(s32[3]{0:T(128)} %pad_add_fusion.scal, bf16[512,1280]{1,0:T(8,128)(2,1)} %bitcast.12, bf16[640,1280]{1,0:T(8,128)(2,1)} %w_ref.1), custom_call_target="tpu_custom_call" | custom-call | flops 4600000000 | bytes 400000 | tf_op jit(solution)/shard_map/attention_grad/pallas_call | solution.py:94
  18.7 0.0 collective-permute-start.1
  18.8 4.2 %collective-permute-done.2.refs_1_.refs_0_ = bf16[2,320,512]{2,1,0:T(8,128)(2,1)S(1)} collective-permute-done((bf16[2,320,512]{2,1,0:T(8,128)(2,1)}, bf16[2,320,512]{2,1,0:T(8,128)(2,1)S(1)}, u32[]{:S(2)}, u32[]{:S(2)}) %collective-permute-start.2) | collective-permute-done | bytes 655392 | tf_op jit(solution)/shard_map/ppermute | solution.py:330
  23.0 3.8 %collective-permute-start.4 = (bf16[2,320,512]{2,1,0:T(8,128)(2,1)S(1)}, bf16[2,320,512]{2,1,0:T(8,128)(2,1)}, u32[]{:S(2)}, u32[]{:S(2)}) collective-permute-start(bf16[2,320,512]{2,1,0:T(8,128)(2,1)S(1)} %collective-permute-done.2.refs_1_.refs_0_), channel_id=1, source_target_pairs={{1,3},{2,0},{3,5},{4,2},{5,7},{6,4},{7,9},{8,6},{9,11},{10,8},{11,... | collective-permute-start | bytes 1966088 | tf_op jit(solution)/shard_map/ppermute | solution.py:336
  26.8 3.2 %collective-permute-done.qp = bf16[1,320,512]{2,1,0:T(8,128)(2,1)S(1)} collective-permute-done((bf16[1,320,512]{2,1,0:T(8,128)(2,1)}, bf16[1,320,512]{2,1,0:T(8,128)(2,1)S(1)}, u32[]{:S(2)}, u32[]{:S(2)}) %collective-permute-start) | collective-permute-done | bytes 327712 | tf_op jit(solution)/shard_map/ppermute | solution.py:330
  30.0 2.0 %collective-permute-start.3 = (bf16[2,320,512]{2,1,0:T(8,128)(2,1)S(1)}, bf16[2,320,512]{2,1,0:T(8,128)(2,1)}, u32[]{:S(2)}, u32[]{:S(2)}) collective-permute-start(bf16[2,320,512]{2,1,0:T(8,128)(2,1)S(1)} %collective-permute-done.2.refs_1_.refs_0_), channel_id=1, source_target_pairs={{0,2},{2,4},{3,1},{4,6},{5,3},{6,8},{7,5},{8,10},{9,7},{10,12},{11... | collective-permute-start | bytes 1966088 | tf_op jit(solution)/shard_map/ppermute | solution.py:333
  32.0 0.0 collective-permute-done.6.refs_3_.refs_1_
  32.0 0.0 collective-permute-done.5.refs_2_
  32.0 0.0 copy-done
  32.0 0.0 copy-done.3
  32.0 16.3 %forward_2340.1 = (f32[1,320,512]{2,1,0:T(8,128)}, f32[1,320,512]{2,1,0:T(8,128)}, f32[5,4,512]{2,1,0:T(4,128)}) custom-call(s32[3]{0:T(128)} %pad_add_fusion.scal, bf16[1,320,512]{2,1,0:T(8,128)(2,1)} %get-tuple-element.29.qm, bf16[1,320,512]{2,1,0:T(8,128)(2,1)} %copy-done.3, bf16[2,320,512]{2,1,0:T(8,128)(2,1)} %get-tuple-element.34.refs_0_.refs_3_, ...), custom_call_target="tpu_custom_call" | custom-call | flops 18400000000 | bytes 1600000 | tf_op jit(solution)/shard_map/forward_2340/pallas_call | solution.py:172
  48.3 0.0 collective-permute-done.4.refs_1_
  48.3 0.0 collective-permute-done.3.refs_0_
  48.3 10.1 %forward_15.1 = (bf16[1,320,512]{2,1,0:T(8,128)(2,1)}, bf16[1,320,512]{2,1,0:T(8,128)(2,1)}, f32[5,2,512]{2,1,0:T(2,128)}) custom-call(s32[3]{0:T(128)} %pad_add_fusion.scal, bf16[1,320,512]{2,1,0:T(8,128)(2,1)} %get-tuple-element.29.qm, bf16[1,320,512]{2,1,0:T(8,128)(2,1)} %copy-done.3, bf16[2,320,512]{2,1,0:T(8,128)(2,1)} %collective-permute-done.3.refs_0_, ...), custom_call_target="tpu_custom_call" | custom-call | flops 9200000000 | bytes 800000 | tf_op jit(solution)/shard_map/forward_15/pallas_call | solution.py:172
  58.4 2.6 %collective-permute-start.12 = (bf16[1,320,512]{2,1,0:T(8,128)(2,1)}, bf16[1,320,512]{2,1,0:T(8,128)(2,1)S(1)}, u32[]{:S(2)}, u32[]{:S(2)}) collective-permute-start(bf16[1,320,512]{2,1,0:T(8,128)(2,1)} %get-tuple-element.39.op), channel_id=1, source_target_pairs={{0,1},{1,0},{2,3},{3,2},{4,5},{5,4},{6,7},{7,6},{8,9},{9,8},{10,11... | collective-permute-start | bytes 983048 | tf_op jit(solution)/shard_map/ppermute | solution.py:330
  61.0 0.0 collective-permute-done.1.gp
  61.0 12.8 %backward_15.1 = (bf16[2,320,512]{2,1,0:T(8,128)(2,1)}, bf16[2,320,512]{2,1,0:T(8,128)(2,1)}, f32[1,320,512]{2,1,0:T(8,128)}, f32[1,320,512]{2,1,0:T(8,128)}) custom-call(s32[3]{0:T(128)} %pad_add_fusion.scal, bf16[1,320,512]{2,1,0:T(8,128)(2,1)} %get-tuple-element.29.qm, bf16[1,320,512]{2,1,0:T(8,128)(2,1)} %copy-done.3, ...), custom_call_target="tpu_custom_call" | custom-call | flops 14949999616 | bytes 1300000 | tf_op jit(solution)/shard_map/backward_15/pallas_call | solution.py:248
  73.9 3.8 %collective-permute-start.7 = (bf16[2,320,512]{2,1,0:T(8,128)(2,1)}, bf16[2,320,512]{2,1,0:T(8,128)(2,1)S(1)}, u32[]{:S(2)}, u32[]{:S(2)}) collective-permute-start(bf16[2,320,512]{2,1,0:T(8,128)(2,1)} %get-tuple-element.43), channel_id=1, source_target_pairs={{1,3},{2,0},{3,5},{4,2},{5,7},{6,4},{7,9},{8,6},{9,11},{10,8},{11,... | collective-permute-start | bytes 1966088 | tf_op jit(solution)/shard_map/ppermute | solution.py:336
  77.7 2.0 %collective-permute-start.8 = (bf16[2,320,512]{2,1,0:T(8,128)(2,1)}, bf16[2,320,512]{2,1,0:T(8,128)(2,1)}, u32[]{:S(2)}, u32[]{:S(2)}) collective-permute-start(bf16[2,320,512]{2,1,0:T(8,128)(2,1)} %get-tuple-element.44), channel_id=1, source_target_pairs={{0,2},{2,4},{3,1},{4,6},{5,3},{6,8},{7,5},{8,10},{9,7},{10,12},{11... | collective-permute-start | bytes 1966088 | tf_op jit(solution)/shard_map/ppermute | solution.py:333
  79.8 0.0 collective-permute-done.12.o_got
  79.8 0.0 copy-start.4
  79.8 0.7 copy-done.4
  80.5 4.6 %projection_term.1 = bf16[1280,640]{1,0:T(8,128)(2,1)} custom-call(s32[3]{0:T(128)} %pad_add_fusion.scal, bf16[1,320,512]{2,1,0:T(8,128)(2,1)} %get-tuple-element.38.om.o, bf16[1,320,512]{2,1,0:T(8,128)(2,1)} %copy-done.4, bf16[1280,512]{1,0:T(8,128)(2,1)} %get-tuple-element.53.dy_turned), custom_call_target="tpu_custom_call" | custom-call | flops 4600000000 | bytes 400000 | tf_op jit(solution)/shard_map/projection_term/pallas_call | solution.py:300
  85.1 7.5 %all-to-all-start = ((bf16[16,80,640]{2,1,0:T(8,128)(2,1)}), bf16[16,80,640]{2,1,0:T(8,128)(2,1)}, u32[]{:S(2)}, u32[]{:S(2)}) async-start(bf16[16,80,640]{2,1,0:T(8,128)(2,1)} %bitcast.11), calls=%async_computation | async-start | bytes 3276800 | tf_op jit(solution)/shard_map/all_to_all | solution.py:367
  92.6 0.0 collective-permute-done.7.refs_6_
  92.6 0.0 copy-start.1
  92.6 2.5 %collective-permute-done.8.refs_7_ = bf16[2,320,512]{2,1,0:T(8,128)(2,1)} collective-permute-done((bf16[2,320,512]{2,1,0:T(8,128)(2,1)}, bf16[2,320,512]{2,1,0:T(8,128)(2,1)}, u32[]{:S(2)}, u32[]{:S(2)}) %collective-permute-start.8) | collective-permute-done | bytes 655392 | tf_op jit(solution)/shard_map/ppermute | solution.py:333
  95.0 0.0 copy-done.1
  95.0 26.9 %backward_3042.1 = (bf16[3,320,512]{2,1,0:T(8,128)(2,1)}, bf16[2,320,512]{2,1,0:T(8,128)(2,1)}, bf16[2,320,512]{2,1,0:T(8,128)(2,1)}, f32[2,320,512]{2,1,0:T(8,128)}, bf16[1,320,512]{2,1,0:T(8,128)(2,1)}) custom-call(s32[3]{0:T(128)} %pad_add_fusion.scal, bf16[1,320,512]{2,1,0:T(8,128)(2,1)} %get-tuple-element.29.qm, bf16[1,320,512]{2,1,0:T(8,128)(2,1)} %copy-done.3, ...), custom_call_target="tpu_custom_call" | custom-call | flops 31050000384 | bytes 2700000 | tf_op jit(solution)/shard_map/backward_3042/pallas_call | solution.py:248
  122.0 0.1 collective-permute-start.11
  122.1 3.6 %collective-permute-start.9 = (bf16[2,320,512]{2,1,0:T(8,128)(2,1)}, bf16[2,320,512]{2,1,0:T(8,128)(2,1)S(1)}, u32[]{:S(2)}, u32[]{:S(2)}) collective-permute-start(bf16[2,320,512]{2,1,0:T(8,128)(2,1)} %get-tuple-element.47), channel_id=1, source_target_pairs={{1,3},{2,0},{3,5},{4,2},{5,7},{6,4},{7,9},{8,6},{9,11},{10,8},{11,... | collective-permute-start | bytes 1966088 | tf_op jit(solution)/shard_map/ppermute | solution.py:336
  125.7 2.2 %collective-permute-start.10 = (bf16[2,320,512]{2,1,0:T(8,128)(2,1)}, bf16[2,320,512]{2,1,0:T(8,128)(2,1)}, u32[]{:S(2)}, u32[]{:S(2)}) collective-permute-start(bf16[2,320,512]{2,1,0:T(8,128)(2,1)} %get-tuple-element.48), channel_id=1, source_target_pairs={{0,2},{2,4},{3,1},{4,6},{5,3},{6,8},{7,5},{8,10},{9,7},{10,12},{11... | collective-permute-start | bytes 1966088 | tf_op jit(solution)/shard_map/ppermute | solution.py:333
  128.0 0.0 all-to-all-done
  128.0 1.7 %convert_reduce_fusion = f32[80,640]{1,0:T(8,128)S(1)} fusion(bf16[16,80,640]{2,1,0:T(8,128)(2,1)} %all-to-all-done), kind=kLoop, calls=%fused_computation | loop fusion | flops 1587200 | bytes 1843200 | tf_op jit(solution)/shard_map/reduce_sum | solution.py:368
  129.7 0.8 reshape.15
  130.5 10.2 %all-to-all-start.1 = ((f32[16,5,640]{2,1,0:T(8,128)}), f32[16,5,640]{2,1,0:T(8,128)S(1)}, u32[]{:S(2)}, u32[]{:S(2)}) async-start(f32[16,5,640]{2,1,0:T(8,128)} %reshape.15), calls=%async_computation.1 | async-start | bytes 655360 | tf_op jit(solution)/shard_map/all_to_all | solution.py:370
  140.6 0.9 collective-permute-done.9.a
  141.5 5.9 %collective-permute-done.10.b = bf16[2,320,512]{2,1,0:T(8,128)(2,1)} collective-permute-done((bf16[2,320,512]{2,1,0:T(8,128)(2,1)}, bf16[2,320,512]{2,1,0:T(8,128)(2,1)}, u32[]{:S(2)}, u32[]{:S(2)}) %collective-permute-start.10) | collective-permute-done | bytes 655392 | tf_op jit(solution)/shard_map/ppermute | solution.py:333
  147.5 0.0 collective-permute-done.11.got
  147.5 4.3 %sum_and_turn.1 = (bf16[512,640]{1,0:T(8,128)(2,1)}, bf16[512,640]{1,0:T(8,128)(2,1)}, bf16[512,640]{1,0:T(8,128)(2,1)}) custom-call(s32[3]{0:T(128)} %pad_add_fusion.scal, bf16[1,320,512]{2,1,0:T(8,128)(2,1)} %get-tuple-element.45.dq, f32[2,320,512]{2,1,0:T(8,128)} %get-tuple-element.46.mid, bf16[2,320,512]{2,1,0:T(8,128)(2,1)} %copy-done.2, ...), custom_call_target="tpu_custom_call" | custom-call | flops 4600000000 | bytes 400000 | tf_op jit(solution)/shard_map/sum_and_turn/pallas_call | solution.py:277
  151.7 2.3 %all-to-all-done.1 = f32[16,5,640]{2,1,0:T(8,128)S(1)} async-done(((f32[16,5,640]{2,1,0:T(8,128)}), f32[16,5,640]{2,1,0:T(8,128)S(1)}, u32[]{:S(2)}, u32[]{:S(2)}) %all-to-all-start.1) | async-done | bytes 204832 | tf_op jit(solution)/shard_map/all_to_all | solution.py:370
  154.0 0.6 reduce_sum.19
  (4 shorter events, 0.0 us)
Async XLA Ops:
  5.1 17.8 %collective-permute-start.2 = (bf16[2,320,512]{2,1,0:T(8,128)(2,1)}, bf16[2,320,512]{2,1,0:T(8,128)(2,1)S(1)}, u32[]{:S(2)}, u32[]{:S(2)}) collective-permute-start(bf16[2,320,512]{2,1,0:T(8,128)(2,1)} %get-tuple-element.33), channel_id=1, source_target_pairs={{0,1},{1,0},{2,3},{3,2},{4,5},{5,4},{6,7},{7,6},{8,9},{9,8},{10,11... | collective-permute-start | bytes 1966088 | tf_op jit(solution)/shard_map/ppermute | solution.py:330
  6.0 26.0 %collective-permute-start.6 = (bf16[2,320,512]{2,1,0:T(8,128)(2,1)}, bf16[2,320,512]{2,1,0:T(8,128)(2,1)}, u32[]{:S(2)}, u32[]{:S(2)}) collective-permute-start(bf16[2,320,512]{2,1,0:T(8,128)(2,1)} %get-tuple-element.34.refs_0_.refs_3_), channel_id=1, source_target_pairs={{0,2},{2,4},{3,1},{4,6},{5,3},{6,8},{7,5},{8,10},{9,7},{10,12},{11... | collective-permute-start | bytes 1966088 | tf_op jit(solution)/shard_map/ppermute | solution.py:333
  8.0 24.0 %collective-permute-start.5 = (bf16[2,320,512]{2,1,0:T(8,128)(2,1)}, bf16[2,320,512]{2,1,0:T(8,128)(2,1)}, u32[]{:S(2)}, u32[]{:S(2)}) collective-permute-start(bf16[2,320,512]{2,1,0:T(8,128)(2,1)} %get-tuple-element.34.refs_0_.refs_3_), channel_id=1, source_target_pairs={{1,3},{2,0},{3,5},{4,2},{5,7},{6,4},{7,9},{8,6},{9,11},{10,8},{11,... | collective-permute-start | bytes 1966088 | tf_op jit(solution)/shard_map/ppermute | solution.py:336
  11.8 18.2 %collective-permute-start = (bf16[1,320,512]{2,1,0:T(8,128)(2,1)}, bf16[1,320,512]{2,1,0:T(8,128)(2,1)S(1)}, u32[]{:S(2)}, u32[]{:S(2)}) collective-permute-start(bf16[1,320,512]{2,1,0:T(8,128)(2,1)} %get-tuple-element.30), channel_id=1, source_target_pairs={{0,1},{1,0},{2,3},{3,2},{4,5},{5,4},{6,7},{7,6},{8,9},{9,8},{10,11... | collective-permute-start | bytes 983048 | tf_op jit(solution)/shard_map/ppermute | solution.py:330
  18.7 42.3 %collective-permute-start.1 = (bf16[1,320,512]{2,1,0:T(8,128)(2,1)}, bf16[1,320,512]{2,1,0:T(8,128)(2,1)}, u32[]{:S(2)}, u32[]{:S(2)}) collective-permute-start(bf16[1,320,512]{2,1,0:T(8,128)(2,1)} %get-tuple-element.32), channel_id=1, source_target_pairs={{0,1},{1,0},{2,3},{3,2},{4,5},{5,4},{6,7},{7,6},{8,9},{9,8},{10,11... | collective-permute-start | bytes 983048 | tf_op jit(solution)/shard_map/ppermute | solution.py:330
  23.0 9.1 %copy-start = (bf16[2,320,512]{2,1,0:T(8,128)(2,1)}, bf16[2,320,512]{2,1,0:T(8,128)(2,1)S(1)}, u32[]{:S(2)}) copy-start(bf16[2,320,512]{2,1,0:T(8,128)(2,1)S(1)} %collective-permute-done.2.refs_1_.refs_0_) | copy-start | bytes 1966084
  23.0 25.4 %collective-permute-start.4 = (bf16[2,320,512]{2,1,0:T(8,128)(2,1)S(1)}, bf16[2,320,512]{2,1,0:T(8,128)(2,1)}, u32[]{:S(2)}, u32[]{:S(2)}) collective-permute-start(bf16[2,320,512]{2,1,0:T(8,128)(2,1)S(1)} %collective-permute-done.2.refs_1_.refs_0_), channel_id=1, source_target_pairs={{1,3},{2,0},{3,5},{4,2},{5,7},{6,4},{7,9},{8,6},{9,11},{10,8},{11,... | collective-permute-start | bytes 1966088 | tf_op jit(solution)/shard_map/ppermute | solution.py:336
  30.0 2.0 %copy-start.3 = (bf16[1,320,512]{2,1,0:T(8,128)(2,1)}, bf16[1,320,512]{2,1,0:T(8,128)(2,1)S(1)}, u32[]{:S(2)}) copy-start(bf16[1,320,512]{2,1,0:T(8,128)(2,1)S(1)} %collective-permute-done.qp) | copy-start | bytes 983044
  30.0 18.3 %collective-permute-start.3 = (bf16[2,320,512]{2,1,0:T(8,128)(2,1)S(1)}, bf16[2,320,512]{2,1,0:T(8,128)(2,1)}, u32[]{:S(2)}, u32[]{:S(2)}) collective-permute-start(bf16[2,320,512]{2,1,0:T(8,128)(2,1)S(1)} %collective-permute-done.2.refs_1_.refs_0_), channel_id=1, source_target_pairs={{0,2},{2,4},{3,1},{4,6},{5,3},{6,8},{7,5},{8,10},{9,7},{10,12},{11... | collective-permute-start | bytes 1966088 | tf_op jit(solution)/shard_map/ppermute | solution.py:333
  58.4 21.4 %collective-permute-start.12 = (bf16[1,320,512]{2,1,0:T(8,128)(2,1)}, bf16[1,320,512]{2,1,0:T(8,128)(2,1)S(1)}, u32[]{:S(2)}, u32[]{:S(2)}) collective-permute-start(bf16[1,320,512]{2,1,0:T(8,128)(2,1)} %get-tuple-element.39.op), channel_id=1, source_target_pairs={{0,1},{1,0},{2,3},{3,2},{4,5},{5,4},{6,7},{7,6},{8,9},{9,8},{10,11... | collective-permute-start | bytes 983048 | tf_op jit(solution)/shard_map/ppermute | solution.py:330
  73.9 18.7 %collective-permute-start.7 = (bf16[2,320,512]{2,1,0:T(8,128)(2,1)}, bf16[2,320,512]{2,1,0:T(8,128)(2,1)S(1)}, u32[]{:S(2)}, u32[]{:S(2)}) collective-permute-start(bf16[2,320,512]{2,1,0:T(8,128)(2,1)} %get-tuple-element.43), channel_id=1, source_target_pairs={{1,3},{2,0},{3,5},{4,2},{5,7},{6,4},{7,9},{8,6},{9,11},{10,8},{11,... | collective-permute-start | bytes 1966088 | tf_op jit(solution)/shard_map/ppermute | solution.py:336
  77.7 17.3 %collective-permute-start.8 = (bf16[2,320,512]{2,1,0:T(8,128)(2,1)}, bf16[2,320,512]{2,1,0:T(8,128)(2,1)}, u32[]{:S(2)}, u32[]{:S(2)}) collective-permute-start(bf16[2,320,512]{2,1,0:T(8,128)(2,1)} %get-tuple-element.44), channel_id=1, source_target_pairs={{0,2},{2,4},{3,1},{4,6},{5,3},{6,8},{7,5},{8,10},{9,7},{10,12},{11... | collective-permute-start | bytes 1966088 | tf_op jit(solution)/shard_map/ppermute | solution.py:333
  79.8 0.7 copy-start.4
  85.1 42.9 %all-to-all-start = ((bf16[16,80,640]{2,1,0:T(8,128)(2,1)}), bf16[16,80,640]{2,1,0:T(8,128)(2,1)}, u32[]{:S(2)}, u32[]{:S(2)}) async-start(bf16[16,80,640]{2,1,0:T(8,128)(2,1)} %bitcast.11), calls=%async_computation | async-start | bytes 3276800 | tf_op jit(solution)/shard_map/all_to_all | solution.py:367
  92.6 2.5 %copy-start.1 = (bf16[2,320,512]{2,1,0:T(8,128)(2,1)}, bf16[2,320,512]{2,1,0:T(8,128)(2,1)S(1)}, u32[]{:S(2)}) copy-start(bf16[2,320,512]{2,1,0:T(8,128)(2,1)S(1)} %collective-permute-done.7.refs_6_) | copy-start | bytes 1966084
  122.0 25.5 %collective-permute-start.11 = (bf16[3,320,512]{2,1,0:T(8,128)(2,1)}, bf16[3,320,512]{2,1,0:T(8,128)(2,1)}, u32[]{:S(2)}, u32[]{:S(2)}) collective-permute-start(bf16[3,320,512]{2,1,0:T(8,128)(2,1)} %get-tuple-element.49), channel_id=1, source_target_pairs={{0,1},{1,0},{2,3},{3,2},{4,5},{5,4},{6,7},{7,6},{8,9},{9,8},{10,11... | collective-permute-start | bytes 2949128 | tf_op jit(solution)/shard_map/ppermute | solution.py:330
  122.1 19.5 %collective-permute-start.9 = (bf16[2,320,512]{2,1,0:T(8,128)(2,1)}, bf16[2,320,512]{2,1,0:T(8,128)(2,1)S(1)}, u32[]{:S(2)}, u32[]{:S(2)}) collective-permute-start(bf16[2,320,512]{2,1,0:T(8,128)(2,1)} %get-tuple-element.47), channel_id=1, source_target_pairs={{1,3},{2,0},{3,5},{4,2},{5,7},{6,4},{7,9},{8,6},{9,11},{10,8},{11,... | collective-permute-start | bytes 1966088 | tf_op jit(solution)/shard_map/ppermute | solution.py:336
  125.7 21.8 %collective-permute-start.10 = (bf16[2,320,512]{2,1,0:T(8,128)(2,1)}, bf16[2,320,512]{2,1,0:T(8,128)(2,1)}, u32[]{:S(2)}, u32[]{:S(2)}) collective-permute-start(bf16[2,320,512]{2,1,0:T(8,128)(2,1)} %get-tuple-element.48), channel_id=1, source_target_pairs={{0,2},{2,4},{3,1},{4,6},{5,3},{6,8},{7,5},{8,10},{9,7},{10,12},{11... | collective-permute-start | bytes 1966088 | tf_op jit(solution)/shard_map/ppermute | solution.py:333
  130.5 23.5 %all-to-all-start.1 = ((f32[16,5,640]{2,1,0:T(8,128)}), f32[16,5,640]{2,1,0:T(8,128)S(1)}, u32[]{:S(2)}, u32[]{:S(2)}) async-start(f32[16,5,640]{2,1,0:T(8,128)} %reshape.15), calls=%async_computation.1 | async-start | bytes 655360 | tf_op jit(solution)/shard_map/all_to_all | solution.py:370
  141.5 6.0 %copy-start.2 = (bf16[2,320,512]{2,1,0:T(8,128)(2,1)}, bf16[2,320,512]{2,1,0:T(8,128)(2,1)S(1)}, u32[]{:S(2)}) copy-start(bf16[2,320,512]{2,1,0:T(8,128)(2,1)S(1)} %collective-permute-done.9.a) | copy-start | bytes 1966084

commit v5 on v4

--- a/solution.py
+++ b/solution.py
@@ -16,6 +16,7 @@
 SCALE = HDIM ** (-0.5)
 BASE2 = SCALE * math.log2(math.e)
 BIG = 1e30
+FAR = 48.0
 F32 = jnp.float32
 BF16 = jnp.bfloat16
 
@@ -120,46 +121,65 @@
             turned[n] = jnp.transpose(kv[n][0])
         return mm(turned[n], qs[i], 1, 0)
 
-    top = [None, None]
-    total = [None, None]
-    out = [None, None]
     if carry:
         stats, o_in, refs = refs[0], refs[1:3], refs[3:]
-        for i in (0, 1):
-            top[i] = stats[0, i : i + 1, :]
-            total[i] = stats[0, 2 + i : 3 + i, :]
-            out[i] = o_in[i][0]
     om, op, stats_out = refs
-    ahead = scores(*units[0])
-    for n, (b, i) in enumerate(units):
-        s = ahead
-        if n + 1 < len(units):
-            ahead = scores(*units[n + 1])
-        flag = side_flag(scal, js[b])
-        here = jnp.max(s, axis=0, keepdims=True) * BASE2
-        if flag is not None:
-            here = jnp.where(flag > 0, here, -BIG)
-        first = top[i] is None
-        new = here if first else jnp.maximum(top[i], here)
-        sub = new if flag is None else jnp.where(flag > 0, new, BIG)
-        e = jnp.exp2(s * BASE2 - sub)
-        part = jnp.sum(e, axis=0, keepdims=True)
-        pv = mm(kv[b][1], e.astype(BF16), 1, 0)
-        if first:
-            total[i], out[i] = part, pv
-        else:
-            fade = jnp.exp2(top[i] - new)
-            total[i] = total[i] * fade + part
-            out[i] = out[i] * fade + pv
-        top[i] = new
-    for i, ref in ((0, om), (1, op)):
-        if last:
-            ref[0] = (out[i] * (1.0 / total[i])).astype(BF16)
-            stats_out[0, i : i + 1, :] = top[i] + jnp.log2(total[i])
-        else:
-            ref[0] = out[i]
-            stats_out[0, i : i + 1, :] = top[i]
-            stats_out[0, 2 + i : 3 + i, :] = total[i]
+
+    def run(running):
+        top, total, out = [None, None], [None, None], [None, None]
+        over = None
+        if carry:
+            for i in (0, 1):
+                top[i] = stats[0, i : i + 1, :]
+                total[i] = stats[0, 2 + i : 3 + i, :]
+                out[i] = o_in[i][0]
+        ahead = scores(*units[0])
+        for n, (b, i) in enumerate(units):
+            s = ahead
+            if n + 1 < len(units):
+                ahead = scores(*units[n + 1])
+            flag = side_flag(scal, js[b])
+            here = jnp.max(s, axis=0, keepdims=True) * BASE2
+            if flag is not None:
+                here = jnp.where(flag > 0, here, -BIG)
+            first = top[i] is None
+            if first:
+                new = here
+            elif running:
+                new = jnp.maximum(top[i], here)
+            else:
+                new = top[i]
+                over = here - new if over is None else jnp.maximum(over, here - new)
+            sub = new if flag is None else jnp.where(flag > 0, new, BIG)
+            e = jnp.exp2(s * BASE2 - sub)
+            part = jnp.sum(e, axis=0, keepdims=True)
+            pv = mm(kv[b][1], e.astype(BF16), 1, 0)
+            if first:
+                total[i], out[i] = part, pv
+            elif running:
+                fade = jnp.exp2(top[i] - new)
+                total[i] = total[i] * fade + part
+                out[i] = out[i] * fade + pv
+            else:
+                total[i] = total[i] + part
+                out[i] = out[i] + pv
+            top[i] = new
+        for i, ref in ((0, om), (1, op)):
+            if last:
+                ref[0] = (out[i] * (1.0 / total[i])).astype(BF16)
+                stats_out[0, i : i + 1, :] = top[i] + jnp.log2(total[i])
+            else:
+                ref[0] = out[i]
+                stats_out[0, i : i + 1, :] = top[i]
+                stats_out[0, 2 + i : 3 + i, :] = total[i]
+        return over
+
+    far = jnp.max(run(False)) > FAR
+
+    @pl.when(far)
+    def _():
+        turned.clear()
+        run(True)
 
 
 def stat_block(rows):
@@ -186,11 +206,15 @@
     )(scal, *q, *[kv[j] for j in js], *given)
 
 
-def backward_kernel(js, late, scal, qm, qp, gm, gp, om, op, lse, *refs):
+def backward_kernel(js, pairs, stage, scal, qm, qp, gm, gp, om, op, lse, *refs):
     n = len(js)
     kv, refs = refs[:n], refs[n:]
-    if late:
-        dq_in, arrived, refs = refs[:2], refs[2:4], refs[4:]
+    mine, partners = any(i == 0 for _, i in pairs), any(i == 1 for _, i in pairs)
+    dq_in = ()
+    if stage > 0:
+        dq_in, refs = refs[: mine + partners], refs[mine + partners :]
+    if stage == 1:
+        arrived, refs = refs[:2], refs[2:]
     dkv, dq_out = refs[:n], refs[n:]
     qs = (qm[0], qp[0])
     gs = (gm[0], gp[0])
@@ -200,8 +224,8 @@
         jnp.sum(gs[i].astype(F32) * os[i].astype(F32), axis=0, keepdims=True) for i in (0, 1)
     ]
     q_turned = [jnp.transpose(x) for x in qs]
-    dq = [dq_in[0][0], dq_in[1][0]] if late else [None, None]
-    units = [(idx, i) for idx, j in enumerate(js) for i in (0, 1) if j not in UNSEEN[i]]
+    dq = [x[0] for x in dq_in] if stage > 0 else [None, None]
+    units = [(js.index(j), i) for j, i in pairs]
     turned = {}
 
     def products(idx, i):
@@ -228,51 +252,52 @@
         dq[i] = x if dq[i] is None else dq[i] + x
         if n + 1 == len(units) or units[n + 1][0] != idx:
             dk = jnp.transpose(dk) * SCALE
-            if late and js[idx] == 3:
+            if stage == 1 and js[idx] == 3:
                 dk = dk + arrived[0][0].astype(F32) + arrived[1][0].astype(F32)
                 dv = dv + arrived[0][1].astype(F32) + arrived[1][1].astype(F32)
             dkv[idx][0] = dk.astype(dkv[idx].dtype)
             dkv[idx][1] = dv.astype(dkv[idx].dtype)
             dk = dv = None
-    if late:
-        dq_out[0][0] = (dq[0] * SCALE).astype(BF16)
-        dkv[js.index(3)][2] = (dq[1] * SCALE).astype(BF16)
-    else:
+    if stage == 0:
         dq_out[0][0] = dq[0]
         dq_out[1][0] = dq[1]
-
-
-def backward(js, scal, q, g, o, lse, kv, outs, dq_in=(), arrived=(), us=13):
-    late = bool(arrived)
-    dq_out = [head_major(1, BF16)] if late else [head_major(1, F32)] * 2
-    return pl.pallas_call(
-        functools.partial(backward_kernel, js, late),
+    elif stage == 1:
+        dkv[js.index(3)][2] = (dq[1] * SCALE).astype(BF16)
+        dq_out[0][0] = dq[0]
+    else:
+        dq_out[0][0] = (dq[0] * SCALE).astype(BF16)
+
+
+def backward(stage, pairs, scal, q, g, o, lse, kv, outs, given=(), us=13):
+    js = tuple(dict.fromkeys(j for j, _ in pairs))
+    dq_out = [head_major(1, BF16 if stage == 2 else F32)] * (2 if stage == 0 else 1)
+    return pl.pallas_call(
+        functools.partial(backward_kernel, js, pairs, stage),
         grid_spec=pltpu.PrefetchScalarGridSpec(
             num_scalar_prefetch=1,
             grid=(HALF,),
             in_specs=[head_block(1)] * 6
             + [stat_block(2)]
             + [head_block(2)] * len(js)
-            + [head_block(1)] * len(dq_in)
-            + [head_block(2)] * len(arrived),
+            + [head_block(x.shape[0]) for x in given],
             out_specs=[head_block(x.shape[0]) for x in outs]
             + [head_block(1)] * len(dq_out),
         ),
         out_shape=list(outs) + dq_out,
         name="backward_" + "".join(str(j) for j in js),
         **params(us),
-    )(scal, *q, *g, *o, lse, *[kv[j] for j in js], *dq_in, *arrived)
-
-
-def finish_kernel(scal, dq, mid, a, b, got, gq, gk, gv):
+    )(scal, *q, *g, *o, lse, *[kv[j] for j in js], *given)
+
+
+def finish_kernel(scal, dq, mid, rest, a, b, got, gq, gk, gv):
     odd = scal[2] > 0
     gq[...] = jnp.transpose(in_order(odd, dq[0], got[2]))
     for n, ref in ((0, gk), (1, gv)):
-        total = mid[n] + a[n].astype(F32) + b[n].astype(F32)
+        total = mid[n] + rest[n] + a[n].astype(F32) + b[n].astype(F32)
         ref[...] = jnp.transpose(in_order(odd, total.astype(BF16), got[n]))
 
 
-def finish(scal, dq, mid, a, b, got):
+def finish(scal, dq, mid, rest, a, b, got):
     out = (TOK, 2 * ROWS)
     return pl.pallas_call(
         finish_kernel,
@@ -280,14 +305,14 @@
             num_scalar_prefetch=1,
             grid=(1,),
             in_specs=[whole((1, ROWS, TOK))]
-            + [whole((2, ROWS, TOK))] * 3
+            + [whole((2, ROWS, TOK))] * 4
             + [whole((3, ROWS, TOK))],
             out_specs=[whole(out)] * 3,
         ),
         out_shape=[jax.ShapeDtypeStruct(out, BF16)] * 3,
         name="sum_and_turn",
         **params(4),
-    )(scal, dq, mid, a, b, got)
+    )(scal, dq, mid, rest, a, b, got)
 
 
 def project_kernel(norm, scal, o, o_got, dy_turned, term):
@@ -352,14 +377,18 @@
     o = (o_mine, o_send)
 
     pair = head_major(2)
-    pa, pb, dq_m, dq_p = backward((1, 5), scal, q, g, o, lse, kv, (pair, pair))
+    work = (scal, q, g, o, lse, kv)
+    pa, pb, dq_m, dq_p = backward(0, ((1, 0), (1, 1), (5, 1)), *work, (pair, pair))
     arrived = (to_b(pa), to_a(pb))
-    outs = (head_major(3), pair, pair, head_major(2, F32))
-    for_partner, pa, pb, mid, dq = backward(
-        (3, 0, 4, 2), scal, q, g, o, lse, kv, outs, (dq_m, dq_p), arrived, 27
+    whole_pair = head_major(2, F32)
+    outs = (head_major(3), pair, pair, whole_pair)
+    pairs = ((3, 0), (3, 1), (0, 0), (4, 0), (4, 1), (2, 1))
+    for_partner, pa, pb, mid, dq_m = backward(
+        1, pairs, *work, outs, (dq_m, dq_p, *arrived), 24
     )
     got = swap(for_partner)
     back_a, back_b = to_b(pa), to_a(pb)
+    rest, dq = backward(2, ((2, 0),), *work, (whole_pair,), (dq_m,), 7)
 
     dps = lax.axis_size("dp")
     norm = float(TOK * blocks * dps) ** (-0.5)
@@ -370,7 +399,7 @@
     term = lax.all_to_all(term, "ctx", 0, 0)
     proj = jnp.sum(term, axis=0)
 
-    gq, gk, gv = finish(scal, dq, mid, back_a, back_b, got)
+    gq, gk, gv = finish(scal, dq, mid, rest, back_a, back_b, got)
     return gq[None], gk[None], gv[None], proj
 
 

time: 157 us -> 175 us (1.11)
  Pallas kernels: 83.6 us -> 103 us
  waiting for transfers between devices: 19 us -> 12.5 us
  starting transfers between devices: 46.7 us -> 48.9 us
    pallas_call x2, Pallas kernels: 26.4 us -> 41.8 us  [forward(): pl.pallas_call(functools.partial(forward_kernel, js, bool(given), last),...]
    ppermute x4, waiting for transfers between devices: 8.4 us -> 0.01 us  [to_a(): return lax.ppermute(x, 'ctx', step_a)]
    pallas_call x2 -> x3, Pallas kernels: 39.8 us -> 43.4 us  [backward(): pl.pallas_call(functools.partial(backward_kernel, js, pairs, stage), grid...]
    all_to_all x1, waiting for transfers between devices: 2.27 us -> 5.05 us  [shards(): term = lax.all_to_all(term, 'ctx', 0, 0)]
    all_to_all x1, starting transfers between devices: 7.45 us -> 10.1 us  [shards(): term = lax.all_to_all(term.reshape(dps, -1, term.shape[1]), 'dp', 0, 0)]
  transfers between devices with their start and end apart: 15 -> 15, of which waited for: 6 -> 3; matrix products, arithmetic and copies ran while one was open for 2% -> 1% of each run, Pallas kernels for 52% -> 58%
where the time goes in v5:
time: 175 us; the launch traced here: 171 us
  Pallas kernels  103 us (59%)
  starting transfers between devices  48.9 us (28%)
  waiting for transfers between devices  12.5 us (7%)
  local copies, waits for them, and re-layouts  3.2 us (2%)
  other arithmetic  2.91 us (2%)
    pallas_call x3, Pallas kernels, backward(): pl.pallas_call(functools.partial(backward_kernel, js, pairs, stage), grid...  43.4 us
    pallas_call x2, Pallas kernels, forward(): pl.pallas_call(functools.partial(forward_kernel, js, bool(given), last),...  41.8 us
    ppermute x4, starting transfers between devices, to_b(): return lax.ppermute(x, 'ctx', step_b)  14 us
    all_to_all x1, starting transfers between devices, shards(): term = lax.all_to_all(term, 'ctx', 0, 0)  10.9 us
    all_to_all x1, starting transfers between devices, shards(): term = lax.all_to_all(term.reshape(dps, -1, term.shape[1]), 'dp', 0, 0)  10.1 us
    ppermute x4, starting transfers between devices, to_a(): return lax.ppermute(x, 'ctx', step_a)  9.45 us
    ppermute x5, waiting for transfers between devices, swap(): return lax.ppermute(x, 'ctx', swap_pairs)  7.4 us
    all_to_all x1, waiting for transfers between devices, shards(): term = lax.all_to_all(term, 'ctx', 0, 0)  5.05 us
  transfers between devices with their start and end apart: 15, of which 3 were waited for; matrix products, arithmetic and copies ran while one was open for 1% of the time, Pallas kernels for 58%

profile of v5, /device:TPU:38, one launch (start us, length us, event | category | flops | bytes accessed | tf_op | source)
XLA Modules:
  0.0 171.5 jit_solution(15473929478431186081)
XLA Ops:
  0.6 0.6 pad_add_fusion.scal
  1.2 3.8 %split_kvq.1 = (bf16[2,320,512]{2,1,0:T(8,128)(2,1)}, bf16[2,320,512]{2,1,0:T(8,128)(2,1)}, bf16[1,320,512]{2,1,0:T(8,128)(2,1)}, bf16[1,320,512]{2,1,0:T(8,128)(2,1)}) custom-call(s32[3]{0:T(128)} %pad_add_fusion.scal, bf16[512,640]{1,0:T(8,128)(2,1)} %bitcast.13, bf16[512,640]{1,0:T(8,128)(2,1)} %bitcast.14, bf16[512,640]{1,0:T(8,128)(2,1)} %bitcast.15), custom_call_target="tpu_custom_call" | custom-call | flops 4600000000 | bytes 400000 | tf_op jit(solution)/shard_map/split_kvq/pallas_call | solution.py:72
  5.0 0.8 collective-permute-start.2
  5.9 2.0 %collective-permute-start.6 = (bf16[2,320,512]{2,1,0:T(8,128)(2,1)}, bf16[2,320,512]{2,1,0:T(8,128)(2,1)}, u32[]{:S(2)}, u32[]{:S(2)}) collective-permute-start(bf16[2,320,512]{2,1,0:T(8,128)(2,1)} %get-tuple-element.36.refs_0_.refs_3_), channel_id=1, source_target_pairs={{0,2},{2,4},{3,1},{4,6},{5,3},{6,8},{7,5},{8,10},{9,7},{10,12},{11... | collective-permute-start | bytes 1966088 | tf_op jit(solution)/shard_map/ppermute | solution.py:358
  7.9 3.8 %collective-permute-start.5 = (bf16[2,320,512]{2,1,0:T(8,128)(2,1)}, bf16[2,320,512]{2,1,0:T(8,128)(2,1)}, u32[]{:S(2)}, u32[]{:S(2)}) collective-permute-start(bf16[2,320,512]{2,1,0:T(8,128)(2,1)} %get-tuple-element.36.refs_0_.refs_3_), channel_id=1, source_target_pairs={{1,3},{2,0},{3,5},{4,2},{5,7},{6,4},{7,9},{8,6},{9,11},{10,8},{11,... | collective-permute-start | bytes 1966088 | tf_op jit(solution)/shard_map/ppermute | solution.py:361
  11.7 2.1 %collective-permute-start = (bf16[1,320,512]{2,1,0:T(8,128)(2,1)}, bf16[1,320,512]{2,1,0:T(8,128)(2,1)S(1)}, u32[]{:S(2)}, u32[]{:S(2)}) collective-permute-start(bf16[1,320,512]{2,1,0:T(8,128)(2,1)} %get-tuple-element.32), channel_id=1, source_target_pairs={{0,1},{1,0},{2,3},{3,2},{4,5},{5,4},{6,7},{7,6},{8,9},{9,8},{10,11... | collective-permute-start | bytes 983048 | tf_op jit(solution)/shard_map/ppermute | solution.py:355
  13.9 4.8 %attention_grad.1 = (bf16[1,320,512]{2,1,0:T(8,128)(2,1)}, bf16[1,320,512]{2,1,0:T(8,128)(2,1)}, bf16[1280,512]{1,0:T(8,128)(2,1)}) custom-call(s32[3]{0:T(128)} %pad_add_fusion.scal, bf16[512,1280]{1,0:T(8,128)(2,1)} %bitcast.12, bf16[640,1280]{1,0:T(8,128)(2,1)} %w_ref.1), custom_call_target="tpu_custom_call" | custom-call | flops 4600000000 | bytes 400000 | tf_op jit(solution)/shard_map/attention_grad/pallas_call | solution.py:95
  18.7 0.0 collective-permute-start.1
  18.7 4.2 %collective-permute-done.2.refs_1_.refs_0_ = bf16[2,320,512]{2,1,0:T(8,128)(2,1)S(1)} collective-permute-done((bf16[2,320,512]{2,1,0:T(8,128)(2,1)}, bf16[2,320,512]{2,1,0:T(8,128)(2,1)S(1)}, u32[]{:S(2)}, u32[]{:S(2)}) %collective-permute-start.2) | collective-permute-done | bytes 655392 | tf_op jit(solution)/shard_map/ppermute | solution.py:355
  22.9 3.8 %collective-permute-start.4 = (bf16[2,320,512]{2,1,0:T(8,128)(2,1)S(1)}, bf16[2,320,512]{2,1,0:T(8,128)(2,1)}, u32[]{:S(2)}, u32[]{:S(2)}) collective-permute-start(bf16[2,320,512]{2,1,0:T(8,128)(2,1)S(1)} %collective-permute-done.2.refs_1_.refs_0_), channel_id=1, source_target_pairs={{1,3},{2,0},{3,5},{4,2},{5,7},{6,4},{7,9},{8,6},{9,11},{10,8},{11,... | collective-permute-start | bytes 1966088 | tf_op jit(solution)/shard_map/ppermute | solution.py:361
  26.7 3.2 %collective-permute-done.qp = bf16[1,320,512]{2,1,0:T(8,128)(2,1)S(1)} collective-permute-done((bf16[1,320,512]{2,1,0:T(8,128)(2,1)}, bf16[1,320,512]{2,1,0:T(8,128)(2,1)S(1)}, u32[]{:S(2)}, u32[]{:S(2)}) %collective-permute-start) | collective-permute-done | bytes 327712 | tf_op jit(solution)/shard_map/ppermute | solution.py:355
  29.9 2.0 %collective-permute-start.3 = (bf16[2,320,512]{2,1,0:T(8,128)(2,1)S(1)}, bf16[2,320,512]{2,1,0:T(8,128)(2,1)}, u32[]{:S(2)}, u32[]{:S(2)}) collective-permute-start(bf16[2,320,512]{2,1,0:T(8,128)(2,1)S(1)} %collective-permute-done.2.refs_1_.refs_0_), channel_id=1, source_target_pairs={{0,2},{2,4},{3,1},{4,6},{5,3},{6,8},{7,5},{8,10},{9,7},{10,12},{11... | collective-permute-start | bytes 1966088 | tf_op jit(solution)/shard_map/ppermute | solution.py:358
  31.9 0.0 collective-permute-done.6.refs_3_.refs_1_
  31.9 0.0 collective-permute-done.5.refs_2_
  32.0 28.3 %forward_2340.1 = (f32[1,320,512]{2,1,0:T(8,128)}, f32[1,320,512]{2,1,0:T(8,128)}, f32[5,4,512]{2,1,0:T(4,128)}) custom-call(s32[3]{0:T(128)} %pad_add_fusion.scal, bf16[1,320,512]{2,1,0:T(8,128)(2,1)} %get-tuple-element.31.qm, bf16[1,320,512]{2,1,0:T(8,128)(2,1)} %copy-done.3, bf16[2,320,512]{2,1,0:T(8,128)(2,1)} %get-tuple-element.36.refs_0_.refs_3_, ...), custom_call_target="tpu_custom_call" | custom-call | flops 18400000000 | bytes 1600000 | tf_op jit(solution)/shard_map/forward_2340/pallas_call | solution.py:192
  60.2 0.0 collective-permute-done.4.refs_1_
  60.2 0.0 collective-permute-done.3.refs_0_
  60.3 13.6 %forward_15.1 = (bf16[1,320,512]{2,1,0:T(8,128)(2,1)}, bf16[1,320,512]{2,1,0:T(8,128)(2,1)}, f32[5,2,512]{2,1,0:T(2,128)}) custom-call(s32[3]{0:T(128)} %pad_add_fusion.scal, bf16[1,320,512]{2,1,0:T(8,128)(2,1)} %get-tuple-element.31.qm, bf16[1,320,512]{2,1,0:T(8,128)(2,1)} %copy-done.3, bf16[2,320,512]{2,1,0:T(8,128)(2,1)} %collective-permute-done.3.refs_0_, ...), custom_call_target="tpu_custom_call" | custom-call | flops 9200000000 | bytes 800000 | tf_op jit(solution)/shard_map/forward_15/pallas_call | solution.py:192
  73.8 1.5 collective-permute-start.12
  75.3 0.0 collective-permute-done.1.gp
  75.3 12.8 %backward_15.1 = (bf16[2,320,512]{2,1,0:T(8,128)(2,1)}, bf16[2,320,512]{2,1,0:T(8,128)(2,1)}, f32[1,320,512]{2,1,0:T(8,128)}, f32[1,320,512]{2,1,0:T(8,128)}) custom-call(s32[3]{0:T(128)} %pad_add_fusion.scal, bf16[1,320,512]{2,1,0:T(8,128)(2,1)} %get-tuple-element.31.qm, bf16[1,320,512]{2,1,0:T(8,128)(2,1)} %copy-done.3, ...), custom_call_target="tpu_custom_call" | custom-call | flops 14949999616 | bytes 1300000 | tf_op jit(solution)/shard_map/backward_15/pallas_call | solution.py:274
  88.1 2.4 %collective-permute-start.7 = (bf16[2,320,512]{2,1,0:T(8,128)(2,1)}, bf16[2,320,512]{2,1,0:T(8,128)(2,1)S(1)}, u32[]{:S(2)}, u32[]{:S(2)}) collective-permute-start(bf16[2,320,512]{2,1,0:T(8,128)(2,1)} %get-tuple-element.45), channel_id=1, source_target_pairs={{1,3},{2,0},{3,5},{4,2},{5,7},{6,4},{7,9},{8,6},{9,11},{10,8},{11,... | collective-permute-start | bytes 1966088 | tf_op jit(solution)/shard_map/ppermute | solution.py:361
  90.5 3.5 %collective-permute-start.8 = (bf16[2,320,512]{2,1,0:T(8,128)(2,1)}, bf16[2,320,512]{2,1,0:T(8,128)(2,1)}, u32[]{:S(2)}, u32[]{:S(2)}) collective-permute-start(bf16[2,320,512]{2,1,0:T(8,128)(2,1)} %get-tuple-element.46), channel_id=1, source_target_pairs={{0,2},{2,4},{3,1},{4,6},{5,3},{6,8},{7,5},{8,10},{9,7},{10,12},{11... | collective-permute-start | bytes 1966088 | tf_op jit(solution)/shard_map/ppermute | solution.py:358
  94.0 0.0 collective-permute-done.12.o_got
  94.0 0.7 copy-done.4
  94.8 4.6 %projection_term.1 = bf16[1280,640]{1,0:T(8,128)(2,1)} custom-call(s32[3]{0:T(128)} %pad_add_fusion.scal, bf16[1,320,512]{2,1,0:T(8,128)(2,1)} %get-tuple-element.40.om.o, bf16[1,320,512]{2,1,0:T(8,128)(2,1)} %copy-done.4, bf16[1280,512]{1,0:T(8,128)(2,1)} %get-tuple-element.57.dy_turned), custom_call_target="tpu_custom_call" | custom-call | flops 4600000000 | bytes 400000 | tf_op jit(solution)/shard_map/projection_term/pallas_call | solution.py:325
  99.4 10.1 %all-to-all-start = ((bf16[16,80,640]{2,1,0:T(8,128)(2,1)}), bf16[16,80,640]{2,1,0:T(8,128)(2,1)}, u32[]{:S(2)}, u32[]{:S(2)}) async-start(bf16[16,80,640]{2,1,0:T(8,128)(2,1)} %bitcast.11), calls=%async_computation | async-start | bytes 3276800 | tf_op jit(solution)/shard_map/all_to_all | solution.py:396
  109.4 0.0 collective-permute-done.7.refs_6_
  109.4 0.0 copy-start.2
  109.4 0.0 collective-permute-done.8.refs_7_
  109.4 0.8 copy-done.2
  110.3 22.8 %backward_3042.1 = (bf16[3,320,512]{2,1,0:T(8,128)(2,1)}, bf16[2,320,512]{2,1,0:T(8,128)(2,1)}, bf16[2,320,512]{2,1,0:T(8,128)(2,1)}, f32[2,320,512]{2,1,0:T(8,128)}, f32[1,320,512]{2,1,0:T(8,128)}) custom-call(s32[3]{0:T(128)} %pad_add_fusion.scal, bf16[1,320,512]{2,1,0:T(8,128)(2,1)} %get-tuple-element.31.qm, bf16[1,320,512]{2,1,0:T(8,128)(2,1)} %copy-done.3, ...), custom_call_target="tpu_custom_call" | custom-call | flops 27599998976 | bytes 2400000 | tf_op jit(solution)/shard_map/backward_3042/pallas_call | solution.py:274
  133.1 0.1 collective-permute-start.11
  133.2 3.9 %collective-permute-start.9 = (bf16[2,320,512]{2,1,0:T(8,128)(2,1)}, bf16[2,320,512]{2,1,0:T(8,128)(2,1)S(1)}, u32[]{:S(2)}, u32[]{:S(2)}) collective-permute-start(bf16[2,320,512]{2,1,0:T(8,128)(2,1)} %get-tuple-element.51), channel_id=1, source_target_pairs={{1,3},{2,0},{3,5},{4,2},{5,7},{6,4},{7,9},{8,6},{9,11},{10,8},{11,... | collective-permute-start | bytes 1966088 | tf_op jit(solution)/shard_map/ppermute | solution.py:361
  137.1 1.9 %collective-permute-start.10 = (bf16[2,320,512]{2,1,0:T(8,128)(2,1)}, bf16[2,320,512]{2,1,0:T(8,128)(2,1)}, u32[]{:S(2)}, u32[]{:S(2)}) collective-permute-start(bf16[2,320,512]{2,1,0:T(8,128)(2,1)} %get-tuple-element.52), channel_id=1, source_target_pairs={{0,2},{2,4},{3,1},{4,6},{5,3},{6,8},{7,5},{8,10},{9,7},{10,12},{11... | collective-permute-start | bytes 1966088 | tf_op jit(solution)/shard_map/ppermute | solution.py:358
  139.1 7.8 %backward_2.1 = (f32[2,320,512]{2,1,0:T(8,128)}, bf16[1,320,512]{2,1,0:T(8,128)(2,1)}) custom-call(s32[3]{0:T(128)} %pad_add_fusion.scal, bf16[1,320,512]{2,1,0:T(8,128)(2,1)} %get-tuple-element.31.qm, bf16[1,320,512]{2,1,0:T(8,128)(2,1)} %copy-done.3, bf16[1,320,512]{2,1,0:T(8,128)(2,1)} %get-tuple-element.33.gm, ...), custom_call_target="tpu_custom_call" | custom-call | flops 8049999872 | bytes 700000 | tf_op jit(solution)/shard_map/backward_2/pallas_call | solution.py:274
  146.8 0.0 all-to-all-done
  146.8 1.7 convert_reduce_fusion
  148.5 0.8 reshape.15
  149.3 10.9 %all-to-all-start.1 = ((f32[16,5,640]{2,1,0:T(8,128)}), f32[16,5,640]{2,1,0:T(8,128)S(1)}, u32[]{:S(2)}, u32[]{:S(2)}) async-start(f32[16,5,640]{2,1,0:T(8,128)} %reshape.15), calls=%async_computation.1 | async-start | bytes 655360 | tf_op jit(solution)/shard_map/all_to_all | solution.py:399
  160.2 0.0 collective-permute-done.9.a
  160.2 0.0 copy-start.1
  160.2 0.0 collective-permute-done.10.b
  160.2 0.0 collective-permute-done.11.got
  160.2 0.9 copy-done.1
  161.1 4.7 %sum_and_turn.1 = (bf16[512,640]{1,0:T(8,128)(2,1)}, bf16[512,640]{1,0:T(8,128)(2,1)}, bf16[512,640]{1,0:T(8,128)(2,1)}) custom-call(s32[3]{0:T(128)} %pad_add_fusion.scal, bf16[1,320,512]{2,1,0:T(8,128)(2,1)} %get-tuple-element.48.dq, f32[2,320,512]{2,1,0:T(8,128)} %get-tuple-element.49.mid, f32[2,320,512]{2,1,0:T(8,128)} %get-tuple-element.50.rest, ...), custom_call_target="tpu_custom_call" | custom-call | flops 4600000000 | bytes 400000 | tf_op jit(solution)/shard_map/sum_and_turn/pallas_call | solution.py:302
  165.8 5.1 %all-to-all-done.1 = f32[16,5,640]{2,1,0:T(8,128)S(1)} async-done(((f32[16,5,640]{2,1,0:T(8,128)}), f32[16,5,640]{2,1,0:T(8,128)S(1)}, u32[]{:S(2)}, u32[]{:S(2)}) %all-to-all-start.1) | async-done | bytes 204832 | tf_op jit(solution)/shard_map/all_to_all | solution.py:399
  170.8 0.6 reduce_sum.19
  (5 shorter events, 0.0 us)
Async XLA Ops:
  5.0 17.8 %collective-permute-start.2 = (bf16[2,320,512]{2,1,0:T(8,128)(2,1)}, bf16[2,320,512]{2,1,0:T(8,128)(2,1)S(1)}, u32[]{:S(2)}, u32[]{:S(2)}) collective-permute-start(bf16[2,320,512]{2,1,0:T(8,128)(2,1)} %get-tuple-element.35), channel_id=1, source_target_pairs={{0,1},{1,0},{2,3},{3,2},{4,5},{5,4},{6,7},{7,6},{8,9},{9,8},{10,11... | collective-permute-start | bytes 1966088 | tf_op jit(solution)/shard_map/ppermute | solution.py:355
  5.9 26.0 %collective-permute-start.6 = (bf16[2,320,512]{2,1,0:T(8,128)(2,1)}, bf16[2,320,512]{2,1,0:T(8,128)(2,1)}, u32[]{:S(2)}, u32[]{:S(2)}) collective-permute-start(bf16[2,320,512]{2,1,0:T(8,128)(2,1)} %get-tuple-element.36.refs_0_.refs_3_), channel_id=1, source_target_pairs={{0,2},{2,4},{3,1},{4,6},{5,3},{6,8},{7,5},{8,10},{9,7},{10,12},{11... | collective-permute-start | bytes 1966088 | tf_op jit(solution)/shard_map/ppermute | solution.py:358
  7.9 24.0 %collective-permute-start.5 = (bf16[2,320,512]{2,1,0:T(8,128)(2,1)}, bf16[2,320,512]{2,1,0:T(8,128)(2,1)}, u32[]{:S(2)}, u32[]{:S(2)}) collective-permute-start(bf16[2,320,512]{2,1,0:T(8,128)(2,1)} %get-tuple-element.36.refs_0_.refs_3_), channel_id=1, source_target_pairs={{1,3},{2,0},{3,5},{4,2},{5,7},{6,4},{7,9},{8,6},{9,11},{10,8},{11,... | collective-permute-start | bytes 1966088 | tf_op jit(solution)/shard_map/ppermute | solution.py:361
  11.7 18.2 %collective-permute-start = (bf16[1,320,512]{2,1,0:T(8,128)(2,1)}, bf16[1,320,512]{2,1,0:T(8,128)(2,1)S(1)}, u32[]{:S(2)}, u32[]{:S(2)}) collective-permute-start(bf16[1,320,512]{2,1,0:T(8,128)(2,1)} %get-tuple-element.32), channel_id=1, source_target_pairs={{0,1},{1,0},{2,3},{3,2},{4,5},{5,4},{6,7},{7,6},{8,9},{9,8},{10,11... | collective-permute-start | bytes 983048 | tf_op jit(solution)/shard_map/ppermute | solution.py:355
  18.7 56.6 %collective-permute-start.1 = (bf16[1,320,512]{2,1,0:T(8,128)(2,1)}, bf16[1,320,512]{2,1,0:T(8,128)(2,1)}, u32[]{:S(2)}, u32[]{:S(2)}) collective-permute-start(bf16[1,320,512]{2,1,0:T(8,128)(2,1)} %get-tuple-element.34), channel_id=1, source_target_pairs={{0,1},{1,0},{2,3},{3,2},{4,5},{5,4},{6,7},{7,6},{8,9},{9,8},{10,11... | collective-permute-start | bytes 983048 | tf_op jit(solution)/shard_map/ppermute | solution.py:355
  22.9 9.1 %copy-start = (bf16[2,320,512]{2,1,0:T(8,128)(2,1)}, bf16[2,320,512]{2,1,0:T(8,128)(2,1)S(1)}, u32[]{:S(2)}) copy-start(bf16[2,320,512]{2,1,0:T(8,128)(2,1)S(1)} %collective-permute-done.2.refs_1_.refs_0_) | copy-start | bytes 1966084
  22.9 37.4 %collective-permute-start.4 = (bf16[2,320,512]{2,1,0:T(8,128)(2,1)S(1)}, bf16[2,320,512]{2,1,0:T(8,128)(2,1)}, u32[]{:S(2)}, u32[]{:S(2)}) collective-permute-start(bf16[2,320,512]{2,1,0:T(8,128)(2,1)S(1)} %collective-permute-done.2.refs_1_.refs_0_), channel_id=1, source_target_pairs={{1,3},{2,0},{3,5},{4,2},{5,7},{6,4},{7,9},{8,6},{9,11},{10,8},{11,... | collective-permute-start | bytes 1966088 | tf_op jit(solution)/shard_map/ppermute | solution.py:361
  29.9 2.0 %copy-start.3 = (bf16[1,320,512]{2,1,0:T(8,128)(2,1)}, bf16[1,320,512]{2,1,0:T(8,128)(2,1)S(1)}, u32[]{:S(2)}) copy-start(bf16[1,320,512]{2,1,0:T(8,128)(2,1)S(1)} %collective-permute-done.qp) | copy-start | bytes 983044
  29.9 30.3 %collective-permute-start.3 = (bf16[2,320,512]{2,1,0:T(8,128)(2,1)S(1)}, bf16[2,320,512]{2,1,0:T(8,128)(2,1)}, u32[]{:S(2)}, u32[]{:S(2)}) collective-permute-start(bf16[2,320,512]{2,1,0:T(8,128)(2,1)S(1)} %collective-permute-done.2.refs_1_.refs_0_), channel_id=1, source_target_pairs={{0,2},{2,4},{3,1},{4,6},{5,3},{6,8},{7,5},{8,10},{9,7},{10,12},{11... | collective-permute-start | bytes 1966088 | tf_op jit(solution)/shard_map/ppermute | solution.py:358
  73.8 20.2 %collective-permute-start.12 = (bf16[1,320,512]{2,1,0:T(8,128)(2,1)}, bf16[1,320,512]{2,1,0:T(8,128)(2,1)S(1)}, u32[]{:S(2)}, u32[]{:S(2)}) collective-permute-start(bf16[1,320,512]{2,1,0:T(8,128)(2,1)} %get-tuple-element.41.op), channel_id=1, source_target_pairs={{0,1},{1,0},{2,3},{3,2},{4,5},{5,4},{6,7},{7,6},{8,9},{9,8},{10,11... | collective-permute-start | bytes 983048 | tf_op jit(solution)/shard_map/ppermute | solution.py:355
  88.1 21.3 %collective-permute-start.7 = (bf16[2,320,512]{2,1,0:T(8,128)(2,1)}, bf16[2,320,512]{2,1,0:T(8,128)(2,1)S(1)}, u32[]{:S(2)}, u32[]{:S(2)}) collective-permute-start(bf16[2,320,512]{2,1,0:T(8,128)(2,1)} %get-tuple-element.45), channel_id=1, source_target_pairs={{1,3},{2,0},{3,5},{4,2},{5,7},{6,4},{7,9},{8,6},{9,11},{10,8},{11,... | collective-permute-start | bytes 1966088 | tf_op jit(solution)/shard_map/ppermute | solution.py:361
  90.5 18.9 %collective-permute-start.8 = (bf16[2,320,512]{2,1,0:T(8,128)(2,1)}, bf16[2,320,512]{2,1,0:T(8,128)(2,1)}, u32[]{:S(2)}, u32[]{:S(2)}) collective-permute-start(bf16[2,320,512]{2,1,0:T(8,128)(2,1)} %get-tuple-element.46), channel_id=1, source_target_pairs={{0,2},{2,4},{3,1},{4,6},{5,3},{6,8},{7,5},{8,10},{9,7},{10,12},{11... | collective-permute-start | bytes 1966088 | tf_op jit(solution)/shard_map/ppermute | solution.py:358
  94.0 0.7 copy-start.4
  99.4 47.5 %all-to-all-start = ((bf16[16,80,640]{2,1,0:T(8,128)(2,1)}), bf16[16,80,640]{2,1,0:T(8,128)(2,1)}, u32[]{:S(2)}, u32[]{:S(2)}) async-start(bf16[16,80,640]{2,1,0:T(8,128)(2,1)} %bitcast.11), calls=%async_computation | async-start | bytes 3276800 | tf_op jit(solution)/shard_map/all_to_all | solution.py:396
  109.4 0.8 copy-start.2
  133.1 27.1 %collective-permute-start.11 = (bf16[3,320,512]{2,1,0:T(8,128)(2,1)}, bf16[3,320,512]{2,1,0:T(8,128)(2,1)}, u32[]{:S(2)}, u32[]{:S(2)}) collective-permute-start(bf16[3,320,512]{2,1,0:T(8,128)(2,1)} %get-tuple-element.53), channel_id=1, source_target_pairs={{0,1},{1,0},{2,3},{3,2},{4,5},{5,4},{6,7},{7,6},{8,9},{9,8},{10,11... | collective-permute-start | bytes 2949128 | tf_op jit(solution)/shard_map/ppermute | solution.py:355
  133.2 27.0 %collective-permute-start.9 = (bf16[2,320,512]{2,1,0:T(8,128)(2,1)}, bf16[2,320,512]{2,1,0:T(8,128)(2,1)S(1)}, u32[]{:S(2)}, u32[]{:S(2)}) collective-permute-start(bf16[2,320,512]{2,1,0:T(8,128)(2,1)} %get-tuple-element.51), channel_id=1, source_target_pairs={{1,3},{2,0},{3,5},{4,2},{5,7},{6,4},{7,9},{8,6},{9,11},{10,8},{11,... | collective-permute-start | bytes 1966088 | tf_op jit(solution)/shard_map/ppermute | solution.py:361
  137.1 23.1 %collective-permute-start.10 = (bf16[2,320,512]{2,1,0:T(8,128)(2,1)}, bf16[2,320,512]{2,1,0:T(8,128)(2,1)}, u32[]{:S(2)}, u32[]{:S(2)}) collective-permute-start(bf16[2,320,512]{2,1,0:T(8,128)(2,1)} %get-tuple-element.52), channel_id=1, source_target_pairs={{0,2},{2,4},{3,1},{4,6},{5,3},{6,8},{7,5},{8,10},{9,7},{10,12},{11... | collective-permute-start | bytes 1966088 | tf_op jit(solution)/shard_map/ppermute | solution.py:358
  149.3 21.5 %all-to-all-start.1 = ((f32[16,5,640]{2,1,0:T(8,128)}), f32[16,5,640]{2,1,0:T(8,128)S(1)}, u32[]{:S(2)}, u32[]{:S(2)}) async-start(f32[16,5,640]{2,1,0:T(8,128)} %reshape.15), calls=%async_computation.1 | async-start | bytes 655360 | tf_op jit(solution)/shard_map/all_to_all | solution.py:399
  160.2 0.9 copy-start.1

commit v6 on v5

--- a/solution.py
+++ b/solution.py
@@ -25,7 +25,7 @@
 
 def params(us):
     return dict(
-        compiler_params=pltpu.CompilerParams(vmem_limit_bytes=63 * 2**20),
+        compiler_params=pltpu.CompilerParams(vmem_limit_bytes=2**26 - 2**17),
         cost_estimate=pl.CostEstimate(
             flops=int(us * 1.15e9), bytes_accessed=int(us * 1e5), transcendentals=0
         ),
@@ -366,6 +366,7 @@
     a_mine, b_mine = to_a(kv_mine), to_b(kv_mine)
     q_got = swap(q_send)
     g_mine, g_send, dy_turned = attention_grad(scal, dy, out_proj)
+    g_send, q_got = lax.optimization_barrier((g_send, q_got))
     g_got = swap(g_send)
     a_got, b_got = to_a(kv_got), to_b(kv_got)
     kv = (a_mine, a_got, kv_mine, kv_got, b_mine, b_got)
@@ -399,6 +400,7 @@
     term = lax.all_to_all(term, "ctx", 0, 0)
     proj = jnp.sum(term, axis=0)
 
+    proj, dq = lax.optimization_barrier((proj, dq))
     gq, gk, gv = finish(scal, dq, mid, rest, back_a, back_b, got)
     return gq[None], gk[None], gv[None], proj
 

time: 175 us -> 179 us (1.023)
  the two profiles are of different devices: /device:TPU:38 before, /device:TPU:32 now
where the time goes in v6:
time: 179 us; the launch traced here: 178 us
  Pallas kernels  100 us (56%)
  starting transfers between devices  54.1 us (30%)
  waiting for transfers between devices  18.5 us (10%)
  other arithmetic  3.9 us (2%)
    pallas_call x3, Pallas kernels, backward(): pl.pallas_call(functools.partial(backward_kernel, js, pairs, stage), grid...  43.3 us
    pallas_call x2, Pallas kernels, forward(): pl.pallas_call(functools.partial(forward_kernel, js, bool(given), last),...  39 us
    ppermute x4, starting transfers between devices, to_a(): return lax.ppermute(x, 'ctx', step_a)  16.6 us
    ppermute x5, waiting for transfers between devices, swap(): return lax.ppermute(x, 'ctx', swap_pairs)  10.7 us
    all_to_all x1, starting transfers between devices, shards(): term = lax.all_to_all(term.reshape(dps, -1, term.shape[1]), 'dp', 0, 0)  10.6 us
    all_to_all x1, starting transfers between devices, shards(): term = lax.all_to_all(term, 'ctx', 0, 0)  10.3 us
    ppermute x4, starting transfers between devices, to_b(): return lax.ppermute(x, 'ctx', step_b)  9.3 us
    all_to_all x1, waiting for transfers between devices, shards(): term = lax.all_to_all(term, 'ctx', 0, 0)  7.8 us
  transfers between devices with their start and end apart: 15, of which 2 were waited for; matrix products, arithmetic and copies ran while one was open for 2% of the time, Pallas kernels for 51%

profile of v6, /device:TPU:32, one launch (start us, length us, event | category | flops | bytes accessed | tf_op | source)
XLA Modules:
  0.0 178.3 jit_solution(4428788743005372046)
XLA Ops:
  0.6 0.6 pad_add_fusion.scal
  1.3 3.8 %split_kvq.1 = (bf16[2,320,512]{2,1,0:T(8,128)(2,1)}, bf16[2,320,512]{2,1,0:T(8,128)(2,1)}, bf16[1,320,512]{2,1,0:T(8,128)(2,1)}, bf16[1,320,512]{2,1,0:T(8,128)(2,1)}) custom-call(s32[3]{0:T(128)} %pad_add_fusion.scal, bf16[512,640]{1,0:T(8,128)(2,1)} %bitcast.13, bf16[512,640]{1,0:T(8,128)(2,1)} %bitcast.14, bf16[512,640]{1,0:T(8,128)(2,1)} %bitcast.15), custom_call_target="tpu_custom_call" | custom-call | flops 4600000000 | bytes 400000 | tf_op jit(solution)/shard_map/split_kvq/pallas_call | solution.py:72
  5.1 1.5 collective-permute-start.1
  6.6 3.8 %collective-permute-start.5 = (bf16[2,320,512]{2,1,0:T(8,128)(2,1)}, bf16[2,320,512]{2,1,0:T(8,128)(2,1)}, u32[]{:S(2)}, u32[]{:S(2)}) collective-permute-start(bf16[2,320,512]{2,1,0:T(8,128)(2,1)} %get-tuple-element.40.refs_0_.refs_3_), channel_id=1, source_target_pairs={{0,2},{2,4},{3,1},{4,6},{5,3},{6,8},{7,5},{8,10},{9,7},{10,12},{11... | collective-permute-start | bytes 1966088 | tf_op jit(solution)/shard_map/ppermute | solution.py:358
  10.4 2.8 %collective-permute-start.4 = (bf16[2,320,512]{2,1,0:T(8,128)(2,1)}, bf16[2,320,512]{2,1,0:T(8,128)(2,1)}, u32[]{:S(2)}, u32[]{:S(2)}) collective-permute-start(bf16[2,320,512]{2,1,0:T(8,128)(2,1)} %get-tuple-element.40.refs_0_.refs_3_), channel_id=1, source_target_pairs={{1,3},{2,0},{3,5},{4,2},{5,7},{6,4},{7,9},{8,6},{9,11},{10,8},{11,... | collective-permute-start | bytes 1966088 | tf_op jit(solution)/shard_map/ppermute | solution.py:361
  13.2 0.1 collective-permute-start
  13.3 4.9 %attention_grad.1 = (bf16[1,320,512]{2,1,0:T(8,128)(2,1)}, bf16[1,320,512]{2,1,0:T(8,128)(2,1)}, bf16[1280,512]{1,0:T(8,128)(2,1)}) custom-call(s32[3]{0:T(128)} %pad_add_fusion.scal, bf16[512,1280]{1,0:T(8,128)(2,1)} %bitcast.12, bf16[640,1280]{1,0:T(8,128)(2,1)} %w_ref.1), custom_call_target="tpu_custom_call" | custom-call | flops 4600000000 | bytes 400000 | tf_op jit(solution)/shard_map/attention_grad/pallas_call | solution.py:95
  18.2 10.7 %collective-permute-done.qp = bf16[1,320,512]{2,1,0:T(8,128)(2,1)} collective-permute-done((bf16[1,320,512]{2,1,0:T(8,128)(2,1)}, bf16[1,320,512]{2,1,0:T(8,128)(2,1)}, u32[]{:S(2)}, u32[]{:S(2)}) %collective-permute-start) | collective-permute-done | bytes 327712 | tf_op jit(solution)/shard_map/ppermute | solution.py:355
  28.9 1.5 collective-permute-start.7
  30.4 0.0 collective-permute-done.1.refs_1_.refs_0_
  30.4 2.0 %collective-permute-start.3 = (bf16[2,320,512]{2,1,0:T(8,128)(2,1)}, bf16[2,320,512]{2,1,0:T(8,128)(2,1)}, u32[]{:S(2)}, u32[]{:S(2)}) collective-permute-start(bf16[2,320,512]{2,1,0:T(8,128)(2,1)} %collective-permute-done.1.refs_1_.refs_0_), channel_id=1, source_target_pairs={{1,3},{2,0},{3,5},{4,2},{5,7},{6,4},{7,9},{8,6},{9,11},{10,8},{11,... | collective-permute-start | bytes 1966088 | tf_op jit(solution)/shard_map/ppermute | solution.py:361
  32.4 3.8 %collective-permute-start.2 = (bf16[2,320,512]{2,1,0:T(8,128)(2,1)}, bf16[2,320,512]{2,1,0:T(8,128)(2,1)}, u32[]{:S(2)}, u32[]{:S(2)}) collective-permute-start(bf16[2,320,512]{2,1,0:T(8,128)(2,1)} %collective-permute-done.1.refs_1_.refs_0_), channel_id=1, source_target_pairs={{0,2},{2,4},{3,1},{4,6},{5,3},{6,8},{7,5},{8,10},{9,7},{10,12},{11... | collective-permute-start | bytes 1966088 | tf_op jit(solution)/shard_map/ppermute | solution.py:358
  36.2 0.0 collective-permute-done.5.refs_3_.refs_1_
  36.2 0.0 collective-permute-done.4.refs_2_
  36.3 28.3 %forward_2340.1 = (f32[1,320,512]{2,1,0:T(8,128)}, f32[1,320,512]{2,1,0:T(8,128)}, f32[5,4,512]{2,1,0:T(4,128)}) custom-call(s32[3]{0:T(128)} %pad_add_fusion.scal, bf16[1,320,512]{2,1,0:T(8,128)(2,1)} %get-tuple-element.35.qm, bf16[1,320,512]{2,1,0:T(8,128)(2,1)} %collective-permute-done.qp, bf16[2,320,512]{2,1,0:T(8,128)(2,1)} %get-tuple-element.40.refs_0_.refs_3_, ...), custom_call_target="tpu_custom_call" | custom-call | flops 18400000000 | bytes 1600000 | tf_op jit(solution)/shard_map/forward_2340/pallas_call | solution.py:192
  64.5 0.0 collective-permute-done.3.refs_1_
  64.5 0.0 collective-permute-done.2.refs_0_
  64.5 10.7 %forward_15.1 = (bf16[1,320,512]{2,1,0:T(8,128)(2,1)}, bf16[1,320,512]{2,1,0:T(8,128)(2,1)}, f32[5,2,512]{2,1,0:T(2,128)}) custom-call(s32[3]{0:T(128)} %pad_add_fusion.scal, bf16[1,320,512]{2,1,0:T(8,128)(2,1)} %get-tuple-element.35.qm, bf16[1,320,512]{2,1,0:T(8,128)(2,1)} %collective-permute-done.qp, bf16[2,320,512]{2,1,0:T(8,128)(2,1)} %collective-permute-done.2.refs_0_, ...), custom_call_target="tpu_custom_call" | custom-call | flops 9200000000 | bytes 800000 | tf_op jit(solution)/shard_map/forward_15/pallas_call | solution.py:192
  75.2 0.4 collective-permute-start.6
  75.6 0.0 collective-permute-done.7.gp
  75.6 12.8 %backward_15.1 = (bf16[2,320,512]{2,1,0:T(8,128)(2,1)}, bf16[2,320,512]{2,1,0:T(8,128)(2,1)}, f32[1,320,512]{2,1,0:T(8,128)}, f32[1,320,512]{2,1,0:T(8,128)}) custom-call(s32[3]{0:T(128)} %pad_add_fusion.scal, bf16[1,320,512]{2,1,0:T(8,128)(2,1)} %get-tuple-element.35.qm, bf16[1,320,512]{2,1,0:T(8,128)(2,1)} %collective-permute-done.qp, ...), custom_call_target="tpu_custom_call" | custom-call | flops 14949999616 | bytes 1300000 | tf_op jit(solution)/shard_map/backward_15/pallas_call | solution.py:274
  88.4 2.5 %collective-permute-start.8 = (bf16[2,320,512]{2,1,0:T(8,128)(2,1)}, bf16[2,320,512]{2,1,0:T(8,128)(2,1)}, u32[]{:S(2)}, u32[]{:S(2)}) collective-permute-start(bf16[2,320,512]{2,1,0:T(8,128)(2,1)} %get-tuple-element.52), channel_id=1, source_target_pairs={{1,3},{2,0},{3,5},{4,2},{5,7},{6,4},{7,9},{8,6},{9,11},{10,8},{11,... | collective-permute-start | bytes 1966088 | tf_op jit(solution)/shard_map/ppermute | solution.py:361
  91.0 5.1 %collective-permute-start.9 = (bf16[2,320,512]{2,1,0:T(8,128)(2,1)}, bf16[2,320,512]{2,1,0:T(8,128)(2,1)}, u32[]{:S(2)}, u32[]{:S(2)}) collective-permute-start(bf16[2,320,512]{2,1,0:T(8,128)(2,1)} %get-tuple-element.53), channel_id=1, source_target_pairs={{0,2},{2,4},{3,1},{4,6},{5,3},{6,8},{7,5},{8,10},{9,7},{10,12},{11... | collective-permute-start | bytes 1966088 | tf_op jit(solution)/shard_map/ppermute | solution.py:358
  96.1 0.0 collective-permute-done.6.o_got
  96.1 4.6 %projection_term.1 = bf16[1280,640]{1,0:T(8,128)(2,1)} custom-call(s32[3]{0:T(128)} %pad_add_fusion.scal, bf16[1,320,512]{2,1,0:T(8,128)(2,1)} %get-tuple-element.44.o.om, bf16[1,320,512]{2,1,0:T(8,128)(2,1)} %collective-permute-done.6.o_got, bf16[1280,512]{1,0:T(8,128)(2,1)} %get-tuple-element.46.dy_turned), custom_call_target="tpu_custom_call" | custom-call | flops 4600000000 | bytes 400000 | tf_op jit(solution)/shard_map/projection_term/pallas_call | solution.py:325
  100.7 10.6 %all-to-all-start = ((bf16[16,80,640]{2,1,0:T(8,128)(2,1)}), bf16[16,80,640]{2,1,0:T(8,128)(2,1)}, u32[]{:S(2)}, u32[]{:S(2)}) async-start(bf16[16,80,640]{2,1,0:T(8,128)(2,1)} %bitcast.11), calls=%async_computation | async-start | bytes 3276800 | tf_op jit(solution)/shard_map/all_to_all | solution.py:397
  111.2 0.0 collective-permute-done.8.refs_6_
  111.3 0.0 collective-permute-done.9.refs_7_
  111.3 22.8 %backward_3042.1 = (bf16[3,320,512]{2,1,0:T(8,128)(2,1)}, bf16[2,320,512]{2,1,0:T(8,128)(2,1)}, bf16[2,320,512]{2,1,0:T(8,128)(2,1)}, f32[2,320,512]{2,1,0:T(8,128)}, f32[1,320,512]{2,1,0:T(8,128)}) custom-call(s32[3]{0:T(128)} %pad_add_fusion.scal, bf16[1,320,512]{2,1,0:T(8,128)(2,1)} %get-tuple-element.35.qm, ...), custom_call_target="tpu_custom_call" | custom-call | flops 27599998976 | bytes 2400000 | tf_op jit(solution)/shard_map/backward_3042/pallas_call | solution.py:274
  134.1 3.9 %collective-permute-start.12 = (bf16[3,320,512]{2,1,0:T(8,128)(2,1)}, bf16[3,320,512]{2,1,0:T(8,128)(2,1)}, u32[]{:S(2)}, u32[]{:S(2)}) collective-permute-start(bf16[3,320,512]{2,1,0:T(8,128)(2,1)} %get-tuple-element.61), channel_id=1, source_target_pairs={{0,1},{1,0},{2,3},{3,2},{4,5},{5,4},{6,7},{7,6},{8,9},{9,8},{10,11... | collective-permute-start | bytes 2949128 | tf_op jit(solution)/shard_map/ppermute | solution.py:355
  137.9 1.9 %collective-permute-start.10 = (bf16[2,320,512]{2,1,0:T(8,128)(2,1)}, bf16[2,320,512]{2,1,0:T(8,128)(2,1)}, u32[]{:S(2)}, u32[]{:S(2)}) collective-permute-start(bf16[2,320,512]{2,1,0:T(8,128)(2,1)} %get-tuple-element.59), channel_id=1, source_target_pairs={{1,3},{2,0},{3,5},{4,2},{5,7},{6,4},{7,9},{8,6},{9,11},{10,8},{11,... | collective-permute-start | bytes 1966088 | tf_op jit(solution)/shard_map/ppermute | solution.py:361
  139.8 3.9 %collective-permute-start.11 = (bf16[2,320,512]{2,1,0:T(8,128)(2,1)}, bf16[2,320,512]{2,1,0:T(8,128)(2,1)}, u32[]{:S(2)}, u32[]{:S(2)}) collective-permute-start(bf16[2,320,512]{2,1,0:T(8,128)(2,1)} %get-tuple-element.60), channel_id=1, source_target_pairs={{0,2},{2,4},{3,1},{4,6},{5,3},{6,8},{7,5},{8,10},{9,7},{10,12},{11... | collective-permute-start | bytes 1966088 | tf_op jit(solution)/shard_map/ppermute | solution.py:358
  143.8 0.0 all-to-all-done
  143.8 1.7 convert_reduce_fusion
  145.5 0.8 reshape.15
  146.2 10.3 %all-to-all-start.1 = ((f32[16,5,640]{2,1,0:T(8,128)}), f32[16,5,640]{2,1,0:T(8,128)}, u32[]{:S(2)}, u32[]{:S(2)}) async-start(f32[16,5,640]{2,1,0:T(8,128)} %reshape.15), calls=%async_computation.1 | async-start | bytes 655360 | tf_op jit(solution)/shard_map/all_to_all | solution.py:400
  156.5 7.7 %backward_2.1 = (f32[2,320,512]{2,1,0:T(8,128)}, bf16[1,320,512]{2,1,0:T(8,128)(2,1)}) custom-call(s32[3]{0:T(128)} %pad_add_fusion.scal, bf16[1,320,512]{2,1,0:T(8,128)(2,1)} %get-tuple-element.35.qm, bf16[1,320,512]{2,1,0:T(8,128)(2,1)} %collective-permute-done.qp, bf16[1,320,512]{2,1,0:T(8,128)(2,1)} %get-tuple-element.47.gm, ...), custom_call_target="tpu_custom_call" | custom-call | flops 8049999872 | bytes 700000 | tf_op jit(solution)/shard_map/backward_2/pallas_call | solution.py:274
  164.2 7.8 %all-to-all-done.1 = f32[16,5,640]{2,1,0:T(8,128)} async-done(((f32[16,5,640]{2,1,0:T(8,128)}), f32[16,5,640]{2,1,0:T(8,128)}, u32[]{:S(2)}, u32[]{:S(2)}) %all-to-all-start.1) | async-done | bytes 204832 | tf_op jit(solution)/shard_map/all_to_all | solution.py:400
  172.0 1.6 reduce_sum.19
  173.6 0.0 collective-permute-done.10.a
  173.6 0.0 collective-permute-done.11.b
  173.6 0.0 collective-permute-done.12.got
  173.6 4.7 %sum_and_turn.1 = (bf16[512,640]{1,0:T(8,128)(2,1)}, bf16[512,640]{1,0:T(8,128)(2,1)}, bf16[512,640]{1,0:T(8,128)(2,1)}) custom-call(s32[3]{0:T(128)} %pad_add_fusion.scal, bf16[1,320,512]{2,1,0:T(8,128)(2,1)} %get-tuple-element.56.dq, f32[2,320,512]{2,1,0:T(8,128)} %get-tuple-element.57.mid, f32[2,320,512]{2,1,0:T(8,128)} %get-tuple-element.58.rest, ...), custom_call_target="tpu_custom_call" | custom-call | flops 4600000000 | bytes 400000 | tf_op jit(solution)/shard_map/sum_and_turn/pallas_call | solution.py:302
Async XLA Ops:
  5.1 25.3 %collective-permute-start.1 = (bf16[2,320,512]{2,1,0:T(8,128)(2,1)}, bf16[2,320,512]{2,1,0:T(8,128)(2,1)}, u32[]{:S(2)}, u32[]{:S(2)}) collective-permute-start(bf16[2,320,512]{2,1,0:T(8,128)(2,1)} %get-tuple-element.39), channel_id=1, source_target_pairs={{0,1},{1,0},{2,3},{3,2},{4,5},{5,4},{6,7},{7,6},{8,9},{9,8},{10,11... | collective-permute-start | bytes 1966088 | tf_op jit(solution)/shard_map/ppermute | solution.py:355
  6.6 29.7 %collective-permute-start.5 = (bf16[2,320,512]{2,1,0:T(8,128)(2,1)}, bf16[2,320,512]{2,1,0:T(8,128)(2,1)}, u32[]{:S(2)}, u32[]{:S(2)}) collective-permute-start(bf16[2,320,512]{2,1,0:T(8,128)(2,1)} %get-tuple-element.40.refs_0_.refs_3_), channel_id=1, source_target_pairs={{0,2},{2,4},{3,1},{4,6},{5,3},{6,8},{7,5},{8,10},{9,7},{10,12},{11... | collective-permute-start | bytes 1966088 | tf_op jit(solution)/shard_map/ppermute | solution.py:358
  10.4 25.9 %collective-permute-start.4 = (bf16[2,320,512]{2,1,0:T(8,128)(2,1)}, bf16[2,320,512]{2,1,0:T(8,128)(2,1)}, u32[]{:S(2)}, u32[]{:S(2)}) collective-permute-start(bf16[2,320,512]{2,1,0:T(8,128)(2,1)} %get-tuple-element.40.refs_0_.refs_3_), channel_id=1, source_target_pairs={{1,3},{2,0},{3,5},{4,2},{5,7},{6,4},{7,9},{8,6},{9,11},{10,8},{11,... | collective-permute-start | bytes 1966088 | tf_op jit(solution)/shard_map/ppermute | solution.py:361
  13.2 15.6 %collective-permute-start = (bf16[1,320,512]{2,1,0:T(8,128)(2,1)}, bf16[1,320,512]{2,1,0:T(8,128)(2,1)}, u32[]{:S(2)}, u32[]{:S(2)}) collective-permute-start(bf16[1,320,512]{2,1,0:T(8,128)(2,1)} %get-tuple-element.37), channel_id=1, source_target_pairs={{0,1},{1,0},{2,3},{3,2},{4,5},{5,4},{6,7},{7,6},{8,9},{9,8},{10,11... | collective-permute-start | bytes 983048 | tf_op jit(solution)/shard_map/ppermute | solution.py:355
  28.9 46.7 %collective-permute-start.7 = (bf16[1,320,512]{2,1,0:T(8,128)(2,1)}, bf16[1,320,512]{2,1,0:T(8,128)(2,1)}, u32[]{:S(2)}, u32[]{:S(2)}) collective-permute-start(bf16[1,320,512]{2,1,0:T(8,128)(2,1)} %get-tuple-element.48), channel_id=1, source_target_pairs={{0,1},{1,0},{2,3},{3,2},{4,5},{5,4},{6,7},{7,6},{8,9},{9,8},{10,11... | collective-permute-start | bytes 983048 | tf_op jit(solution)/shard_map/ppermute | solution.py:355
  30.4 34.2 %collective-permute-start.3 = (bf16[2,320,512]{2,1,0:T(8,128)(2,1)}, bf16[2,320,512]{2,1,0:T(8,128)(2,1)}, u32[]{:S(2)}, u32[]{:S(2)}) collective-permute-start(bf16[2,320,512]{2,1,0:T(8,128)(2,1)} %collective-permute-done.1.refs_1_.refs_0_), channel_id=1, source_target_pairs={{1,3},{2,0},{3,5},{4,2},{5,7},{6,4},{7,9},{8,6},{9,11},{10,8},{11,... | collective-permute-start | bytes 1966088 | tf_op jit(solution)/shard_map/ppermute | solution.py:361
  32.4 32.1 %collective-permute-start.2 = (bf16[2,320,512]{2,1,0:T(8,128)(2,1)}, bf16[2,320,512]{2,1,0:T(8,128)(2,1)}, u32[]{:S(2)}, u32[]{:S(2)}) collective-permute-start(bf16[2,320,512]{2,1,0:T(8,128)(2,1)} %collective-permute-done.1.refs_1_.refs_0_), channel_id=1, source_target_pairs={{0,2},{2,4},{3,1},{4,6},{5,3},{6,8},{7,5},{8,10},{9,7},{10,12},{11... | collective-permute-start | bytes 1966088 | tf_op jit(solution)/shard_map/ppermute | solution.py:358
  75.2 20.8 %collective-permute-start.6 = (bf16[1,320,512]{2,1,0:T(8,128)(2,1)}, bf16[1,320,512]{2,1,0:T(8,128)(2,1)}, u32[]{:S(2)}, u32[]{:S(2)}) collective-permute-start(bf16[1,320,512]{2,1,0:T(8,128)(2,1)} %get-tuple-element.45.op), channel_id=1, source_target_pairs={{0,1},{1,0},{2,3},{3,2},{4,5},{5,4},{6,7},{7,6},{8,9},{9,8},{10,11... | collective-permute-start | bytes 983048 | tf_op jit(solution)/shard_map/ppermute | solution.py:355
  88.4 22.8 %collective-permute-start.8 = (bf16[2,320,512]{2,1,0:T(8,128)(2,1)}, bf16[2,320,512]{2,1,0:T(8,128)(2,1)}, u32[]{:S(2)}, u32[]{:S(2)}) collective-permute-start(bf16[2,320,512]{2,1,0:T(8,128)(2,1)} %get-tuple-element.52), channel_id=1, source_target_pairs={{1,3},{2,0},{3,5},{4,2},{5,7},{6,4},{7,9},{8,6},{9,11},{10,8},{11,... | collective-permute-start | bytes 1966088 | tf_op jit(solution)/shard_map/ppermute | solution.py:361
  91.0 20.3 %collective-permute-start.9 = (bf16[2,320,512]{2,1,0:T(8,128)(2,1)}, bf16[2,320,512]{2,1,0:T(8,128)(2,1)}, u32[]{:S(2)}, u32[]{:S(2)}) collective-permute-start(bf16[2,320,512]{2,1,0:T(8,128)(2,1)} %get-tuple-element.53), channel_id=1, source_target_pairs={{0,2},{2,4},{3,1},{4,6},{5,3},{6,8},{7,5},{8,10},{9,7},{10,12},{11... | collective-permute-start | bytes 1966088 | tf_op jit(solution)/shard_map/ppermute | solution.py:358
  100.7 43.1 %all-to-all-start = ((bf16[16,80,640]{2,1,0:T(8,128)(2,1)}), bf16[16,80,640]{2,1,0:T(8,128)(2,1)}, u32[]{:S(2)}, u32[]{:S(2)}) async-start(bf16[16,80,640]{2,1,0:T(8,128)(2,1)} %bitcast.11), calls=%async_computation | async-start | bytes 3276800 | tf_op jit(solution)/shard_map/all_to_all | solution.py:397
  134.1 39.6 %collective-permute-start.12 = (bf16[3,320,512]{2,1,0:T(8,128)(2,1)}, bf16[3,320,512]{2,1,0:T(8,128)(2,1)}, u32[]{:S(2)}, u32[]{:S(2)}) collective-permute-start(bf16[3,320,512]{2,1,0:T(8,128)(2,1)} %get-tuple-element.61), channel_id=1, source_target_pairs={{0,1},{1,0},{2,3},{3,2},{4,5},{5,4},{6,7},{7,6},{8,9},{9,8},{10,11... | collective-permute-start | bytes 2949128 | tf_op jit(solution)/shard_map/ppermute | solution.py:355
  137.9 35.7 %collective-permute-start.10 = (bf16[2,320,512]{2,1,0:T(8,128)(2,1)}, bf16[2,320,512]{2,1,0:T(8,128)(2,1)}, u32[]{:S(2)}, u32[]{:S(2)}) collective-permute-start(bf16[2,320,512]{2,1,0:T(8,128)(2,1)} %get-tuple-element.59), channel_id=1, source_target_pairs={{1,3},{2,0},{3,5},{4,2},{5,7},{6,4},{7,9},{8,6},{9,11},{10,8},{11,... | collective-permute-start | bytes 1966088 | tf_op jit(solution)/shard_map/ppermute | solution.py:361
  139.8 33.8 %collective-permute-start.11 = (bf16[2,320,512]{2,1,0:T(8,128)(2,1)}, bf16[2,320,512]{2,1,0:T(8,128)(2,1)}, u32[]{:S(2)}, u32[]{:S(2)}) collective-permute-start(bf16[2,320,512]{2,1,0:T(8,128)(2,1)} %get-tuple-element.60), channel_id=1, source_target_pairs={{0,2},{2,4},{3,1},{4,6},{5,3},{6,8},{7,5},{8,10},{9,7},{10,12},{11... | collective-permute-start | bytes 1966088 | tf_op jit(solution)/shard_map/ppermute | solution.py:358
  146.2 25.8 %all-to-all-start.1 = ((f32[16,5,640]{2,1,0:T(8,128)}), f32[16,5,640]{2,1,0:T(8,128)}, u32[]{:S(2)}, u32[]{:S(2)}) async-start(f32[16,5,640]{2,1,0:T(8,128)} %reshape.15), calls=%async_computation.1 | async-start | bytes 655360 | tf_op jit(solution)/shard_map/all_to_all | solution.py:400

commit v7 on v6

--- a/solution.py
+++ b/solution.py
@@ -311,7 +311,7 @@
         ),
         out_shape=[jax.ShapeDtypeStruct(out, BF16)] * 3,
         name="sum_and_turn",
-        **params(4),
+        **params(0.1),
     )(scal, dq, mid, rest, a, b, got)
 
 
@@ -366,7 +366,6 @@
     a_mine, b_mine = to_a(kv_mine), to_b(kv_mine)
     q_got = swap(q_send)
     g_mine, g_send, dy_turned = attention_grad(scal, dy, out_proj)
-    g_send, q_got = lax.optimization_barrier((g_send, q_got))
     g_got = swap(g_send)
     a_got, b_got = to_a(kv_got), to_b(kv_got)
     kv = (a_mine, a_got, kv_mine, kv_got, b_mine, b_got)
@@ -400,7 +399,6 @@
     term = lax.all_to_all(term, "ctx", 0, 0)
     proj = jnp.sum(term, axis=0)
 
-    proj, dq = lax.optimization_barrier((proj, dq))
     gq, gk, gv = finish(scal, dq, mid, rest, back_a, back_b, got)
     return gq[None], gk[None], gv[None], proj
 

time: 179 us -> 170 us (0.950)
  the two profiles are of different devices: /device:TPU:32 before, /device:TPU:38 now
where the time goes in v7:
time: 170 us; the launch traced here: 167 us
  Pallas kernels  97.5 us (57%)
  starting transfers between devices  51.8 us (30%)
  waiting for transfers between devices  11.8 us (7%)
  other arithmetic  3.9 us (2%)
    pallas_call x3, Pallas kernels, backward(): pl.pallas_call(functools.partial(backward_kernel, js, pairs, stage), grid...  43.3 us
    pallas_call x2, Pallas kernels, forward(): pl.pallas_call(functools.partial(forward_kernel, js, bool(given), last),...  36.3 us
    ppermute x4, starting transfers between devices, to_b(): return lax.ppermute(x, 'ctx', step_b)  21.6 us
    all_to_all x1, starting transfers between devices, shards(): term = lax.all_to_all(term, 'ctx', 0, 0)  9.01 us
    ppermute x4, starting transfers between devices, to_a(): return lax.ppermute(x, 'ctx', step_a)  7.86 us
    ppermute x5, waiting for transfers between devices, swap(): return lax.ppermute(x, 'ctx', swap_pairs)  7.48 us
    ppermute x5, starting transfers between devices, swap(): return lax.ppermute(x, 'ctx', swap_pairs)  7.37 us
    all_to_all x1, starting transfers between devices, shards(): term = lax.all_to_all(term.reshape(dps, -1, term.shape[1]), 'dp', 0, 0)  5.94 us
  transfers between devices with their start and end apart: 15, of which 5 were waited for; matrix products, arithmetic and copies ran while one was open for 1% of the time, Pallas kernels for 56%

profile of v7, /device:TPU:38, one launch (start us, length us, event | category | flops | bytes accessed | tf_op | source)
XLA Modules:
  0.0 166.5 jit_solution(15709567019376188088)
XLA Ops:
  0.6 0.6 pad_add_fusion.scal
  1.3 3.8 %split_kvq.1 = (bf16[2,320,512]{2,1,0:T(8,128)(2,1)}, bf16[2,320,512]{2,1,0:T(8,128)(2,1)}, bf16[1,320,512]{2,1,0:T(8,128)(2,1)}, bf16[1,320,512]{2,1,0:T(8,128)(2,1)}) custom-call(s32[3]{0:T(128)} %pad_add_fusion.scal, bf16[512,640]{1,0:T(8,128)(2,1)} %bitcast.13, bf16[512,640]{1,0:T(8,128)(2,1)} %bitcast.14, bf16[512,640]{1,0:T(8,128)(2,1)} %bitcast.15), custom_call_target="tpu_custom_call" | custom-call | flops 4600000000 | bytes 400000 | tf_op jit(solution)/shard_map/split_kvq/pallas_call | solution.py:72
  5.1 0.8 collective-permute-start.2
  5.9 2.0 %collective-permute-start.6 = (bf16[2,320,512]{2,1,0:T(8,128)(2,1)}, bf16[2,320,512]{2,1,0:T(8,128)(2,1)}, u32[]{:S(2)}, u32[]{:S(2)}) collective-permute-start(bf16[2,320,512]{2,1,0:T(8,128)(2,1)} %get-tuple-element.36.refs_0_.refs_3_), channel_id=1, source_target_pairs={{0,2},{2,4},{3,1},{4,6},{5,3},{6,8},{7,5},{8,10},{9,7},{10,12},{11... | collective-permute-start | bytes 1966088 | tf_op jit(solution)/shard_map/ppermute | solution.py:358
  7.9 3.8 %collective-permute-start.5 = (bf16[2,320,512]{2,1,0:T(8,128)(2,1)}, bf16[2,320,512]{2,1,0:T(8,128)(2,1)}, u32[]{:S(2)}, u32[]{:S(2)}) collective-permute-start(bf16[2,320,512]{2,1,0:T(8,128)(2,1)} %get-tuple-element.36.refs_0_.refs_3_), channel_id=1, source_target_pairs={{1,3},{2,0},{3,5},{4,2},{5,7},{6,4},{7,9},{8,6},{9,11},{10,8},{11,... | collective-permute-start | bytes 1966088 | tf_op jit(solution)/shard_map/ppermute | solution.py:361
  11.8 2.1 %collective-permute-start = (bf16[1,320,512]{2,1,0:T(8,128)(2,1)}, bf16[1,320,512]{2,1,0:T(8,128)(2,1)}, u32[]{:S(2)}, u32[]{:S(2)}) collective-permute-start(bf16[1,320,512]{2,1,0:T(8,128)(2,1)} %get-tuple-element.32), channel_id=1, source_target_pairs={{0,1},{1,0},{2,3},{3,2},{4,5},{5,4},{6,7},{7,6},{8,9},{9,8},{10,11... | collective-permute-start | bytes 983048 | tf_op jit(solution)/shard_map/ppermute | solution.py:355
  13.9 4.9 %attention_grad.1 = (bf16[1,320,512]{2,1,0:T(8,128)(2,1)}, bf16[1,320,512]{2,1,0:T(8,128)(2,1)}, bf16[1280,512]{1,0:T(8,128)(2,1)}) custom-call(s32[3]{0:T(128)} %pad_add_fusion.scal, bf16[512,1280]{1,0:T(8,128)(2,1)} %bitcast.12, bf16[640,1280]{1,0:T(8,128)(2,1)} %w_ref.1), custom_call_target="tpu_custom_call" | custom-call | flops 4600000000 | bytes 400000 | tf_op jit(solution)/shard_map/attention_grad/pallas_call | solution.py:95
  18.7 0.0 collective-permute-start.1
  18.7 4.3 %collective-permute-done.2.refs_1_.refs_0_ = bf16[2,320,512]{2,1,0:T(8,128)(2,1)} collective-permute-done((bf16[2,320,512]{2,1,0:T(8,128)(2,1)}, bf16[2,320,512]{2,1,0:T(8,128)(2,1)}, u32[]{:S(2)}, u32[]{:S(2)}) %collective-permute-start.2) | collective-permute-done | bytes 655392 | tf_op jit(solution)/shard_map/ppermute | solution.py:355
  23.0 3.8 %collective-permute-start.4 = (bf16[2,320,512]{2,1,0:T(8,128)(2,1)}, bf16[2,320,512]{2,1,0:T(8,128)(2,1)}, u32[]{:S(2)}, u32[]{:S(2)}) collective-permute-start(bf16[2,320,512]{2,1,0:T(8,128)(2,1)} %collective-permute-done.2.refs_1_.refs_0_), channel_id=1, source_target_pairs={{1,3},{2,0},{3,5},{4,2},{5,7},{6,4},{7,9},{8,6},{9,11},{10,8},{11,... | collective-permute-start | bytes 1966088 | tf_op jit(solution)/shard_map/ppermute | solution.py:361
  26.8 3.2 %collective-permute-done.qp = bf16[1,320,512]{2,1,0:T(8,128)(2,1)} collective-permute-done((bf16[1,320,512]{2,1,0:T(8,128)(2,1)}, bf16[1,320,512]{2,1,0:T(8,128)(2,1)}, u32[]{:S(2)}, u32[]{:S(2)}) %collective-permute-start) | collective-permute-done | bytes 327712 | tf_op jit(solution)/shard_map/ppermute | solution.py:355
  30.0 2.0 %collective-permute-start.3 = (bf16[2,320,512]{2,1,0:T(8,128)(2,1)}, bf16[2,320,512]{2,1,0:T(8,128)(2,1)}, u32[]{:S(2)}, u32[]{:S(2)}) collective-permute-start(bf16[2,320,512]{2,1,0:T(8,128)(2,1)} %collective-permute-done.2.refs_1_.refs_0_), channel_id=1, source_target_pairs={{0,2},{2,4},{3,1},{4,6},{5,3},{6,8},{7,5},{8,10},{9,7},{10,12},{11... | collective-permute-start | bytes 1966088 | tf_op jit(solution)/shard_map/ppermute | solution.py:358
  32.0 0.0 collective-permute-done.6.refs_3_.refs_1_
  32.1 0.0 collective-permute-done.5.refs_2_
  32.1 28.3 %forward_2340.1 = (f32[1,320,512]{2,1,0:T(8,128)}, f32[1,320,512]{2,1,0:T(8,128)}, f32[5,4,512]{2,1,0:T(4,128)}) custom-call(s32[3]{0:T(128)} %pad_add_fusion.scal, bf16[1,320,512]{2,1,0:T(8,128)(2,1)} %get-tuple-element.31.qm, bf16[1,320,512]{2,1,0:T(8,128)(2,1)} %collective-permute-done.qp, bf16[2,320,512]{2,1,0:T(8,128)(2,1)} %get-tuple-element.36.refs_0_.refs_3_, ...), custom_call_target="tpu_custom_call" | custom-call | flops 18400000000 | bytes 1600000 | tf_op jit(solution)/shard_map/forward_2340/pallas_call | solution.py:192
  60.3 0.0 collective-permute-done.4.refs_1_
  60.4 0.0 collective-permute-done.3.refs_0_
  60.4 8.0 %forward_15.1 = (bf16[1,320,512]{2,1,0:T(8,128)(2,1)}, bf16[1,320,512]{2,1,0:T(8,128)(2,1)}, f32[5,2,512]{2,1,0:T(2,128)}) custom-call(s32[3]{0:T(128)} %pad_add_fusion.scal, bf16[1,320,512]{2,1,0:T(8,128)(2,1)} %get-tuple-element.31.qm, bf16[1,320,512]{2,1,0:T(8,128)(2,1)} %collective-permute-done.qp, bf16[2,320,512]{2,1,0:T(8,128)(2,1)} %collective-permute-done.3.refs_0_, ...), custom_call_target="tpu_custom_call" | custom-call | flops 9200000000 | bytes 800000 | tf_op jit(solution)/shard_map/forward_15/pallas_call | solution.py:192
  68.4 4.3 %collective-permute-start.12 = (bf16[1,320,512]{2,1,0:T(8,128)(2,1)}, bf16[1,320,512]{2,1,0:T(8,128)(2,1)}, u32[]{:S(2)}, u32[]{:S(2)}) collective-permute-start(bf16[1,320,512]{2,1,0:T(8,128)(2,1)} %get-tuple-element.41.op), channel_id=1, source_target_pairs={{0,1},{1,0},{2,3},{3,2},{4,5},{5,4},{6,7},{7,6},{8,9},{9,8},{10,11... | collective-permute-start | bytes 983048 | tf_op jit(solution)/shard_map/ppermute | solution.py:355
  72.7 0.0 collective-permute-done.1.gp
  72.7 12.8 %backward_15.1 = (bf16[2,320,512]{2,1,0:T(8,128)(2,1)}, bf16[2,320,512]{2,1,0:T(8,128)(2,1)}, f32[1,320,512]{2,1,0:T(8,128)}, f32[1,320,512]{2,1,0:T(8,128)}) custom-call(s32[3]{0:T(128)} %pad_add_fusion.scal, bf16[1,320,512]{2,1,0:T(8,128)(2,1)} %get-tuple-element.31.qm, bf16[1,320,512]{2,1,0:T(8,128)(2,1)} %collective-permute-done.qp, ...), custom_call_target="tpu_custom_call" | custom-call | flops 14949999616 | bytes 1300000 | tf_op jit(solution)/shard_map/backward_15/pallas_call | solution.py:274
  85.5 8.0 %collective-permute-start.7 = (bf16[2,320,512]{2,1,0:T(8,128)(2,1)}, bf16[2,320,512]{2,1,0:T(8,128)(2,1)}, u32[]{:S(2)}, u32[]{:S(2)}) collective-permute-start(bf16[2,320,512]{2,1,0:T(8,128)(2,1)} %get-tuple-element.45), channel_id=1, source_target_pairs={{1,3},{2,0},{3,5},{4,2},{5,7},{6,4},{7,9},{8,6},{9,11},{10,8},{11,... | collective-permute-start | bytes 1966088 | tf_op jit(solution)/shard_map/ppermute | solution.py:361
  93.5 1.9 %collective-permute-start.8 = (bf16[2,320,512]{2,1,0:T(8,128)(2,1)}, bf16[2,320,512]{2,1,0:T(8,128)(2,1)}, u32[]{:S(2)}, u32[]{:S(2)}) collective-permute-start(bf16[2,320,512]{2,1,0:T(8,128)(2,1)} %get-tuple-element.46), channel_id=1, source_target_pairs={{0,2},{2,4},{3,1},{4,6},{5,3},{6,8},{7,5},{8,10},{9,7},{10,12},{11... | collective-permute-start | bytes 1966088 | tf_op jit(solution)/shard_map/ppermute | solution.py:358
  95.5 0.0 collective-permute-done.12.o_got
  95.5 4.6 %projection_term.1 = bf16[1280,640]{1,0:T(8,128)(2,1)} custom-call(s32[3]{0:T(128)} %pad_add_fusion.scal, bf16[1,320,512]{2,1,0:T(8,128)(2,1)} %get-tuple-element.40.om.o, bf16[1,320,512]{2,1,0:T(8,128)(2,1)} %collective-permute-done.12.o_got, bf16[1280,512]{1,0:T(8,128)(2,1)} %get-tuple-element.57.dy_turned), custom_call_target="tpu_custom_call" | custom-call | flops 4600000000 | bytes 400000 | tf_op jit(solution)/shard_map/projection_term/pallas_call | solution.py:325
  100.1 5.9 %all-to-all-start = ((bf16[16,80,640]{2,1,0:T(8,128)(2,1)}), bf16[16,80,640]{2,1,0:T(8,128)(2,1)}, u32[]{:S(2)}, u32[]{:S(2)}) async-start(bf16[16,80,640]{2,1,0:T(8,128)(2,1)} %bitcast.11), calls=%async_computation | async-start | bytes 3276800 | tf_op jit(solution)/shard_map/all_to_all | solution.py:396
  106.0 0.0 collective-permute-done.7.refs_6_
  106.0 1.9 %collective-permute-done.8.refs_7_ = bf16[2,320,512]{2,1,0:T(8,128)(2,1)} collective-permute-done((bf16[2,320,512]{2,1,0:T(8,128)(2,1)}, bf16[2,320,512]{2,1,0:T(8,128)(2,1)}, u32[]{:S(2)}, u32[]{:S(2)}) %collective-permute-start.8) | collective-permute-done | bytes 655392 | tf_op jit(solution)/shard_map/ppermute | solution.py:358
  107.9 22.8 %backward_3042.1 = (bf16[3,320,512]{2,1,0:T(8,128)(2,1)}, bf16[2,320,512]{2,1,0:T(8,128)(2,1)}, bf16[2,320,512]{2,1,0:T(8,128)(2,1)}, f32[2,320,512]{2,1,0:T(8,128)}, f32[1,320,512]{2,1,0:T(8,128)}) custom-call(s32[3]{0:T(128)} %pad_add_fusion.scal, bf16[1,320,512]{2,1,0:T(8,128)(2,1)} %get-tuple-element.31.qm, ...), custom_call_target="tpu_custom_call" | custom-call | flops 27599998976 | bytes 2400000 | tf_op jit(solution)/shard_map/backward_3042/pallas_call | solution.py:274
  130.6 0.1 collective-permute-start.11
  130.7 6.0 %collective-permute-start.9 = (bf16[2,320,512]{2,1,0:T(8,128)(2,1)}, bf16[2,320,512]{2,1,0:T(8,128)(2,1)}, u32[]{:S(2)}, u32[]{:S(2)}) collective-permute-start(bf16[2,320,512]{2,1,0:T(8,128)(2,1)} %get-tuple-element.51), channel_id=1, source_target_pairs={{1,3},{2,0},{3,5},{4,2},{5,7},{6,4},{7,9},{8,6},{9,11},{10,8},{11,... | collective-permute-start | bytes 1966088 | tf_op jit(solution)/shard_map/ppermute | solution.py:361
  136.7 1.9 %collective-permute-start.10 = (bf16[2,320,512]{2,1,0:T(8,128)(2,1)}, bf16[2,320,512]{2,1,0:T(8,128)(2,1)}, u32[]{:S(2)}, u32[]{:S(2)}) collective-permute-start(bf16[2,320,512]{2,1,0:T(8,128)(2,1)} %get-tuple-element.52), channel_id=1, source_target_pairs={{0,2},{2,4},{3,1},{4,6},{5,3},{6,8},{7,5},{8,10},{9,7},{10,12},{11... | collective-permute-start | bytes 1966088 | tf_op jit(solution)/shard_map/ppermute | solution.py:358
  138.6 0.0 all-to-all-done
  138.7 1.7 %convert_reduce_fusion = f32[80,640]{1,0:T(8,128)S(1)} fusion(bf16[16,80,640]{2,1,0:T(8,128)(2,1)} %all-to-all-done), kind=kLoop, calls=%fused_computation | loop fusion | flops 1587200 | bytes 1843200 | tf_op jit(solution)/shard_map/reduce_sum | solution.py:397
  140.3 0.7 reshape.15
  141.1 9.0 %all-to-all-start.1 = ((f32[16,5,640]{2,1,0:T(8,128)}), f32[16,5,640]{2,1,0:T(8,128)}, u32[]{:S(2)}, u32[]{:S(2)}) async-start(f32[16,5,640]{2,1,0:T(8,128)} %reshape.15), calls=%async_computation.1 | async-start | bytes 655360 | tf_op jit(solution)/shard_map/all_to_all | solution.py:399
  150.1 7.7 %backward_2.1 = (f32[2,320,512]{2,1,0:T(8,128)}, bf16[1,320,512]{2,1,0:T(8,128)(2,1)}) custom-call(s32[3]{0:T(128)} %pad_add_fusion.scal, bf16[1,320,512]{2,1,0:T(8,128)(2,1)} %get-tuple-element.31.qm, bf16[1,320,512]{2,1,0:T(8,128)(2,1)} %collective-permute-done.qp, bf16[1,320,512]{2,1,0:T(8,128)(2,1)} %get-tuple-element.33.gm, ...), custom_call_target="tpu_custom_call" | custom-call | flops 8049999872 | bytes 700000 | tf_op jit(solution)/shard_map/backward_2/pallas_call | solution.py:274
  157.8 0.0 collective-permute-done.9.a
  157.8 1.3 collective-permute-done.10.b
  159.1 0.0 collective-permute-done.11.got
  159.1 4.7 %sum_and_turn.1 = (bf16[512,640]{1,0:T(8,128)(2,1)}, bf16[512,640]{1,0:T(8,128)(2,1)}, bf16[512,640]{1,0:T(8,128)(2,1)}) custom-call(s32[3]{0:T(128)} %pad_add_fusion.scal, bf16[1,320,512]{2,1,0:T(8,128)(2,1)} %get-tuple-element.48.dq, f32[2,320,512]{2,1,0:T(8,128)} %get-tuple-element.49.mid, f32[2,320,512]{2,1,0:T(8,128)} %get-tuple-element.50.rest, ...), custom_call_target="tpu_custom_call" | custom-call | flops 115000000 | bytes 10000 | tf_op jit(solution)/shard_map/sum_and_turn/pallas_call | solution.py:302
  163.8 1.1 all-to-all-done.1
  164.9 1.6 reduce_sum.19
Async XLA Ops:
  5.1 17.9 %collective-permute-start.2 = (bf16[2,320,512]{2,1,0:T(8,128)(2,1)}, bf16[2,320,512]{2,1,0:T(8,128)(2,1)}, u32[]{:S(2)}, u32[]{:S(2)}) collective-permute-start(bf16[2,320,512]{2,1,0:T(8,128)(2,1)} %get-tuple-element.35), channel_id=1, source_target_pairs={{0,1},{1,0},{2,3},{3,2},{4,5},{5,4},{6,7},{7,6},{8,9},{9,8},{10,11... | collective-permute-start | bytes 1966088 | tf_op jit(solution)/shard_map/ppermute | solution.py:355
  5.9 26.1 %collective-permute-start.6 = (bf16[2,320,512]{2,1,0:T(8,128)(2,1)}, bf16[2,320,512]{2,1,0:T(8,128)(2,1)}, u32[]{:S(2)}, u32[]{:S(2)}) collective-permute-start(bf16[2,320,512]{2,1,0:T(8,128)(2,1)} %get-tuple-element.36.refs_0_.refs_3_), channel_id=1, source_target_pairs={{0,2},{2,4},{3,1},{4,6},{5,3},{6,8},{7,5},{8,10},{9,7},{10,12},{11... | collective-permute-start | bytes 1966088 | tf_op jit(solution)/shard_map/ppermute | solution.py:358
  7.9 24.1 %collective-permute-start.5 = (bf16[2,320,512]{2,1,0:T(8,128)(2,1)}, bf16[2,320,512]{2,1,0:T(8,128)(2,1)}, u32[]{:S(2)}, u32[]{:S(2)}) collective-permute-start(bf16[2,320,512]{2,1,0:T(8,128)(2,1)} %get-tuple-element.36.refs_0_.refs_3_), channel_id=1, source_target_pairs={{1,3},{2,0},{3,5},{4,2},{5,7},{6,4},{7,9},{8,6},{9,11},{10,8},{11,... | collective-permute-start | bytes 1966088 | tf_op jit(solution)/shard_map/ppermute | solution.py:361
  11.8 18.3 %collective-permute-start = (bf16[1,320,512]{2,1,0:T(8,128)(2,1)}, bf16[1,320,512]{2,1,0:T(8,128)(2,1)}, u32[]{:S(2)}, u32[]{:S(2)}) collective-permute-start(bf16[1,320,512]{2,1,0:T(8,128)(2,1)} %get-tuple-element.32), channel_id=1, source_target_pairs={{0,1},{1,0},{2,3},{3,2},{4,5},{5,4},{6,7},{7,6},{8,9},{9,8},{10,11... | collective-permute-start | bytes 983048 | tf_op jit(solution)/shard_map/ppermute | solution.py:355
  18.7 54.0 %collective-permute-start.1 = (bf16[1,320,512]{2,1,0:T(8,128)(2,1)}, bf16[1,320,512]{2,1,0:T(8,128)(2,1)}, u32[]{:S(2)}, u32[]{:S(2)}) collective-permute-start(bf16[1,320,512]{2,1,0:T(8,128)(2,1)} %get-tuple-element.34), channel_id=1, source_target_pairs={{0,1},{1,0},{2,3},{3,2},{4,5},{5,4},{6,7},{7,6},{8,9},{9,8},{10,11... | collective-permute-start | bytes 983048 | tf_op jit(solution)/shard_map/ppermute | solution.py:355
  23.0 37.3 %collective-permute-start.4 = (bf16[2,320,512]{2,1,0:T(8,128)(2,1)}, bf16[2,320,512]{2,1,0:T(8,128)(2,1)}, u32[]{:S(2)}, u32[]{:S(2)}) collective-permute-start(bf16[2,320,512]{2,1,0:T(8,128)(2,1)} %collective-permute-done.2.refs_1_.refs_0_), channel_id=1, source_target_pairs={{1,3},{2,0},{3,5},{4,2},{5,7},{6,4},{7,9},{8,6},{9,11},{10,8},{11,... | collective-permute-start | bytes 1966088 | tf_op jit(solution)/shard_map/ppermute | solution.py:361
  30.0 30.3 %collective-permute-start.3 = (bf16[2,320,512]{2,1,0:T(8,128)(2,1)}, bf16[2,320,512]{2,1,0:T(8,128)(2,1)}, u32[]{:S(2)}, u32[]{:S(2)}) collective-permute-start(bf16[2,320,512]{2,1,0:T(8,128)(2,1)} %collective-permute-done.2.refs_1_.refs_0_), channel_id=1, source_target_pairs={{0,2},{2,4},{3,1},{4,6},{5,3},{6,8},{7,5},{8,10},{9,7},{10,12},{11... | collective-permute-start | bytes 1966088 | tf_op jit(solution)/shard_map/ppermute | solution.py:358
  68.4 27.1 %collective-permute-start.12 = (bf16[1,320,512]{2,1,0:T(8,128)(2,1)}, bf16[1,320,512]{2,1,0:T(8,128)(2,1)}, u32[]{:S(2)}, u32[]{:S(2)}) collective-permute-start(bf16[1,320,512]{2,1,0:T(8,128)(2,1)} %get-tuple-element.41.op), channel_id=1, source_target_pairs={{0,1},{1,0},{2,3},{3,2},{4,5},{5,4},{6,7},{7,6},{8,9},{9,8},{10,11... | collective-permute-start | bytes 983048 | tf_op jit(solution)/shard_map/ppermute | solution.py:355
  85.5 20.5 %collective-permute-start.7 = (bf16[2,320,512]{2,1,0:T(8,128)(2,1)}, bf16[2,320,512]{2,1,0:T(8,128)(2,1)}, u32[]{:S(2)}, u32[]{:S(2)}) collective-permute-start(bf16[2,320,512]{2,1,0:T(8,128)(2,1)} %get-tuple-element.45), channel_id=1, source_target_pairs={{1,3},{2,0},{3,5},{4,2},{5,7},{6,4},{7,9},{8,6},{9,11},{10,8},{11,... | collective-permute-start | bytes 1966088 | tf_op jit(solution)/shard_map/ppermute | solution.py:361
  93.5 14.3 %collective-permute-start.8 = (bf16[2,320,512]{2,1,0:T(8,128)(2,1)}, bf16[2,320,512]{2,1,0:T(8,128)(2,1)}, u32[]{:S(2)}, u32[]{:S(2)}) collective-permute-start(bf16[2,320,512]{2,1,0:T(8,128)(2,1)} %get-tuple-element.46), channel_id=1, source_target_pairs={{0,2},{2,4},{3,1},{4,6},{5,3},{6,8},{7,5},{8,10},{9,7},{10,12},{11... | collective-permute-start | bytes 1966088 | tf_op jit(solution)/shard_map/ppermute | solution.py:358
  100.1 38.6 %all-to-all-start = ((bf16[16,80,640]{2,1,0:T(8,128)(2,1)}), bf16[16,80,640]{2,1,0:T(8,128)(2,1)}, u32[]{:S(2)}, u32[]{:S(2)}) async-start(bf16[16,80,640]{2,1,0:T(8,128)(2,1)} %bitcast.11), calls=%async_computation | async-start | bytes 3276800 | tf_op jit(solution)/shard_map/all_to_all | solution.py:396
  130.6 28.5 %collective-permute-start.11 = (bf16[3,320,512]{2,1,0:T(8,128)(2,1)}, bf16[3,320,512]{2,1,0:T(8,128)(2,1)}, u32[]{:S(2)}, u32[]{:S(2)}) collective-permute-start(bf16[3,320,512]{2,1,0:T(8,128)(2,1)} %get-tuple-element.53), channel_id=1, source_target_pairs={{0,1},{1,0},{2,3},{3,2},{4,5},{5,4},{6,7},{7,6},{8,9},{9,8},{10,11... | collective-permute-start | bytes 2949128 | tf_op jit(solution)/shard_map/ppermute | solution.py:355
  130.7 27.1 %collective-permute-start.9 = (bf16[2,320,512]{2,1,0:T(8,128)(2,1)}, bf16[2,320,512]{2,1,0:T(8,128)(2,1)}, u32[]{:S(2)}, u32[]{:S(2)}) collective-permute-start(bf16[2,320,512]{2,1,0:T(8,128)(2,1)} %get-tuple-element.51), channel_id=1, source_target_pairs={{1,3},{2,0},{3,5},{4,2},{5,7},{6,4},{7,9},{8,6},{9,11},{10,8},{11,... | collective-permute-start | bytes 1966088 | tf_op jit(solution)/shard_map/ppermute | solution.py:361
  136.7 22.4 %collective-permute-start.10 = (bf16[2,320,512]{2,1,0:T(8,128)(2,1)}, bf16[2,320,512]{2,1,0:T(8,128)(2,1)}, u32[]{:S(2)}, u32[]{:S(2)}) collective-permute-start(bf16[2,320,512]{2,1,0:T(8,128)(2,1)} %get-tuple-element.52), channel_id=1, source_target_pairs={{0,2},{2,4},{3,1},{4,6},{5,3},{6,8},{7,5},{8,10},{9,7},{10,12},{11... | collective-permute-start | bytes 1966088 | tf_op jit(solution)/shard_map/ppermute | solution.py:358
  141.1 23.9 %all-to-all-start.1 = ((f32[16,5,640]{2,1,0:T(8,128)}), f32[16,5,640]{2,1,0:T(8,128)}, u32[]{:S(2)}, u32[]{:S(2)}) async-start(f32[16,5,640]{2,1,0:T(8,128)} %reshape.15), calls=%async_computation.1 | async-start | bytes 655360 | tf_op jit(solution)/shard_map/all_to_all | solution.py:399

commit v8 on v7

--- a/solution.py
+++ b/solution.py
@@ -57,30 +57,29 @@
     return jnp.concatenate([first, jnp.where(odd, mine, partners)], axis=0)
 
 
-def split_kernel(scal, k_ref, v_ref, q_ref, kv_mine, kv_send, q_mine, q_send):
+def split_kernel(scal, *refs):
     odd = scal[2] > 0
-    for n, ref in enumerate((k_ref, v_ref)):
+    *sources, mine, send = refs
+    for n, ref in enumerate(sources):
         low, high = halves(jnp.transpose(ref[...]))
-        kv_mine[n] = jnp.where(odd, high, low)
-        kv_send[n] = jnp.where(odd, low, high)
-    low, high = halves(jnp.transpose(q_ref[...]))
-    q_mine[0] = jnp.where(odd, high, low)
-    q_send[0] = jnp.where(odd, low, high)
-
-
-def split_heads(scal, k, v, q):
+        mine[n] = jnp.where(odd, high, low)
+        send[n] = jnp.where(odd, low, high)
+
+
+def split_heads(scal, name, *sources):
+    n = len(sources)
     return pl.pallas_call(
         split_kernel,
         grid_spec=pltpu.PrefetchScalarGridSpec(
             num_scalar_prefetch=1,
             grid=(1,),
-            in_specs=[whole(k.shape)] * 3,
-            out_specs=[whole((2, ROWS, TOK))] * 2 + [whole((1, ROWS, TOK))] * 2,
-        ),
-        out_shape=[head_major(2)] * 2 + [head_major(1)] * 2,
-        name="split_kvq",
-        **params(4),
-    )(scal, k, v, q)
+            in_specs=[whole(sources[0].shape)] * n,
+            out_specs=[whole((n, ROWS, TOK))] * 2,
+        ),
+        out_shape=[head_major(n)] * 2,
+        name=name,
+        **params(1.3 * n),
+    )(scal, *sources)
 
 
 def grad_kernel(scal, dy_ref, w_ref, mine, send, dy_turned):
@@ -361,11 +360,13 @@
         return lax.ppermute(x, "ctx", step_b)
 
     dy = grad_out[0]
-    kv_mine, kv_send, q_mine, q_send = split_heads(scal, keys[0], values[0], queries[0])
+    kv_mine, kv_send = split_heads(scal, "split_kv", keys[0], values[0])
     kv_got = swap(kv_send)
     a_mine, b_mine = to_a(kv_mine), to_b(kv_mine)
+    q_mine, q_send = split_heads(scal, "split_q", queries[0])
     q_got = swap(q_send)
     g_mine, g_send, dy_turned = attention_grad(scal, dy, out_proj)
+    kv_got, g_send = lax.optimization_barrier((kv_got, g_send))
     g_got = swap(g_send)
     a_got, b_got = to_a(kv_got), to_b(kv_got)
     kv = (a_mine, a_got, kv_mine, kv_got, b_mine, b_got)

time: 170 us -> 167 us (0.982)
  waiting for transfers between devices: 11.8 us -> 3.83 us
  Pallas kernels: 97.5 us -> 104 us
    ppermute x5, waiting for transfers between devices: 7.48 us -> 1.59 us  [swap(): return lax.ppermute(x, 'ctx', swap_pairs)]
    pallas_call x2, Pallas kernels: 36.3 us -> 40.4 us  [forward(): pl.pallas_call(functools.partial(forward_kernel, js, bool(given), last),...]
    ppermute x4, starting transfers between devices: 21.6 us -> 18 us  [to_b(): return lax.ppermute(x, 'ctx', step_b)]
    all_to_all x1, starting transfers between devices: 5.94 us -> 9.27 us  [shards(): term = lax.all_to_all(term.reshape(dps, -1, term.shape[1]), 'dp', 0, 0)]
    ppermute x5, starting transfers between devices: 7.37 us -> 4.13 us  [swap(): return lax.ppermute(x, 'ctx', swap_pairs)]
    ppermute x4, waiting for transfers between devices: 3.21 us -> 0.63 us  [to_a(): return lax.ppermute(x, 'ctx', step_a)]
    pallas_call x1 -> x2, Pallas kernels: 3.8 us -> 6.2 us  [split_heads(): pl.pallas_call(split_kernel, grid_spec=pltpu.PrefetchScalarGridSpec(num_s...]
  transfers between devices with their start and end apart: 15 -> 15, of which waited for: 5 -> 4; matrix products, arithmetic and copies ran while one was open for 1% -> 1% of each run, Pallas kernels for 56% -> 62%
where the time goes in v8:
time: 167 us; the launch traced here: 163 us
  Pallas kernels  104 us (62%)
  starting transfers between devices  50.1 us (30%)
  other arithmetic  3.87 us (2%)
  waiting for transfers between devices  3.83 us (2%)
    pallas_call x3, Pallas kernels, backward(): pl.pallas_call(functools.partial(backward_kernel, js, pairs, stage), grid...  43.3 us
    pallas_call x2, Pallas kernels, forward(): pl.pallas_call(functools.partial(forward_kernel, js, bool(given), last),...  40.4 us
    ppermute x4, starting transfers between devices, to_b(): return lax.ppermute(x, 'ctx', step_b)  18 us
    all_to_all x1, starting transfers between devices, shards(): term = lax.all_to_all(term, 'ctx', 0, 0)  10 us
    all_to_all x1, starting transfers between devices, shards(): term = lax.all_to_all(term.reshape(dps, -1, term.shape[1]), 'dp', 0, 0)  9.27 us
    ppermute x4, starting transfers between devices, to_a(): return lax.ppermute(x, 'ctx', step_a)  8.7 us
    pallas_call x2, Pallas kernels, split_heads(): pl.pallas_call(split_kernel, grid_spec=pltpu.PrefetchScalarGridSpec(num_s...  6.2 us
    pallas_call x1, Pallas kernels, attention_grad(): pl.pallas_call(grad_kernel, grid_spec=pltpu.PrefetchScalarGridSpec(num_sc...  4.85 us
  transfers between devices with their start and end apart: 15, of which 4 were waited for; matrix products, arithmetic and copies ran while one was open for 1% of the time, Pallas kernels for 62%

profile of v8, /device:TPU:38, one launch (start us, length us, event | category | flops | bytes accessed | tf_op | source)
XLA Modules:
  0.0 163.4 jit_solution(1295140482909415847)
XLA Ops:
  0.7 0.6 pad_add_fusion.scal
  1.2 3.4 %split_kv.1 = (bf16[2,320,512]{2,1,0:T(8,128)(2,1)}, bf16[2,320,512]{2,1,0:T(8,128)(2,1)}) custom-call(s32[3]{0:T(128)} %pad_add_fusion.scal, bf16[512,640]{1,0:T(8,128)(2,1)} %bitcast.13, bf16[512,640]{1,0:T(8,128)(2,1)} %bitcast.14), custom_call_target="tpu_custom_call" | custom-call | flops 2990000128 | bytes 260000 | tf_op jit(solution)/shard_map/split_kv/pallas_call | solution.py:71
  4.6 0.8 collective-permute-start.1
  5.5 2.0 %collective-permute-start.6 = (bf16[2,320,512]{2,1,0:T(8,128)(2,1)}, bf16[2,320,512]{2,1,0:T(8,128)(2,1)}, u32[]{:S(2)}, u32[]{:S(2)}) collective-permute-start(bf16[2,320,512]{2,1,0:T(8,128)(2,1)} %get-tuple-element.40.refs_0_.refs_3_), channel_id=1, source_target_pairs={{0,2},{2,4},{3,1},{4,6},{5,3},{6,8},{7,5},{8,10},{9,7},{10,12},{11... | collective-permute-start | bytes 1966088 | tf_op jit(solution)/shard_map/ppermute | solution.py:357
  7.5 3.8 %collective-permute-start.5 = (bf16[2,320,512]{2,1,0:T(8,128)(2,1)}, bf16[2,320,512]{2,1,0:T(8,128)(2,1)}, u32[]{:S(2)}, u32[]{:S(2)}) collective-permute-start(bf16[2,320,512]{2,1,0:T(8,128)(2,1)} %get-tuple-element.40.refs_0_.refs_3_), channel_id=1, source_target_pairs={{1,3},{2,0},{3,5},{4,2},{5,7},{6,4},{7,9},{8,6},{9,11},{10,8},{11,... | collective-permute-start | bytes 1966088 | tf_op jit(solution)/shard_map/ppermute | solution.py:360
  11.3 2.8 %split_q.1 = (bf16[1,320,512]{2,1,0:T(8,128)(2,1)}, bf16[1,320,512]{2,1,0:T(8,128)(2,1)}) custom-call(s32[3]{0:T(128)} %pad_add_fusion.scal, bf16[512,640]{1,0:T(8,128)(2,1)} %bitcast.15), custom_call_target="tpu_custom_call" | custom-call | flops 1495000064 | bytes 130000 | tf_op jit(solution)/shard_map/split_q/pallas_call | solution.py:71
  14.1 2.0 %collective-permute-start = (bf16[1,320,512]{2,1,0:T(8,128)(2,1)}, bf16[1,320,512]{2,1,0:T(8,128)(2,1)}, u32[]{:S(2)}, u32[]{:S(2)}) collective-permute-start(bf16[1,320,512]{2,1,0:T(8,128)(2,1)} %get-tuple-element.34), channel_id=1, source_target_pairs={{0,1},{1,0},{2,3},{3,2},{4,5},{5,4},{6,7},{7,6},{8,9},{9,8},{10,11... | collective-permute-start | bytes 983048 | tf_op jit(solution)/shard_map/ppermute | solution.py:354
  16.1 4.8 %attention_grad.1 = (bf16[1,320,512]{2,1,0:T(8,128)(2,1)}, bf16[1,320,512]{2,1,0:T(8,128)(2,1)}, bf16[1280,512]{1,0:T(8,128)(2,1)}) custom-call(s32[3]{0:T(128)} %pad_add_fusion.scal, bf16[512,1280]{1,0:T(8,128)(2,1)} %bitcast.12, bf16[640,1280]{1,0:T(8,128)(2,1)} %w_ref.1), custom_call_target="tpu_custom_call" | custom-call | flops 4600000000 | bytes 400000 | tf_op jit(solution)/shard_map/attention_grad/pallas_call | solution.py:94
  21.0 1.6 collective-permute-done.1.refs_1_.refs_0_
  22.6 3.8 %collective-permute-start.4 = (bf16[2,320,512]{2,1,0:T(8,128)(2,1)}, bf16[2,320,512]{2,1,0:T(8,128)(2,1)}, u32[]{:S(2)}, u32[]{:S(2)}) collective-permute-start(bf16[2,320,512]{2,1,0:T(8,128)(2,1)} %collective-permute-done.1.refs_1_.refs_0_), channel_id=1, source_target_pairs={{1,3},{2,0},{3,5},{4,2},{5,7},{6,4},{7,9},{8,6},{9,11},{10,8},{11,... | collective-permute-start | bytes 1966088 | tf_op jit(solution)/shard_map/ppermute | solution.py:360
  26.4 2.8 %collective-permute-start.3 = (bf16[2,320,512]{2,1,0:T(8,128)(2,1)}, bf16[2,320,512]{2,1,0:T(8,128)(2,1)}, u32[]{:S(2)}, u32[]{:S(2)}) collective-permute-start(bf16[2,320,512]{2,1,0:T(8,128)(2,1)} %collective-permute-done.1.refs_1_.refs_0_), channel_id=1, source_target_pairs={{0,2},{2,4},{3,1},{4,6},{5,3},{6,8},{7,5},{8,10},{9,7},{10,12},{11... | collective-permute-start | bytes 1966088 | tf_op jit(solution)/shard_map/ppermute | solution.py:357
  29.2 0.0 collective-permute-done.qp
  29.3 0.1 collective-permute-start.2
  29.4 0.0 collective-permute-done.6.refs_3_.refs_1_
  29.4 0.0 collective-permute-done.5.refs_2_
  29.4 28.3 %forward_2340.1 = (f32[1,320,512]{2,1,0:T(8,128)}, f32[1,320,512]{2,1,0:T(8,128)}, f32[5,4,512]{2,1,0:T(4,128)}) custom-call(s32[3]{0:T(128)} %pad_add_fusion.scal, bf16[1,320,512]{2,1,0:T(8,128)(2,1)} %get-tuple-element.33.qm, bf16[1,320,512]{2,1,0:T(8,128)(2,1)} %collective-permute-done.qp, bf16[2,320,512]{2,1,0:T(8,128)(2,1)} %get-tuple-element.40.refs_0_.refs_3_, ...), custom_call_target="tpu_custom_call" | custom-call | flops 18400000000 | bytes 1600000 | tf_op jit(solution)/shard_map/forward_2340/pallas_call | solution.py:191
  57.7 0.0 collective-permute-done.4.refs_1_
  57.7 0.0 collective-permute-done.3.refs_0_
  57.7 12.1 %forward_15.1 = (bf16[1,320,512]{2,1,0:T(8,128)(2,1)}, bf16[1,320,512]{2,1,0:T(8,128)(2,1)}, f32[5,2,512]{2,1,0:T(2,128)}) custom-call(s32[3]{0:T(128)} %pad_add_fusion.scal, bf16[1,320,512]{2,1,0:T(8,128)(2,1)} %get-tuple-element.33.qm, bf16[1,320,512]{2,1,0:T(8,128)(2,1)} %collective-permute-done.qp, bf16[2,320,512]{2,1,0:T(8,128)(2,1)} %collective-permute-done.3.refs_0_, ...), custom_call_target="tpu_custom_call" | custom-call | flops 9200000000 | bytes 800000 | tf_op jit(solution)/shard_map/forward_15/pallas_call | solution.py:191
  69.8 0.8 collective-permute-start.12
  70.6 0.0 collective-permute-done.2.gp
  70.6 12.8 %backward_15.1 = (bf16[2,320,512]{2,1,0:T(8,128)(2,1)}, bf16[2,320,512]{2,1,0:T(8,128)(2,1)}, f32[1,320,512]{2,1,0:T(8,128)}, f32[1,320,512]{2,1,0:T(8,128)}) custom-call(s32[3]{0:T(128)} %pad_add_fusion.scal, bf16[1,320,512]{2,1,0:T(8,128)(2,1)} %get-tuple-element.33.qm, bf16[1,320,512]{2,1,0:T(8,128)(2,1)} %collective-permute-done.qp, ...), custom_call_target="tpu_custom_call" | custom-call | flops 14949999616 | bytes 1300000 | tf_op jit(solution)/shard_map/backward_15/pallas_call | solution.py:273
  83.5 5.3 %collective-permute-start.7 = (bf16[2,320,512]{2,1,0:T(8,128)(2,1)}, bf16[2,320,512]{2,1,0:T(8,128)(2,1)}, u32[]{:S(2)}, u32[]{:S(2)}) collective-permute-start(bf16[2,320,512]{2,1,0:T(8,128)(2,1)} %get-tuple-element.49), channel_id=1, source_target_pairs={{1,3},{2,0},{3,5},{4,2},{5,7},{6,4},{7,9},{8,6},{9,11},{10,8},{11,... | collective-permute-start | bytes 1966088 | tf_op jit(solution)/shard_map/ppermute | solution.py:360
  88.8 1.9 %collective-permute-start.8 = (bf16[2,320,512]{2,1,0:T(8,128)(2,1)}, bf16[2,320,512]{2,1,0:T(8,128)(2,1)}, u32[]{:S(2)}, u32[]{:S(2)}) collective-permute-start(bf16[2,320,512]{2,1,0:T(8,128)(2,1)} %get-tuple-element.50), channel_id=1, source_target_pairs={{0,2},{2,4},{3,1},{4,6},{5,3},{6,8},{7,5},{8,10},{9,7},{10,12},{11... | collective-permute-start | bytes 1966088 | tf_op jit(solution)/shard_map/ppermute | solution.py:357
  90.8 0.0 collective-permute-done.12.o_got
  90.8 4.6 %projection_term.1 = bf16[1280,640]{1,0:T(8,128)(2,1)} custom-call(s32[3]{0:T(128)} %pad_add_fusion.scal, bf16[1,320,512]{2,1,0:T(8,128)(2,1)} %get-tuple-element.44.om.o, bf16[1,320,512]{2,1,0:T(8,128)(2,1)} %collective-permute-done.12.o_got, bf16[1280,512]{1,0:T(8,128)(2,1)} %get-tuple-element.61.dy_turned), custom_call_target="tpu_custom_call" | custom-call | flops 4600000000 | bytes 400000 | tf_op jit(solution)/shard_map/projection_term/pallas_call | solution.py:324
  95.4 9.3 %all-to-all-start = ((bf16[16,80,640]{2,1,0:T(8,128)(2,1)}), bf16[16,80,640]{2,1,0:T(8,128)(2,1)}, u32[]{:S(2)}, u32[]{:S(2)}) async-start(bf16[16,80,640]{2,1,0:T(8,128)(2,1)} %bitcast.11), calls=%async_computation | async-start | bytes 3276800 | tf_op jit(solution)/shard_map/all_to_all | solution.py:397
  104.6 0.0 collective-permute-done.7.refs_6_
  104.6 0.6 collective-permute-done.8.refs_7_
  105.2 22.8 %backward_3042.1 = (bf16[3,320,512]{2,1,0:T(8,128)(2,1)}, bf16[2,320,512]{2,1,0:T(8,128)(2,1)}, bf16[2,320,512]{2,1,0:T(8,128)(2,1)}, f32[2,320,512]{2,1,0:T(8,128)}, f32[1,320,512]{2,1,0:T(8,128)}) custom-call(s32[3]{0:T(128)} %pad_add_fusion.scal, bf16[1,320,512]{2,1,0:T(8,128)(2,1)} %get-tuple-element.33.qm, ...), custom_call_target="tpu_custom_call" | custom-call | flops 27599998976 | bytes 2400000 | tf_op jit(solution)/shard_map/backward_3042/pallas_call | solution.py:273
  128.0 0.4 collective-permute-start.11
  128.3 5.0 %collective-permute-start.9 = (bf16[2,320,512]{2,1,0:T(8,128)(2,1)}, bf16[2,320,512]{2,1,0:T(8,128)(2,1)}, u32[]{:S(2)}, u32[]{:S(2)}) collective-permute-start(bf16[2,320,512]{2,1,0:T(8,128)(2,1)} %get-tuple-element.55), channel_id=1, source_target_pairs={{1,3},{2,0},{3,5},{4,2},{5,7},{6,4},{7,9},{8,6},{9,11},{10,8},{11,... | collective-permute-start | bytes 1966088 | tf_op jit(solution)/shard_map/ppermute | solution.py:360
  133.4 1.9 %collective-permute-start.10 = (bf16[2,320,512]{2,1,0:T(8,128)(2,1)}, bf16[2,320,512]{2,1,0:T(8,128)(2,1)}, u32[]{:S(2)}, u32[]{:S(2)}) collective-permute-start(bf16[2,320,512]{2,1,0:T(8,128)(2,1)} %get-tuple-element.56), channel_id=1, source_target_pairs={{0,2},{2,4},{3,1},{4,6},{5,3},{6,8},{7,5},{8,10},{9,7},{10,12},{11... | collective-permute-start | bytes 1966088 | tf_op jit(solution)/shard_map/ppermute | solution.py:357
  135.3 0.0 all-to-all-done
  135.3 1.7 %convert_reduce_fusion = f32[80,640]{1,0:T(8,128)S(1)} fusion(bf16[16,80,640]{2,1,0:T(8,128)(2,1)} %all-to-all-done), kind=kLoop, calls=%fused_computation | loop fusion | flops 1587200 | bytes 1843200 | tf_op jit(solution)/shard_map/reduce_sum | solution.py:398
  137.0 0.7 reshape.15
  137.7 10.0 %all-to-all-start.1 = ((f32[16,5,640]{2,1,0:T(8,128)}), f32[16,5,640]{2,1,0:T(8,128)}, u32[]{:S(2)}, u32[]{:S(2)}) async-start(f32[16,5,640]{2,1,0:T(8,128)} %reshape.15), calls=%async_computation.1 | async-start | bytes 655360 | tf_op jit(solution)/shard_map/all_to_all | solution.py:400
  147.8 7.7 %backward_2.1 = (f32[2,320,512]{2,1,0:T(8,128)}, bf16[1,320,512]{2,1,0:T(8,128)(2,1)}) custom-call(s32[3]{0:T(128)} %pad_add_fusion.scal, bf16[1,320,512]{2,1,0:T(8,128)(2,1)} %get-tuple-element.33.qm, bf16[1,320,512]{2,1,0:T(8,128)(2,1)} %collective-permute-done.qp, bf16[1,320,512]{2,1,0:T(8,128)(2,1)} %get-tuple-element.35.gm, ...), custom_call_target="tpu_custom_call" | custom-call | flops 8049999872 | bytes 700000 | tf_op jit(solution)/shard_map/backward_2/pallas_call | solution.py:273
  155.5 0.0 collective-permute-done.9.a
  155.5 0.1 collective-permute-done.10.b
  155.5 0.0 collective-permute-done.11.got
  155.5 4.7 %sum_and_turn.1 = (bf16[512,640]{1,0:T(8,128)(2,1)}, bf16[512,640]{1,0:T(8,128)(2,1)}, bf16[512,640]{1,0:T(8,128)(2,1)}) custom-call(s32[3]{0:T(128)} %pad_add_fusion.scal, bf16[1,320,512]{2,1,0:T(8,128)(2,1)} %get-tuple-element.52.dq, f32[2,320,512]{2,1,0:T(8,128)} %get-tuple-element.53.mid, f32[2,320,512]{2,1,0:T(8,128)} %get-tuple-element.54.rest, ...), custom_call_target="tpu_custom_call" | custom-call | flops 115000000 | bytes 10000 | tf_op jit(solution)/shard_map/sum_and_turn/pallas_call | solution.py:301
  160.2 1.6 all-to-all-done.1
  161.8 1.6 reduce_sum.19
Async XLA Ops:
  4.6 17.9 %collective-permute-start.1 = (bf16[2,320,512]{2,1,0:T(8,128)(2,1)}, bf16[2,320,512]{2,1,0:T(8,128)(2,1)}, u32[]{:S(2)}, u32[]{:S(2)}) collective-permute-start(bf16[2,320,512]{2,1,0:T(8,128)(2,1)} %get-tuple-element.36), channel_id=1, source_target_pairs={{0,1},{1,0},{2,3},{3,2},{4,5},{5,4},{6,7},{7,6},{8,9},{9,8},{10,11... | collective-permute-start | bytes 1966088 | tf_op jit(solution)/shard_map/ppermute | solution.py:354
  5.5 23.9 %collective-permute-start.6 = (bf16[2,320,512]{2,1,0:T(8,128)(2,1)}, bf16[2,320,512]{2,1,0:T(8,128)(2,1)}, u32[]{:S(2)}, u32[]{:S(2)}) collective-permute-start(bf16[2,320,512]{2,1,0:T(8,128)(2,1)} %get-tuple-element.40.refs_0_.refs_3_), channel_id=1, source_target_pairs={{0,2},{2,4},{3,1},{4,6},{5,3},{6,8},{7,5},{8,10},{9,7},{10,12},{11... | collective-permute-start | bytes 1966088 | tf_op jit(solution)/shard_map/ppermute | solution.py:357
  7.5 21.9 %collective-permute-start.5 = (bf16[2,320,512]{2,1,0:T(8,128)(2,1)}, bf16[2,320,512]{2,1,0:T(8,128)(2,1)}, u32[]{:S(2)}, u32[]{:S(2)}) collective-permute-start(bf16[2,320,512]{2,1,0:T(8,128)(2,1)} %get-tuple-element.40.refs_0_.refs_3_), channel_id=1, source_target_pairs={{1,3},{2,0},{3,5},{4,2},{5,7},{6,4},{7,9},{8,6},{9,11},{10,8},{11,... | collective-permute-start | bytes 1966088 | tf_op jit(solution)/shard_map/ppermute | solution.py:360
  14.1 15.1 %collective-permute-start = (bf16[1,320,512]{2,1,0:T(8,128)(2,1)}, bf16[1,320,512]{2,1,0:T(8,128)(2,1)}, u32[]{:S(2)}, u32[]{:S(2)}) collective-permute-start(bf16[1,320,512]{2,1,0:T(8,128)(2,1)} %get-tuple-element.34), channel_id=1, source_target_pairs={{0,1},{1,0},{2,3},{3,2},{4,5},{5,4},{6,7},{7,6},{8,9},{9,8},{10,11... | collective-permute-start | bytes 983048 | tf_op jit(solution)/shard_map/ppermute | solution.py:354
  22.6 35.1 %collective-permute-start.4 = (bf16[2,320,512]{2,1,0:T(8,128)(2,1)}, bf16[2,320,512]{2,1,0:T(8,128)(2,1)}, u32[]{:S(2)}, u32[]{:S(2)}) collective-permute-start(bf16[2,320,512]{2,1,0:T(8,128)(2,1)} %collective-permute-done.1.refs_1_.refs_0_), channel_id=1, source_target_pairs={{1,3},{2,0},{3,5},{4,2},{5,7},{6,4},{7,9},{8,6},{9,11},{10,8},{11,... | collective-permute-start | bytes 1966088 | tf_op jit(solution)/shard_map/ppermute | solution.py:360
  26.4 31.3 %collective-permute-start.3 = (bf16[2,320,512]{2,1,0:T(8,128)(2,1)}, bf16[2,320,512]{2,1,0:T(8,128)(2,1)}, u32[]{:S(2)}, u32[]{:S(2)}) collective-permute-start(bf16[2,320,512]{2,1,0:T(8,128)(2,1)} %collective-permute-done.1.refs_1_.refs_0_), channel_id=1, source_target_pairs={{0,2},{2,4},{3,1},{4,6},{5,3},{6,8},{7,5},{8,10},{9,7},{10,12},{11... | collective-permute-start | bytes 1966088 | tf_op jit(solution)/shard_map/ppermute | solution.py:357
  29.3 41.4 %collective-permute-start.2 = (bf16[1,320,512]{2,1,0:T(8,128)(2,1)}, bf16[1,320,512]{2,1,0:T(8,128)(2,1)}, u32[]{:S(2)}, u32[]{:S(2)}) collective-permute-start(bf16[1,320,512]{2,1,0:T(8,128)(2,1)} %get-tuple-element.38), channel_id=1, source_target_pairs={{0,1},{1,0},{2,3},{3,2},{4,5},{5,4},{6,7},{7,6},{8,9},{9,8},{10,11... | collective-permute-start | bytes 983048 | tf_op jit(solution)/shard_map/ppermute | solution.py:354
  69.8 21.0 %collective-permute-start.12 = (bf16[1,320,512]{2,1,0:T(8,128)(2,1)}, bf16[1,320,512]{2,1,0:T(8,128)(2,1)}, u32[]{:S(2)}, u32[]{:S(2)}) collective-permute-start(bf16[1,320,512]{2,1,0:T(8,128)(2,1)} %get-tuple-element.45.op), channel_id=1, source_target_pairs={{0,1},{1,0},{2,3},{3,2},{4,5},{5,4},{6,7},{7,6},{8,9},{9,8},{10,11... | collective-permute-start | bytes 983048 | tf_op jit(solution)/shard_map/ppermute | solution.py:354
  83.5 21.1 %collective-permute-start.7 = (bf16[2,320,512]{2,1,0:T(8,128)(2,1)}, bf16[2,320,512]{2,1,0:T(8,128)(2,1)}, u32[]{:S(2)}, u32[]{:S(2)}) collective-permute-start(bf16[2,320,512]{2,1,0:T(8,128)(2,1)} %get-tuple-element.49), channel_id=1, source_target_pairs={{1,3},{2,0},{3,5},{4,2},{5,7},{6,4},{7,9},{8,6},{9,11},{10,8},{11,... | collective-permute-start | bytes 1966088 | tf_op jit(solution)/shard_map/ppermute | solution.py:360
  88.8 16.4 %collective-permute-start.8 = (bf16[2,320,512]{2,1,0:T(8,128)(2,1)}, bf16[2,320,512]{2,1,0:T(8,128)(2,1)}, u32[]{:S(2)}, u32[]{:S(2)}) collective-permute-start(bf16[2,320,512]{2,1,0:T(8,128)(2,1)} %get-tuple-element.50), channel_id=1, source_target_pairs={{0,2},{2,4},{3,1},{4,6},{5,3},{6,8},{7,5},{8,10},{9,7},{10,12},{11... | collective-permute-start | bytes 1966088 | tf_op jit(solution)/shard_map/ppermute | solution.py:357
  95.4 40.0 %all-to-all-start = ((bf16[16,80,640]{2,1,0:T(8,128)(2,1)}), bf16[16,80,640]{2,1,0:T(8,128)(2,1)}, u32[]{:S(2)}, u32[]{:S(2)}) async-start(bf16[16,80,640]{2,1,0:T(8,128)(2,1)} %bitcast.11), calls=%async_computation | async-start | bytes 3276800 | tf_op jit(solution)/shard_map/all_to_all | solution.py:397
  128.0 27.5 %collective-permute-start.11 = (bf16[3,320,512]{2,1,0:T(8,128)(2,1)}, bf16[3,320,512]{2,1,0:T(8,128)(2,1)}, u32[]{:S(2)}, u32[]{:S(2)}) collective-permute-start(bf16[3,320,512]{2,1,0:T(8,128)(2,1)} %get-tuple-element.57), channel_id=1, source_target_pairs={{0,1},{1,0},{2,3},{3,2},{4,5},{5,4},{6,7},{7,6},{8,9},{9,8},{10,11... | collective-permute-start | bytes 2949128 | tf_op jit(solution)/shard_map/ppermute | solution.py:354
  128.3 27.1 %collective-permute-start.9 = (bf16[2,320,512]{2,1,0:T(8,128)(2,1)}, bf16[2,320,512]{2,1,0:T(8,128)(2,1)}, u32[]{:S(2)}, u32[]{:S(2)}) collective-permute-start(bf16[2,320,512]{2,1,0:T(8,128)(2,1)} %get-tuple-element.55), channel_id=1, source_target_pairs={{1,3},{2,0},{3,5},{4,2},{5,7},{6,4},{7,9},{8,6},{9,11},{10,8},{11,... | collective-permute-start | bytes 1966088 | tf_op jit(solution)/shard_map/ppermute | solution.py:360
  133.4 22.1 %collective-permute-start.10 = (bf16[2,320,512]{2,1,0:T(8,128)(2,1)}, bf16[2,320,512]{2,1,0:T(8,128)(2,1)}, u32[]{:S(2)}, u32[]{:S(2)}) collective-permute-start(bf16[2,320,512]{2,1,0:T(8,128)(2,1)} %get-tuple-element.56), channel_id=1, source_target_pairs={{0,2},{2,4},{3,1},{4,6},{5,3},{6,8},{7,5},{8,10},{9,7},{10,12},{11... | collective-permute-start | bytes 1966088 | tf_op jit(solution)/shard_map/ppermute | solution.py:357
  137.7 24.0 %all-to-all-start.1 = ((f32[16,5,640]{2,1,0:T(8,128)}), f32[16,5,640]{2,1,0:T(8,128)}, u32[]{:S(2)}, u32[]{:S(2)}) async-start(f32[16,5,640]{2,1,0:T(8,128)} %reshape.15), calls=%async_computation.1 | async-start | bytes 655360 | tf_op jit(solution)/shard_map/all_to_all | solution.py:400
